TPU v7x, 128 devices: a whole 4x4x4 slice. The times are simulated.
128 devices in a mesh: gz: 8 (over x_hi, z), gy: 16 (over y, x_lo, core).
Axes of the slice: x: 4 (x_hi: 2, x_lo: 2; x = x_hi * 2 + x_lo), y: 4, z: 4, core: 2. Of those that a mesh axis runs over, the one named last changes fastest.
Arguments:
- volume: float32 [96, 128, 256], P('gz', 'gy'), may hold values from -6 to 6
- projector: bfloat16 [4, 1024, 128, 256], P(None, None, 'gy'), may hold values from -0.03125 to 0.03125
- measured: float32 [1024, 96], P(None, 'gz'), may hold values from -6 to 6
- subset: int32 [1], replicated, may hold values from 0 to 1023
- timestep: int32 [1], replicated, may hold values from 100 to 1000
- axial_in: bfloat16 [9, 64, 1], replicated, may hold values from -2 to 2
- axial_bias_in: float32 [64], replicated, may hold values from -3 to 3
- axial_mid: bfloat16 [9, 64, 64], replicated, may hold values from -0.25 to 0.25
- axial_bias_mid: float32 [64], replicated, may hold values from -3 to 3
- axial_out: bfloat16 [9, 1, 64], replicated, may hold values from -0.25 to 0.25
- coronal_in: bfloat16 [9, 64, 1], replicated, may hold values from -2 to 2
- coronal_bias_in: float32 [64], replicated, may hold values from -3 to 3
- coronal_mid: bfloat16 [9, 64, 64], replicated, may hold values from -0.25 to 0.25
- coronal_bias_mid: float32 [64], replicated, may hold values from -3 to 3
- coronal_out: bfloat16 [9, 1, 64], replicated, may hold values from -0.25 to 0.25
Outputs:
- restored: float32 [96, 128, 256], P('gz', 'gy')
- residual: float32 [1024, 96], P('gy', 'gz')
All inputs are finite; a program needn't handle non-finite values.
Results may differ from a plain program's by a relative error of at most 0.0075.
Values may be sent and summed in bfloat16 or wider, within the bound.
No kernel may reach another device: no remote copies, remote signals or barrier semaphores. Data moves between devices by JAX's collectives and lax.ppermute only.
A program may use at most 192 MiB of HBM per device.

v0:
```python
import jax
import jax.numpy as jnp
from jax import lax
from jax.sharding import PartitionSpec as P

SUBSETS = 4


SIGMA_STEP = 0.002
RELAX_TOP = 4.0


def with_halo(value, sides, width):
    for axis, dim in sides:
        size, length = (lax.axis_size(axis), value.shape[dim])
        up = [(i, (i + 1) % size) for i in range(size - 1)]
        down = [(j, i) for i, j in up]
        last = lax.slice_in_dim(value, length - width, length, axis=dim)
        leading = lax.slice_in_dim(value, 0, width, axis=dim)
        before = lax.ppermute(last, axis, up)
        after = lax.ppermute(leading, axis, down)
        value = jnp.concatenate([before, value, after], axis=dim)
    return value


def noise_scales(timestep):
    sigma = timestep[0].astype(jnp.float32) * SIGMA_STEP
    scale_in = 1.0 / jnp.sqrt(1.0 + sigma * sigma)
    return (scale_in, sigma * scale_in)


def plane_conv(inputs, taps, dim):
    padded = jnp.pad(inputs, [(0, 0)] * (inputs.ndim - 1) + [(1, 1)])
    length = inputs.shape[dim] - 2
    across = inputs.shape[-1]
    last_dim = inputs.ndim - 1
    summed = None
    for tap_row in range(3):
        row_band = lax.slice_in_dim(padded, tap_row, tap_row + length, axis=dim)
        for tap_col in range(3):
            shifted = lax.slice_in_dim(row_band, tap_col, tap_col + across, axis=last_dim)
            contrib = jnp.einsum(
                "oc,c...->o...",
                taps[3 * tap_row + tap_col],
                shifted,
                preferred_element_type=jnp.float32,
            )
            summed = contrib if summed is None else summed + contrib
    return summed


def activate(summed, bias):
    return jnp.maximum(summed + bias[:, None, None, None], 0.0).astype(jnp.bfloat16)


def row_halo(block):
    return with_halo(block, (("gy", 2),), 1)


def zero_rim(block):
    return jnp.pad(block, ((0, 0), (1, 1), (0, 0), (0, 0)))


def run_layers(entry, extend, dim, first_taps, first_bias, middle_taps, middle_bias, last_taps):
    hidden_one = activate(plane_conv(extend(entry), first_taps, dim), first_bias)
    hidden_two = activate(plane_conv(extend(hidden_one), middle_taps, dim), middle_bias)
    return plane_conv(extend(hidden_two), last_taps, dim)[0]


def per_device(
    volume,
    projector,
    measured,
    subset,
    timestep,
    axial_in,
    axial_bias_in,
    axial_mid,
    axial_bias_mid,
    axial_out,
    coronal_in,
    coronal_bias_in,
    coronal_mid,
    coronal_bias_mid,
    coronal_out,
):
    scale_in, scale_out = noise_scales(timestep)
    view = subset[0] % SUBSETS
    epoch = (subset[0] // SUBSETS).astype(jnp.float32)
    relax = RELAX_TOP / (1.0 + epoch / 64.0)
    slices_here, rows_here, across = volume.shape
    ray_count = projector.shape[1]
    entry = (volume * scale_in).astype(jnp.bfloat16)[None]
    denoised = run_layers(
        entry, row_halo, 2, axial_in, axial_bias_in, axial_mid, axial_bias_mid, axial_out
    )
    axial = volume + scale_out * denoised
    flat = axial.astype(jnp.bfloat16).reshape(slices_here, rows_here * across)
    chosen = lax.dynamic_index_in_dim(projector, view, 0, keepdims=False).reshape(
        ray_count, rows_here * across
    )
    share_rays = ray_count // lax.axis_size("gy")
    ray_start = lax.axis_index("gy") * share_rays
    partial_sino = lax.dot_general(
        chosen, flat, (((1,), (1,)), ((), ())), preferred_element_type=jnp.float32
    )
    sinogram = lax.psum(partial_sino, "gy")
    full_residual = measured - sinogram
    residual = lax.dynamic_slice_in_dim(full_residual, ray_start, share_rays, 0)
    back = lax.dot_general(
        full_residual.astype(jnp.bfloat16),
        chosen,
        (((0,), (0,)), ((), ())),
        preferred_element_type=jnp.float32,
    )
    corrected = axial + relax * back.reshape(slices_here, rows_here, across)
    standing = lax.all_to_all(corrected, "gz", split_axis=1, concat_axis=0, tiled=True)
    coronal_entry = (standing * scale_in).astype(jnp.bfloat16)[None]
    coronal_net = run_layers(
        coronal_entry,
        zero_rim,
        1,
        coronal_in,
        coronal_bias_in,
        coronal_mid,
        coronal_bias_mid,
        coronal_out,
    )
    standing_out = standing + scale_out * coronal_net
    restored = lax.all_to_all(standing_out, "gz", split_axis=0, concat_axis=1, tiled=True)
    return (restored, residual)


def solution(mesh):
    in_specs = (
        P("gz", "gy", None),
        P(None, None, "gy", None),
        P(None, "gz"),
        P(),
        P(),
        P(),
        P(),
        P(),
        P(),
        P(),
        P(),
        P(),
        P(),
        P(),
        P(),
    )
    out_specs = (P("gz", "gy", None), P("gy", "gz"))
    return jax.shard_map(
        per_device, mesh=mesh, in_specs=in_specs, out_specs=out_specs, check_vma=False
    )
```

profile of v0, /device:TPU:0, one launch (start us, length us, event | category | flops | bytes accessed | tf_op | source)
XLA Modules:
  0.0 253.5 jit_solution(16969664286213442356)
XLA Ops:
  8.8 5.4 %fusion.16 = bf16[64,12,8,256]{3,0,2,1:T(8,128)(2,1)S(1)} fusion(f32[64]{0:T(128)} %param.21, f32[64]{0:T(128)S(1)} %get-tuple-element.46, f32[12,8,256]{2,1,0:T(8,128)S(1)} %get-tuple-element.48, f32[64]{0:T(128)S(1)} %get-tuple-element.47, f32[12,8,256]{2,1,0:T(8,128)S(1)} %get-tuple-element.27, f32[64]{0:T(128)S(1)} %get-tuple-element.40, ...), kind=kLoop, calls=%fused_computation.36 | loop fusion | flops 31457280 | bytes 4033024 | tf_op jit(solution)/shard_map/convert_element_type | solution.py:53
  14.2 4.4 %collective-permute-start.2 = (bf16[64,12,1,256]{3,0,2,1:T(8,128)(2,1)S(1)}, bf16[64,12,1,256]{3,0,2,1:T(8,128)(2,1)S(1)}, u32[]{:S(2)}, u32[]{:S(2)}) collective-permute-start(bf16[64,12,1,256]{3,0,2,1:T(8,128)(2,1)S(1)} %get-tuple-element.8), channel_id=1, source_target_pairs={{0,1},{1,2},{2,3},{3,4},{4,5},{5,6},{6,7},{7,8},{8,9},{9,10},{10,1... | collective-permute-start | bytes 1179656 | tf_op jit(solution)/shard_map/ppermute | solution.py:20
  20.4 3.6 %fusion.149 = f32[12,8,256,64]{2,3,1,0:T(8,128)} fusion(bf16[64,12,8,256]{3,0,2,1:T(8,128)(2,1)S(1)} %fusion.16, bf16[9,64,64]{2,1,0:T(8,128)(2,1)S(1)} %copy-done.2), kind=kOutput, calls=%fused_computation.188 | convolution fusion | flops 201326592 | bytes 9453568 | tf_op jit(solution)/shard_map/oc,c...->o.../dot_general | solution.py:42
  24.1 4.0 %fusion.5 = bf16[64,12,10,258]{3,0,2,1:T(8,128)(2,1)S(1)} fusion(bf16[64,12,1,256]{3,0,2,1:T(8,128)(2,1)S(1)} %collective-permute-done.3, bf16[64,12,8,256]{3,0,2,1:T(8,128)(2,1)S(1)} %fusion.16, bf16[64,12,1,256]{3,0,2,1:T(8,128)(2,1)S(1)} %collective-permute-done.2), kind=kLoop, calls=%fused_computation.25 | loop fusion | flops 23777280 | bytes 7895040 | tf_op jit(solution)/shard_map/concatenate | solution.py:22
  31.7 3.7 %fusion.59 = f32[12,8,256,64]{2,3,1,0:T(8,128)} fusion(bf16[64,12,10,258]{3,0,2,1:T(8,128)(2,1)S(1)} %fusion.5, bf16[9,64,64]{2,1,0:T(8,128)(2,1)S(1)} %copy-done.2), kind=kOutput, calls=%fused_computation.74 | convolution fusion | flops 201326592 | bytes 9453568 | tf_op jit(solution)/shard_map/oc,c...->o.../dot_general | solution.py:42
  35.4 3.7 %fusion.61 = f32[12,8,256,64]{2,3,1,0:T(8,128)} fusion(bf16[64,12,10,258]{3,0,2,1:T(8,128)(2,1)S(1)} %fusion.5, bf16[9,64,64]{2,1,0:T(8,128)(2,1)S(1)} %copy-done.2), kind=kOutput, calls=%fused_computation.76 | convolution fusion | flops 201326592 | bytes 9453568 | tf_op jit(solution)/shard_map/oc,c...->o.../dot_general | solution.py:42
  39.1 3.9 %fusion.63 = f32[12,8,256,64]{2,3,1,0:T(8,128)} fusion(bf16[64,12,10,258]{3,0,2,1:T(8,128)(2,1)S(1)} %fusion.5, bf16[9,64,64]{2,1,0:T(8,128)(2,1)S(1)} %copy-done.2), kind=kOutput, calls=%fused_computation.78 | convolution fusion | flops 201326592 | bytes 9453568 | tf_op jit(solution)/shard_map/oc,c...->o.../dot_general | solution.py:42
  53.7 16.9 %fusion.97 = bf16[64,12,8,256]{3,0,2,1:T(8,128)(2,1)S(1)} fusion(f32[64]{0:T(128)S(1)} %copy-done.8, f32[12,8,256,64]{2,3,1,0:T(8,128)} %fusion.55, f32[12,8,256,64]{2,3,1,0:T(8,128)} %fusion.57, f32[12,8,256,64]{2,3,1,0:T(8,128)} %fusion.59, f32[12,8,256,64]{2,3,1,0:T(8,128)} %fusion.149, f32[12,8,256,64]{2,3,1,0:T(8,128)} %fusion.61, ...), kind=kOutput, calls=%fused_computation.107 | convolution fusion | flops 218628096 | bytes 56640000 | tf_op jit(solution)/shard_map/oc,c...->o.../dot_general | solution.py:42
  71.6 8.3 %collective-permute-start.4 = (bf16[64,12,1,256]{3,0,2,1:T(8,128)(2,1)}, bf16[64,12,1,256]{3,0,2,1:T(8,128)(2,1)S(1)}, u32[]{:S(2)}, u32[]{:S(2)}) collective-permute-start(bf16[64,12,1,256]{3,0,2,1:T(8,128)(2,1)} %get-tuple-element.6), channel_id=1, source_target_pairs={{0,1},{1,2},{2,3},{3,4},{4,5},{5,6},{6,7},{7,8},{8,9},{9,10},{10,1... | collective-permute-start | bytes 1179656 | tf_op jit(solution)/shard_map/ppermute | solution.py:20
  81.3 4.5 %constant_dynamic-slice_fusion.1 = bf16[1,1024,8,256]{3,2,1,0:T(8,128)(2,1)} fusion(bf16[4,1024,8,256]{3,2,1,0:T(8,128)(2,1)} %param.16, s32[]{:T(128)S(6)} %select_n.20), kind=kLoop, calls=%fused_computation.268 | loop fusion | bytes 8388612 | tf_op jit(solution)/shard_map/jit(dynamic_index_in_dim)/dynamic_slice | solution.py:99
  85.8 6.7 %copy.67 = bf16[1,1024,8,256]{1,3,2,0:T(8,128)(2,1)} copy(bf16[1,1024,8,256]{3,2,1,0:T(8,128)(2,1)} %constant_dynamic-slice_fusion.1) | data formatting | bytes 8388608
  93.1 5.0 %select_maximum_fusion = bf16[64,12,10,258]{3,0,2,1:T(8,128)(2,1)S(1)} fusion(bf16[64,12,1,256]{3,0,2,1:T(8,128)(2,1)} %collective-permute-done.5, bf16[64,12,8,256]{3,0,2,1:T(8,128)(2,1)S(1)} %fusion.97, bf16[64,12,1,256]{3,0,2,1:T(8,128)(2,1)S(1)} %collective-permute-done.4), kind=kLoop, calls=%fused_computation.19 | loop fusion | flops 23777280 | bytes 7895040 | tf_op jit(solution)/shard_map/concatenate | solution.py:22
  106.7 54.2 %psum.7 = f32[1024,12]{0,1:T(8,128)S(1)} all-reduce(f32[1024,12]{0,1:T(8,128)S(1)} %fusion.249), channel_id=1, replica_groups=mesh['gz'=8,'gy'=16] {'gy'}, use_global_device_ids=true, to_apply=%region_0.1 | all-reduce | flops 12288 | bytes 98304 | tf_op jit(solution)/shard_map/psum | solution.py:107
  160.9 4.0 %fusion.105 = f32[12,8,256]{2,0,1:T(8,128)} fusion(f32[12,8,256]{2,0,1:T(8,128)S(1)} %get-tuple-element.5, bf16[1,1024,8,256]{1,3,2,0:T(8,128)(2,1)} %copy.67, f32[]{:T(128)S(6)} %div.19, f32[1024,12]{0,1:T(8,128)S(1)} %sub.8), kind=kOutput, calls=%fused_computation.109 | convolution fusion | flops 50393088 | bytes 4440068 | tf_op jit(solution)/shard_map/dot_general | solution.py:110
  165.0 7.9 %all-to-all-start = ((f32[12,8,256]{2,0,1:T(8,128)}), f32[12,8,256]{2,0,1:T(8,128)S(1)}, u32[]{:S(2)}, u32[]{:S(2)}) async-start(f32[12,8,256]{2,0,1:T(8,128)} %fusion.105), calls=%async_computation | async-start | bytes 262144 | tf_op jit(solution)/shard_map/all_to_all | solution.py:117
  172.9 8.0 %all-to-all-done = f32[12,8,256]{2,0,1:T(8,128)S(1)} async-done(((f32[12,8,256]{2,0,1:T(8,128)}), f32[12,8,256]{2,0,1:T(8,128)S(1)}, u32[]{:S(2)}, u32[]{:S(2)}) %all-to-all-start) | async-done | bytes 98336 | tf_op jit(solution)/shard_map/all_to_all | solution.py:117
  181.2 4.6 %fusion.239 = bf16[64,96,1,256]{3,0,1,2:T(8,128)(2,1)S(1)} fusion(f32[64]{0:T(128)S(1)} %copy-done.9, f32[64]{0:T(128)S(1)} %get-tuple-element.37, f32[96,256]{1,0:T(8,128)S(1)} %get-tuple-element.21, f32[64]{0:T(128)S(1)} %get-tuple-element.38, f32[96,256]{1,0:T(8,128)S(1)} %get-tuple-element.25, f32[64]{0:T(128)S(1)} %get-tuple-element.31, ...), kind=kLoop, calls=%fused_computation.298 | loop fusion | flops 31457280 | bytes 4033024 | tf_op jit(solution)/shard_map/convert_element_type | solution.py:53
  185.8 7.0 %fusion.79 = f32[96,256,64]{1,2,0:T(8,128)} fusion(bf16[9,64,64]{2,1,0:T(8,128)(2,1)S(1)} %copy-done.3, f32[64]{0:T(128)S(1)} %copy-done.9, f32[64]{0:T(128)S(1)} %get-tuple-element.37, f32[96,256]{1,0:T(8,128)S(1)} %get-tuple-element.21, f32[64]{0:T(128)S(1)} %get-tuple-element.38, f32[96,256]{1,0:T(8,128)S(1)} %get-tuple-element.25, ...), kind=kOutput, calls=%fused_computation.95 | convolution fusion | flops 232783872 | bytes 7197696 | tf_op jit(solution)/shard_map/oc,c...->o.../dot_general | solution.py:42
  194.3 3.8 %fusion.21 = f32[96,256,64]{1,2,0:T(8,128)} fusion(bf16[64,98,1,256]{3,0,1,2:T(8,128)(2,1)S(1)} %pad.38, bf16[9,64,64]{2,1,0:T(8,128)(2,1)S(1)} %copy-done.3), kind=kOutput, calls=%fused_computation.40 | convolution fusion | flops 201326592 | bytes 9519104 | tf_op jit(solution)/shard_map/oc,c...->o.../dot_general | solution.py:42
  198.0 3.8 %fusion.24 = f32[96,256,64]{1,2,0:T(8,128)} fusion(bf16[64,98,1,256]{3,0,1,2:T(8,128)(2,1)S(1)} %pad.38, bf16[9,64,64]{2,1,0:T(8,128)(2,1)S(1)} %copy-done.3), kind=kOutput, calls=%fused_computation.42 | convolution fusion | flops 201326592 | bytes 9519104 | tf_op jit(solution)/shard_map/oc,c...->o.../dot_general | solution.py:42
  201.8 3.6 %fusion.27 = f32[96,256,64]{1,2,0:T(8,128)} fusion(bf16[64,98,1,256]{3,0,1,2:T(8,128)(2,1)S(1)} %pad.38, bf16[9,64,64]{2,1,0:T(8,128)(2,1)S(1)} %copy-done.3), kind=kOutput, calls=%fused_computation.44 | convolution fusion | flops 201326592 | bytes 9519104 | tf_op jit(solution)/shard_map/oc,c...->o.../dot_general | solution.py:42
  205.4 3.7 %fusion.30 = f32[96,256,64]{1,2,0:T(8,128)} fusion(bf16[64,98,1,256]{3,0,1,2:T(8,128)(2,1)S(1)} %pad.38, bf16[9,64,64]{2,1,0:T(8,128)(2,1)S(1)} %copy-done.3), kind=kOutput, calls=%fused_computation.46 | convolution fusion | flops 201326592 | bytes 9519104 | tf_op jit(solution)/shard_map/oc,c...->o.../dot_general | solution.py:42
  216.3 15.3 %maximum_convert_fusion = bf16[96,256,64]{1,2,0:T(8,128)(2,1)S(1)} fusion(f32[96,256,64]{1,2,0:T(8,128)} %fusion.75, f32[96,256,64]{1,2,0:T(8,128)} %fusion.30, f32[96,256,64]{1,2,0:T(8,128)} %fusion.27, f32[96,256,64]{1,2,0:T(8,128)} %fusion.79, f32[96,256,64]{1,2,0:T(8,128)} %fusion.24, f32[96,256,64]{1,2,0:T(8,128)} %fusion.21, ...), kind=kOutput, calls=%fused_computation.3 | convolution fusion | flops 218628096 | bytes 56705536 | tf_op jit(solution)/shard_map/oc,c...->o.../dot_general | solution.py:42
  245.3 7.2 %all-to-all-done.1 = f32[96,1,256]{2,1,0:T(1,128)S(1)} async-done(((f32[96,1,256]{2,1,0:T(1,128)}), f32[96,1,256]{2,1,0:T(1,128)S(1)}, u32[]{:S(2)}, u32[]{:S(2)}) %all-to-all-start.1) | async-done | bytes 98336 | tf_op jit(solution)/shard_map/all_to_all | solution.py:130
  (85 shorter events, 57.7 us)
Async XLA Ops:
  0.6 19.8 %copy-start.2 = (bf16[9,64,64]{2,1,0:T(8,128)(2,1)S(1)}, bf16[9,64,64]{2,1,0:T(8,128)(2,1)}, u32[]{:S(2)}) copy-start(bf16[9,64,64]{2,1,0:T(8,128)(2,1)} %param.22) | copy-start | bytes 221188
  2.3 4.3 %collective-permute-start = (bf16[1,12,1,256]{3,2,1,0:T(2,128)(2,1)S(1)}, bf16[1,12,1,256]{3,2,1,0:T(2,128)(2,1)S(1)}, u32[]{:S(2)}, u32[]{:S(2)}) collective-permute-start(bf16[1,12,1,256]{3,2,1,0:T(2,128)(2,1)S(1)} %get-tuple-element.28), channel_id=1, source_target_pairs={{0,1},{1,2},{2,3},{3,4},{4,5},{5,6},{6,7},{7,8},{8,9},{9,10},{10,1... | collective-permute-start | bytes 18440 | tf_op jit(solution)/shard_map/ppermute | solution.py:20
  3.6 4.9 %collective-permute-start.1 = (bf16[1,12,1,256]{3,2,1,0:T(2,128)(2,1)S(1)}, bf16[1,12,1,256]{3,2,1,0:T(2,128)(2,1)S(1)}, u32[]{:S(2)}, u32[]{:S(2)}) collective-permute-start(bf16[1,12,1,256]{3,2,1,0:T(2,128)(2,1)S(1)} %get-tuple-element.29), channel_id=1, source_target_pairs={{1,0},{2,1},{3,2},{4,3},{5,4},{6,5},{7,6},{8,7},{9,8},{10,9},{11,1... | collective-permute-start | bytes 18440 | tf_op jit(solution)/shard_map/ppermute | solution.py:21
  14.2 9.8 %collective-permute-start.2 = (bf16[64,12,1,256]{3,0,2,1:T(8,128)(2,1)S(1)}, bf16[64,12,1,256]{3,0,2,1:T(8,128)(2,1)S(1)}, u32[]{:S(2)}, u32[]{:S(2)}) collective-permute-start(bf16[64,12,1,256]{3,0,2,1:T(8,128)(2,1)S(1)} %get-tuple-element.8), channel_id=1, source_target_pairs={{0,1},{1,2},{2,3},{3,4},{4,5},{5,6},{6,7},{7,8},{8,9},{9,10},{10,1... | collective-permute-start | bytes 1179656 | tf_op jit(solution)/shard_map/ppermute | solution.py:20
  18.6 5.5 %collective-permute-start.3 = (bf16[64,12,1,256]{3,0,2,1:T(8,128)(2,1)S(1)}, bf16[64,12,1,256]{3,0,2,1:T(8,128)(2,1)S(1)}, u32[]{:S(2)}, u32[]{:S(2)}) collective-permute-start(bf16[64,12,1,256]{3,0,2,1:T(8,128)(2,1)S(1)} %get-tuple-element.9), channel_id=1, source_target_pairs={{1,0},{2,1},{3,2},{4,3},{5,4},{6,5},{7,6},{8,7},{9,8},{10,9},{11,1... | collective-permute-start | bytes 1179656 | tf_op jit(solution)/shard_map/ppermute | solution.py:21
  50.0 3.6 %copy-start.8 = (f32[64]{0:T(128)S(1)}, f32[64]{0:T(128)}, u32[]{:S(2)}) copy-start(f32[64]{0:T(128)} %param.23) | copy-start | bytes 772
  71.6 21.5 %collective-permute-start.4 = (bf16[64,12,1,256]{3,0,2,1:T(8,128)(2,1)}, bf16[64,12,1,256]{3,0,2,1:T(8,128)(2,1)S(1)}, u32[]{:S(2)}, u32[]{:S(2)}) collective-permute-start(bf16[64,12,1,256]{3,0,2,1:T(8,128)(2,1)} %get-tuple-element.6), channel_id=1, source_target_pairs={{0,1},{1,2},{2,3},{3,4},{4,5},{5,6},{6,7},{7,8},{8,9},{9,10},{10,1... | collective-permute-start | bytes 1179656 | tf_op jit(solution)/shard_map/ppermute | solution.py:20
  79.8 13.2 %collective-permute-start.5 = (bf16[64,12,1,256]{3,0,2,1:T(8,128)(2,1)}, bf16[64,12,1,256]{3,0,2,1:T(8,128)(2,1)}, u32[]{:S(2)}, u32[]{:S(2)}) collective-permute-start(bf16[64,12,1,256]{3,0,2,1:T(8,128)(2,1)} %get-tuple-element.7), channel_id=1, source_target_pairs={{1,0},{2,1},{3,2},{4,3},{5,4},{6,5},{7,6},{8,7},{9,8},{10,9},{11,1... | collective-permute-start | bytes 1179656 | tf_op jit(solution)/shard_map/ppermute | solution.py:21
  85.8 6.7 %copy-start.6 = (bf16[9,1,64]{2,0,1:T(8,128)(2,1)S(1)}, bf16[9,1,64]{2,0,1:T(8,128)(2,1)}, u32[]{:S(2)}) copy-start(bf16[9,1,64]{2,0,1:T(8,128)(2,1)} %param.24) | copy-start | bytes 3460
  103.4 2.3 copy-start.1
  103.4 2.7 %copy-start = (bf16[1,1024,8,256]{1,3,2,0:T(8,128)(2,1)S(1)}, bf16[1,1024,8,256]{1,3,2,0:T(8,128)(2,1)}, u32[]{:S(2)}) copy-start(bf16[1,1024,8,256]{1,3,2,0:T(8,128)(2,1)} %copy.67) | copy-start | bytes 12582916
  103.9 57.0 %copy-start.4 = (f32[1024,12]{0,1:T(8,128)S(1)}, f32[1024,12]{0,1:T(8,128)}, u32[]{:S(2)}) copy-start(f32[1024,12]{0,1:T(8,128)} %param.17) | copy-start | bytes 147460
  105.7 67.2 %copy-start.5 = (bf16[9,64,1]{1,0,2:T(8,128)(2,1)S(1)}, bf16[9,64,1]{1,0,2:T(8,128)(2,1)}, u32[]{:S(2)}) copy-start(bf16[9,64,1]{1,0,2:T(8,128)(2,1)} %param.25) | copy-start | bytes 3460
  105.7 75.5 %copy-start.9 = (f32[64]{0:T(128)S(1)}, f32[64]{0:T(128)}, u32[]{:S(2)}) copy-start(f32[64]{0:T(128)} %param.26) | copy-start | bytes 772
  106.7 79.1 %copy-start.3 = (bf16[9,64,64]{2,1,0:T(8,128)(2,1)S(1)}, bf16[9,64,64]{2,1,0:T(8,128)(2,1)}, u32[]{:S(2)}) copy-start(bf16[9,64,64]{2,1,0:T(8,128)(2,1)} %param.27) | copy-start | bytes 221188
  165.0 16.0 %all-to-all-start = ((f32[12,8,256]{2,0,1:T(8,128)}), f32[12,8,256]{2,0,1:T(8,128)S(1)}, u32[]{:S(2)}, u32[]{:S(2)}) async-start(f32[12,8,256]{2,0,1:T(8,128)} %fusion.105), calls=%async_computation | async-start | bytes 262144 | tf_op jit(solution)/shard_map/all_to_all | solution.py:117
  212.7 3.6 %copy-start.10 = (f32[64]{0:T(128)S(1)}, f32[64]{0:T(128)}, u32[]{:S(2)}) copy-start(f32[64]{0:T(128)} %param.28) | copy-start | bytes 772
  231.6 0.7 copy-start.7
  241.3 11.2 %all-to-all-start.1 = ((f32[96,1,256]{2,1,0:T(1,128)}), f32[96,1,256]{2,1,0:T(1,128)S(1)}, u32[]{:S(2)}, u32[]{:S(2)}) async-start(f32[96,1,256]{2,1,0:T(1,128)} %copy.29), calls=%async_computation.1 | async-start | bytes 196608 | tf_op jit(solution)/shard_map/all_to_all | solution.py:130
where the time goes:
time: 257 us; the launch traced here: 253 us
  matrix products  112 us (44%)
  blocking collectives  54.2 us (21%)
  starting transfers between devices  29.8 us (12%)
  other arithmetic  21.7 us (8%)
  waiting for transfers between devices  17.1 us (7%)
  local copies, waits for them, and re-layouts  15.6 us (6%)
  between operations  2.72 us (1%)
    dot_general x36, matrix products, plane_conv(): jnp.einsum('oc,c...->o...', taps[3 * tap_row + tap_col], shifted, preferr...  108 us
    psum x1, blocking collectives, per_device(): sinogram = lax.psum(partial_sino, 'gy')  54.2 us
    ppermute x3, starting transfers between devices, with_halo(): before = lax.ppermute(last, axis, up)  13.9 us
    convert_element_type x2, other arithmetic, activate(): jnp.maximum(summed + bias[:, None, None, None], 0.0).astype(jnp.bfloat16)  9.96 us
    concatenate x3, other arithmetic, with_halo(): value = jnp.concatenate([before, value, after], axis=dim)  9.21 us
    all_to_all x1, waiting for transfers between devices, per_device(): lax.all_to_all(corrected, 'gz', split_axis=1, concat_axis=0, tiled=True)  8.01 us
    all_to_all x1, starting transfers between devices, per_device(): lax.all_to_all(corrected, 'gz', split_axis=1, concat_axis=0, tiled=True)  7.93 us
    all_to_all x1, waiting for transfers between devices, per_device(): lax.all_to_all(standing_out, 'gz', split_axis=0, concat_axis=1, tiled=True)  7.19 us
  transfers between devices with their start and end apart: 8, of which 3 were waited for; matrix products, arithmetic and copies ran while one was open for 7% of the time, Pallas kernels for 0%

commit v1 on v0

v1 whole, which is shorter than its diff:
```python
import functools

import jax
import jax.numpy as jnp
import numpy as np
from jax import lax
from jax.experimental import pallas as pl
from jax.experimental.pallas import tpu as pltpu
from jax.sharding import PartitionSpec as P

SUBSETS = 4
SIGMA_STEP = 0.002
RELAX_TOP = 4.0
HALO = 3
BF = jnp.bfloat16
F32 = jnp.float32
VMEM_LIMIT = 48 << 20


def noise_scales(timestep):
    sigma = timestep[0].astype(F32) * SIGMA_STEP
    scale_in = 1.0 / jnp.sqrt(1.0 + sigma * sigma)
    return (scale_in, sigma * scale_in)


def entry_selector(own, first, second, ones, slots):
    rows = own + 4
    table = np.zeros((2, rows, 11, 3, slots), np.float32)
    for parity in range(2):
        before, after = (second, first) if parity == 0 else (first, second)
        place = (
            [before + k for k in range(HALO)]
            + list(range(own))
            + [after + k for k in range(HALO)]
        )
        for row in range(rows):
            for a in range(3):
                for b in range(3):
                    table[parity, row, 3 * a + b, b, place[row + a]] = 1.0
            table[parity, row, 9, 1, ones] = 1.0
            table[parity, row, 10, 1, ones + 1] = 1.0
    return table.reshape(2, rows, 11, 3 * slots)


def layer_weights(first_taps, first_bias, middle_taps, middle_bias, last_taps, selector, own, index, count):
    rows_one, rows_two = own + 4, own + 2
    base = index * own
    total = count * own
    row_one = base - 2 + jnp.arange(rows_one)
    keep_one = ((row_one >= 0) & (row_one < total)).astype(F32)
    row_two = base - 1 + jnp.arange(rows_two)
    keep_two = ((row_two >= 0) & (row_two < total)).astype(F32)
    high = first_bias.astype(BF)
    low = (first_bias - high.astype(F32)).astype(BF)
    stack = jnp.concatenate([first_taps[:, :, 0], high[None], low[None]], axis=0)
    chosen = lax.dynamic_index_in_dim(jnp.asarray(selector, BF), index % 2, 0, keepdims=False)
    one = jnp.einsum("ko,ikq->ioq", stack, chosen, preferred_element_type=F32)
    one = (one * keep_one[:, None, None]).astype(BF).reshape(rows_one * 64, -1)
    middle = middle_taps.reshape(3, 3, 64, 64).transpose(0, 2, 1, 3).reshape(192, 192)
    padded = -(-own // 8) * 8
    spread = np.zeros((padded, rows_two, 3), np.float32)
    for i in range(own):
        for a in range(3):
            spread[i, i + a, a] = 1.0
    last = jnp.einsum(
        "ija,abc->bijc",
        jnp.asarray(spread, BF),
        last_taps.reshape(3, 3, 64),
        preferred_element_type=F32,
    )
    last = (last * keep_two[None, None, :, None]).astype(BF).reshape(3 * padded, rows_two * 64)
    bias = jnp.broadcast_to(middle_bias[:, None], (64, 256))
    return one, middle, bias, last


def shifted(block):
    lane = lax.broadcasted_iota(jnp.int32, block.shape, 1)
    zero = jnp.zeros((), block.dtype)
    across = block.shape[1]
    left = jnp.where(lane == 0, zero, pltpu.roll(block, 1, 1))
    right = jnp.where(lane == across - 1, zero, pltpu.roll(block, across - 1, 1))
    return left, right


def network(entry, rows_one, one_ref, middle_ref, bias_ref, last_ref, taps_ref, hidden_ref):
    left, right = shifted(entry.astype(F32))
    spread = jnp.concatenate([left.astype(BF), entry, right.astype(BF)], axis=0)
    for row in range(rows_one):
        hidden = jnp.dot(one_ref[row * 64 : (row + 1) * 64, :], spread, preferred_element_type=F32)
        hidden = jnp.maximum(hidden, 0.0).astype(BF)
        left, right = shifted(hidden)
        taps_ref[row * 192 : row * 192 + 64, :] = left
        taps_ref[row * 192 + 64 : row * 192 + 128, :] = hidden
        taps_ref[row * 192 + 128 : row * 192 + 192, :] = right
    bias = bias_ref[...]
    held = []
    for row in range(rows_one):
        held.append(
            jnp.dot(
                middle_ref[...], taps_ref[row * 192 : (row + 1) * 192, :], preferred_element_type=F32
            )
        )
        if row >= 2:
            out = row - 2
            summed = held[out][0:64] + held[out + 1][64:128] + held[out + 2][128:192] + bias
            hidden_ref[out * 64 : (out + 1) * 64, :] = jnp.maximum(summed, 0.0).astype(BF)
    last = jnp.dot(last_ref[...], hidden_ref[...], preferred_element_type=F32)
    rows = last.shape[0] // 3
    left, _ = shifted(last[0:rows])
    _, right = shifted(last[2 * rows :])
    return left + last[rows : 2 * rows] + right


def axial_kernel(
    view_ref,
    scale_ref,
    volume_ref,
    entry_ref,
    one_ref,
    middle_ref,
    bias_ref,
    last_ref,
    fold_ref,
    projector_ref,
    axial_ref,
    partial_ref,
    taps_ref,
    hidden_ref,
    chosen_ref,
    picked_ref,
    sem,
):
    copy = pltpu.make_async_copy(projector_ref.at[view_ref[0]], chosen_ref, sem)
    copy.start()
    axial_ref[...] = jnp.zeros_like(axial_ref)
    scale_out = scale_ref[1]

    def plane(p, carry):
        net = network(entry_ref[p], 12, one_ref, middle_ref, bias_ref, last_ref, taps_ref, hidden_ref)
        value = volume_ref[p] + scale_out * net
        for y in range(8):
            axial_ref[y, pl.ds(p, 1), :] = value[y : y + 1, :]
        return carry

    lax.fori_loop(0, 12, plane, 0)
    copy.wait()
    flat = axial_ref[...].reshape(128, 256).astype(BF)
    lane = lax.broadcasted_iota(jnp.int32, (16, 256), 1) % 8
    for part in range(32):
        product = lax.dot_general(
            flat,
            chosen_ref[part * 256 : (part + 1) * 256, :],
            (((1,), (1,)), ((), ())),
            preferred_element_type=F32,
        )
        picked = product[0:16]
        for y in range(1, 8):
            picked = jnp.where(lane == y, product[y * 16 : (y + 1) * 16], picked)
        row, column = (part // 4) * 16, (part % 4) * 256
        picked_ref[row : row + 16, column : column + 256] = picked
    picked = picked_ref[...]
    high = picked.astype(BF)
    low = (picked - high.astype(F32)).astype(BF)
    fold = fold_ref[...]
    partial_ref[...] = jnp.dot(high, fold, preferred_element_type=F32) + jnp.dot(
        low, fold, preferred_element_type=F32
    )


def back_kernel(
    view_ref,
    place_ref,
    scale_ref,
    measured_ref,
    sinogram_ref,
    axial_ref,
    unfold_ref,
    projector_ref,
    corrected_ref,
    residual_ref,
    chosen_ref,
    held_ref,
    turned_ref,
    sems,
):
    copies = []
    for part in range(8):
        rows = pl.ds(part * 1024, 1024)
        copies.append(
            pltpu.make_async_copy(
                projector_ref.at[view_ref[0], rows], chosen_ref.at[rows], sems.at[part]
            )
        )
        copies[-1].start()
    residual = measured_ref[...] - sinogram_ref[...]
    held_ref[...] = residual
    wide = jnp.dot(residual.astype(BF), unfold_ref[...], preferred_element_type=F32).astype(BF)
    lane = lax.broadcasted_iota(jnp.int32, (16, 1024), 1) % 8
    zero = jnp.zeros((), BF)
    total = jnp.zeros((128, 256), F32)
    for part in range(8):
        rays = wide[part * 16 : (part + 1) * 16]
        spread = jnp.concatenate([jnp.where(lane == y, rays, zero) for y in range(8)], axis=0)
        copies[part].wait()
        total = total + jnp.dot(
            spread, chosen_ref[part * 1024 : (part + 1) * 1024, :], preferred_element_type=F32
        )
    corrected_ref[...] = axial_ref[...] + scale_ref[2] * total.reshape(8, 16, 256)
    block = held_ref[pl.ds(pl.multiple_of(place_ref[0] * 16, 16), 16), :]
    turned_ref[...] = block.T
    start = pl.multiple_of(place_ref[1] * 64, 64)
    residual_ref[...] = turned_ref[pl.ds(start, 64), 0:12]


def coronal_kernel(
    scale_ref,
    corrected_ref,
    entry_ref,
    one_ref,
    middle_ref,
    bias_ref,
    last_ref,
    restored_ref,
    taps_ref,
    hidden_ref,
):
    scale_out = scale_ref[1]

    def plane(p, carry):
        net = network(entry_ref[p], 16, one_ref, middle_ref, bias_ref, last_ref, taps_ref, hidden_ref)
        value = corrected_ref[p] + scale_out * net
        for z in range(12):
            restored_ref[z, pl.ds(p, 1), :] = value[z : z + 1, :]
        return carry

    lax.fori_loop(0, 8, plane, 0)


def vmem():
    return pl.BlockSpec(memory_space=pltpu.VMEM)


def smem():
    return pl.BlockSpec(memory_space=pltpu.SMEM)


def params():
    return pltpu.CompilerParams(vmem_limit_bytes=VMEM_LIMIT)


def inner_pairs(size):
    return [(i, i ^ 1) for i in range(size)]


def outer_pairs(size):
    ups = [(i, i + 1) for i in range(1, size - 1, 2)]
    return ups + [(j, i) for i, j in ups]


def exchange(leading, trailing, axis):
    size = lax.axis_size(axis)
    odd = lax.axis_index(axis) % 2 == 1
    inner = jnp.where(odd, leading, trailing)
    outer = jnp.where(odd, trailing, leading)
    second = lax.ppermute(outer, axis, outer_pairs(size))
    first = lax.ppermute(inner, axis, inner_pairs(size))
    return first, second


def sum_over_gy(partial):
    def partner(value, bits):
        return lax.ppermute(value, "gy", [(i, i ^ bits) for i in range(16)]).astype(F32)

    total = partial
    total = total + partner(total.astype(BF), 1)
    total = total + partner(total.astype(BF), 2)
    sent = total.astype(BF)
    return total + partner(sent, 4) + partner(sent, 8) + partner(sent, 12)


AXIAL_SELECTOR = entry_selector(8, 8, 11, 14, 16)
CORONAL_SELECTOR = entry_selector(12, 16, 19, 30, 32)
FOLD = np.repeat(np.eye(128, dtype=np.float32), 8, axis=0)


def per_device(
    volume,
    projector,
    measured,
    subset,
    timestep,
    axial_in,
    axial_bias_in,
    axial_mid,
    axial_bias_mid,
    axial_out,
    coronal_in,
    coronal_bias_in,
    coronal_mid,
    coronal_bias_mid,
    coronal_out,
):
    scale_in, scale_out = noise_scales(timestep)
    view = subset % SUBSETS
    epoch = (subset[0] // SUBSETS).astype(F32)
    relax = RELAX_TOP / (1.0 + epoch / 64.0)
    scales = jnp.stack([scale_in, scale_out, relax])
    gy, gz = lax.axis_index("gy"), lax.axis_index("gz")
    size_y, size_z = lax.axis_size("gy"), lax.axis_size("gz")
    place = jnp.stack([gy // 2, gy % 2]).astype(jnp.int32)

    entry = (volume * scale_in).astype(BF)
    first, second = exchange(entry[:, :HALO], entry[:, -HALO:], "gy")
    axial_weights = layer_weights(
        axial_in, axial_bias_in, axial_mid, axial_bias_mid, axial_out, AXIAL_SELECTOR, 8, gy, size_y
    )
    coronal_weights = layer_weights(
        coronal_in,
        coronal_bias_in,
        coronal_mid,
        coronal_bias_mid,
        coronal_out,
        CORONAL_SELECTOR,
        12,
        gz,
        size_z,
    )
    flat_projector = projector.reshape(4, 8192, 256)
    turned = jnp.pad(measured.reshape(8, 128, 12).transpose(0, 2, 1), ((0, 0), (0, 4), (0, 0)))
    turned = turned.reshape(128, 128)
    axial_entry = jnp.concatenate([entry, first, second, jnp.ones((12, 2, 256), BF)], axis=1)
    axial, partial = pl.pallas_call(
        axial_kernel,
        name="axial",
        out_shape=(
            jax.ShapeDtypeStruct((8, 16, 256), F32),
            jax.ShapeDtypeStruct((128, 128), F32),
        ),
        in_specs=[smem(), smem()] + [vmem()] * 7 + [pl.BlockSpec(memory_space=pl.ANY)],
        out_specs=(vmem(), vmem()),
        scratch_shapes=[
            pltpu.VMEM((12 * 192, 256), BF),
            pltpu.VMEM((10 * 64, 256), BF),
            pltpu.VMEM((8192, 256), BF),
            pltpu.VMEM((128, 1024), F32),
            pltpu.SemaphoreType.DMA,
        ],
        compiler_params=params(),
    )(view, scales, volume, axial_entry, *axial_weights, jnp.asarray(FOLD, BF), flat_projector)
    sinogram = sum_over_gy(partial)
    corrected, residual = pl.pallas_call(
        back_kernel,
        name="back",
        out_shape=(
            jax.ShapeDtypeStruct((8, 16, 256), F32),
            jax.ShapeDtypeStruct((64, 12), F32),
        ),
        in_specs=[smem(), smem(), smem()] + [vmem()] * 4 + [pl.BlockSpec(memory_space=pl.ANY)],
        out_specs=(vmem(), vmem()),
        scratch_shapes=[
            pltpu.VMEM((8192, 256), BF),
            pltpu.VMEM((128, 128), F32),
            pltpu.VMEM((128, 16), F32),
            pltpu.SemaphoreType.DMA((8,)),
        ],
        compiler_params=params(),
    )(view, place, scales, turned, sinogram, axial, jnp.asarray(FOLD.T, BF), flat_projector)
    entry = (corrected * scale_in).astype(BF)
    first, second = exchange(entry[:, :HALO], entry[:, 12 - HALO : 12], "gz")
    coronal_entry = jnp.concatenate(
        [entry, first, second, jnp.zeros((8, 8, 256), BF), jnp.ones((8, 2, 256), BF)], axis=1
    )
    restored = pl.pallas_call(
        coronal_kernel,
        name="coronal",
        out_shape=jax.ShapeDtypeStruct((12, 8, 256), F32),
        in_specs=[smem()] + [vmem()] * 6,
        out_specs=vmem(),
        scratch_shapes=[
            pltpu.VMEM((16 * 192, 256), BF),
            pltpu.VMEM((14 * 64, 256), BF),
        ],
        compiler_params=params(),
    )(scales, corrected, coronal_entry, *coronal_weights)
    return (restored, residual)


def solution(mesh):
    in_specs = (
        P("gz", "gy", None),
        P(None, None, "gy", None),
        P(None, "gz"),
    ) + (P(),) * 12
    out_specs = (P("gz", "gy", None), P("gy", "gz"))
    return jax.shard_map(
        per_device, mesh=mesh, in_specs=in_specs, out_specs=out_specs, check_vma=False
    )
```

time: 257 us -> 73.2 us (0.28)
  the two profiles are of different devices: /device:TPU:0 before, /device:TPU:6 now
where the time goes in v1:
time: 73.2 us; the launch traced here: 72.2 us
  Pallas kernels  29 us (40%)
  starting transfers between devices  16 us (22%)
  waiting for transfers between devices  11.4 us (16%)
  local copies, waits for them, and re-layouts  7.23 us (10%)
  matrix products  3.33 us (5%)
  other arithmetic  2.76 us (4%)
  between operations  2.39 us (3%)
    pallas_call x1, Pallas kernels, per_device(): pl.pallas_call(axial_kernel, name='axial', out_shape=(jax.ShapeDtypeStruc...  15 us
    pallas_call x1, Pallas kernels, per_device(): pl.pallas_call(coronal_kernel, name='coronal', out_shape=jax.ShapeDtypeSt...  10.7 us
    ppermute x5, waiting for transfers between devices, partner(): lax.ppermute(value, 'gy', [(i, i ^ bits) for i in range(16)]).astype(F32)  8.66 us
    ppermute x2, starting transfers between devices, exchange(): second = lax.ppermute(outer, axis, outer_pairs(size))  7.8 us
    ppermute x5, starting transfers between devices, partner(): lax.ppermute(value, 'gy', [(i, i ^ bits) for i in range(16)]).astype(F32)  6.15 us
    unnamed x16, local copies, waits for them, and re-layouts  3.4 us
    pallas_call x1, Pallas kernels, per_device(): pl.pallas_call(back_kernel, name='back', out_shape=(jax.ShapeDtypeStruct(...  3.35 us
    ppermute x2, waiting for transfers between devices, exchange(): second = lax.ppermute(outer, axis, outer_pairs(size))  2.78 us
  transfers between devices with their start and end apart: 9, of which 5 were waited for; matrix products, arithmetic and copies ran while one was open for 13% of the time, Pallas kernels for 0%

profile of v1, /device:TPU:6, one launch (start us, length us, event | category | flops | bytes accessed | tf_op | source)
XLA Modules:
  0.0 72.2 jit_solution(9410317590245278804)
XLA Ops:
  1.4 0.9 %multiply_convert_fusion.1 = bf16[12,8,256]{2,1,0:T(8,128)(2,1)S(1)} fusion(f32[12,8,256]{2,1,0:T(8,128)} %volume_ref.1, f32[]{:T(128)} %bitcast.1), kind=kLoop, calls=%fused_computation.15 | loop fusion | flops 49152 | bytes 147460 | tf_op jit(solution)/shard_map/convert_element_type | solution.py:312
  2.4 2.8 %collective-permute-start.1 = (bf16[12,3,256]{2,1,0:T(4,128)(2,1)S(1)}, bf16[12,3,256]{2,1,0:T(4,128)(2,1)S(1)}, u32[]{:S(2)}, u32[]{:S(2)}) collective-permute-start(bf16[12,3,256]{2,1,0:T(4,128)(2,1)S(1)} %get-tuple-element.17), channel_id=1, source_target_pairs={{1,2},{3,4},{5,6},{7,8},{9,10},{11,12},{13,14},{2,1},{4,3},{6,5},{... | collective-permute-start | bytes 55304 | tf_op jit(solution)/shard_map/ppermute | solution.py:265
  5.3 0.7 %convert_bitcast_fusion.3 = (bf16[1,64]{1,0:T(2,128)(2,1)S(1)}, bf16[1,64]{1,0:T(2,128)(2,1)S(1)}) fusion(f32[64]{0:T(128)} %param.27), kind=kLoop, calls=%fused_computation.54 | loop fusion | flops 256 | bytes 512 | tf_op jit(solution)/shard_map/broadcast_in_dim | solution.py:55
  8.2 0.9 %fusion.6 = bf16[3,8,10,64]{3,2,0,1:T(8,128)(2,1)S(1)} fusion(bf16[8,10,3,1]{1,2,3,0:T(4,128)(2,1)} %constant.145, f32[10]{0:T(128)S(1)} %and_convert_fusion.2, bf16[3,3,64]{2,1,0:T(4,128)(2,1)S(1)} %reshape.92), kind=kOutput, calls=%fused_computation.10 | convolution fusion | flops 122880 | bytes 32392 | tf_op jit(solution)/shard_map/ija,abc->bijc/dot_general | solution.py:65
  9.2 1.0 %fusion.4 = bf16[12,64,48]{1,2,0:T(8,128)(2,1)S(1)} fusion(f32[12]{0:T(128)S(1)} %and_convert_fusion.3, bf16[2,12,11,48]{3,2,1,0:T(8,128)(2,1)} %constant.134.clone, s32[]{:T(128)S(6)} %select_n.69, bf16[1,64]{1,0:T(2,128)(2,1)S(1)} %get-tuple-element.21, bf16[1,64]{1,0:T(2,128)(2,1)S(1)} %get-tuple-element.20, bf16[9,64]{1,0:T(8,128)(2,1)} %bitcast.92), kind=kOutput, calls=%fused_computation.8 | convolution fusion | flops 888960 | bytes 127284 | tf_op jit(solution)/shard_map/ko,ikq->ioq/dot_general | solution.py:57
  10.2 1.1 %fusion = bf16[16,96,64]{1,2,0:T(8,128)(2,1)S(1)} fusion(f32[16]{0:T(128)S(1)} %and_convert_fusion.1, bf16[2,16,11,96]{3,2,1,0:T(8,128)(2,1)} %constant.136.clone, s32[]{:T(128)S(6)} %select_n.74, bf16[1,64]{1,0:T(2,128)(2,1)S(1)} %get-tuple-element.19, bf16[1,64]{1,0:T(2,128)(2,1)S(1)} %get-tuple-element.18, bf16[9,64]{1,0:T(8,128)(2,1)} %bitcast.93), kind=kOutput, calls=%fused_computation.1 | convolution fusion | flops 2363520 | bytes 266564 | tf_op jit(solution)/shard_map/ko,ikq->ioq/dot_general | solution.py:57
  11.7 1.0 %copy.56 = bf16[3,3,64,64]{3,1,2,0:T(4,128)(2,1)S(1)} copy(bf16[3,3,64,64]{3,2,1,0:T(8,128)(2,1)} %bitcast.89) | data formatting | bytes 147456 | tf_op jit(solution)/shard_map/reshape | solution.py:59
  12.9 0.9 %copy.43 = f32[2,8,8,128]{3,2,1,0:T(8,128)S(1)} copy(f32[2,8,8,128]{3,1,2,0:T(8,128)} %bitcast.91) | data formatting | bytes 131072
  14.7 0.9 %copy-done = f32[12,8,256]{2,1,0:T(8,128)S(1)} copy-done((f32[12,8,256]{2,1,0:T(8,128)S(1)}, f32[12,8,256]{2,1,0:T(8,128)}, u32[]{:S(2)}) %copy-start) | copy-done | bytes 98328
  15.6 0.9 %copy-done.1 = bf16[1024,128]{1,0:T(8,128)(2,1)S(1)} copy-done((bf16[1024,128]{1,0:T(8,128)(2,1)S(1)}, bf16[1024,128]{1,0:T(8,128)(2,1)}, u32[]{:S(2)}) %copy-start.1) | copy-done | bytes 262168
  16.5 15.0 %axial.1 = (f32[8,16,256]{2,1,0:T(8,128)S(1)}, f32[128,128]{1,0:T(8,128)S(1)}) custom-call(s32[1]{0:T(128)S(6)} %select_n.63.view_ref, f32[3]{0:T(128)S(1)} %pad_maximum_fusion.scale_ref, f32[12,8,256]{2,1,0:T(8,128)S(1)} %copy-done, bf16[12,16,256]{2,1,0:T(8,128)(2,1)S(1)} %maximum_maximum_fusion.entry_ref, bf16[768,48]{1,0:T(8,128)(2,1)S(1)} %bitcast.81, ...), custom_call_target="tpu_custom_call" | custom-call | tf_op jit(solution)/shard_map/axial/pallas_call | solution.py:332
  31.5 1.1 %collective-permute-start.2 = (bf16[128,128]{1,0:T(8,128)(2,1)S(1)}, bf16[128,128]{1,0:T(8,128)(2,1)S(1)}, u32[]{:S(2)}, u32[]{:S(2)}) collective-permute-start(bf16[128,128]{1,0:T(8,128)(2,1)S(1)} %convert_element_type.121), channel_id=1, source_target_pairs={{0,1},{1,0},{2,3},{3,2},{4,5},{5,4},{6,7},{7,6},{8,9},{9,8},{10,11... | collective-permute-start | bytes 98312 | tf_op jit(solution)/shard_map/ppermute | solution.py:272
  32.6 0.9 %collective-permute-done.2 = bf16[128,128]{1,0:T(8,128)(2,1)S(1)} collective-permute-done((bf16[128,128]{1,0:T(8,128)(2,1)S(1)}, bf16[128,128]{1,0:T(8,128)(2,1)S(1)}, u32[]{:S(2)}, u32[]{:S(2)}) %collective-permute-start.2) | collective-permute-done | bytes 32800 | tf_op jit(solution)/shard_map/ppermute | solution.py:272
  33.8 3.7 %collective-permute-done.3 = bf16[128,128]{1,0:T(8,128)(2,1)S(1)} collective-permute-done((bf16[128,128]{1,0:T(8,128)(2,1)S(1)}, bf16[128,128]{1,0:T(8,128)(2,1)S(1)}, u32[]{:S(2)}, u32[]{:S(2)}) %collective-permute-start.3) | collective-permute-done | bytes 32800 | tf_op jit(solution)/shard_map/ppermute | solution.py:272
  37.5 1.7 %collective-permute-start.4 = (bf16[128,128]{1,0:T(8,128)(2,1)S(1)}, bf16[128,128]{1,0:T(8,128)(2,1)S(1)}, u32[]{:S(2)}, u32[]{:S(2)}) collective-permute-start(bf16[128,128]{1,0:T(8,128)(2,1)S(1)} %fusion.12), channel_id=1, source_target_pairs={{0,4},{1,5},{2,6},{3,7},{4,0},{5,1},{6,2},{7,3},{8,12},{9,13},{10,... | collective-permute-start | bytes 98312 | tf_op jit(solution)/shard_map/ppermute | solution.py:272
  39.2 2.2 %collective-permute-start.5 = (bf16[128,128]{1,0:T(8,128)(2,1)S(1)}, bf16[128,128]{1,0:T(8,128)(2,1)S(1)}, u32[]{:S(2)}, u32[]{:S(2)}) collective-permute-start(bf16[128,128]{1,0:T(8,128)(2,1)S(1)} %fusion.12), channel_id=1, source_target_pairs={{0,8},{1,9},{2,10},{3,11},{4,12},{5,13},{6,14},{7,15},{8,0},{9,1},... | collective-permute-start | bytes 98312 | tf_op jit(solution)/shard_map/ppermute | solution.py:272
  41.4 0.9 %collective-permute-start.6 = (bf16[128,128]{1,0:T(8,128)(2,1)S(1)}, bf16[128,128]{1,0:T(8,128)(2,1)S(1)}, u32[]{:S(2)}, u32[]{:S(2)}) collective-permute-start(bf16[128,128]{1,0:T(8,128)(2,1)S(1)} %fusion.12), channel_id=1, source_target_pairs={{0,12},{1,13},{2,14},{3,15},{4,8},{5,9},{6,10},{7,11},{8,4},{9,5},... | collective-permute-start | bytes 98312 | tf_op jit(solution)/shard_map/ppermute | solution.py:272
  42.4 2.2 %collective-permute-done.5 = bf16[128,128]{1,0:T(8,128)(2,1)S(1)} collective-permute-done((bf16[128,128]{1,0:T(8,128)(2,1)S(1)}, bf16[128,128]{1,0:T(8,128)(2,1)S(1)}, u32[]{:S(2)}, u32[]{:S(2)}) %collective-permute-start.5) | collective-permute-done | bytes 32800 | tf_op jit(solution)/shard_map/ppermute | solution.py:272
  44.6 1.9 %collective-permute-done.6 = bf16[128,128]{1,0:T(8,128)(2,1)S(1)} collective-permute-done((bf16[128,128]{1,0:T(8,128)(2,1)S(1)}, bf16[128,128]{1,0:T(8,128)(2,1)S(1)}, u32[]{:S(2)}, u32[]{:S(2)}) %collective-permute-start.6) | collective-permute-done | bytes 32800 | tf_op jit(solution)/shard_map/ppermute | solution.py:272
  46.5 3.4 %back.1 = (f32[8,16,256]{2,1,0:T(8,128)S(1)}, f32[64,12]{1,0:T(8,128)S(1)}) custom-call(s32[1]{0:T(128)S(6)} %select_n.63.view_ref, s32[2]{0:T(128)S(1)} %pad_add_fusion.place_ref, f32[3]{0:T(128)S(1)} %pad_maximum_fusion.scale_ref, f32[128,128]{1,0:T(8,128)S(1)} %bitcast.82, f32[128,128]{1,0:T(8,128)S(1)} %convert_add_fusion.sinogram_ref, ...), custom_call_target="tpu_custom_call" | custom-call | tf_op jit(solution)/shard_map/back/pallas_call | solution.py:351
  50.0 2.0 %collective-permute-start.7 = (bf16[8,3,256]{2,1,0:T(4,128)(2,1)S(1)}, bf16[8,3,256]{2,1,0:T(4,128)(2,1)S(1)}, u32[]{:S(2)}, u32[]{:S(2)}) collective-permute-start(bf16[8,3,256]{2,1,0:T(4,128)(2,1)S(1)} %get-tuple-element.15), channel_id=1, source_target_pairs={{0,16},{16,0},{32,48},{48,32},{64,80},{80,64},{96,112},{112,96},{1... | collective-permute-start | bytes 36872 | tf_op jit(solution)/shard_map/ppermute | solution.py:266
  52.0 5.0 %collective-permute-start.8 = (bf16[8,3,256]{2,1,0:T(4,128)(2,1)S(1)}, bf16[8,3,256]{2,1,0:T(4,128)(2,1)S(1)}, u32[]{:S(2)}, u32[]{:S(2)}) collective-permute-start(bf16[8,3,256]{2,1,0:T(4,128)(2,1)S(1)} %get-tuple-element.14), channel_id=1, source_target_pairs={{16,32},{48,64},{80,96},{32,16},{64,48},{96,80},{17,33},{49,65},{8... | collective-permute-start | bytes 36872 | tf_op jit(solution)/shard_map/ppermute | solution.py:265
  58.4 2.8 %collective-permute-done.8 = bf16[8,3,256]{2,1,0:T(4,128)(2,1)S(1)} collective-permute-done((bf16[8,3,256]{2,1,0:T(4,128)(2,1)S(1)}, bf16[8,3,256]{2,1,0:T(4,128)(2,1)S(1)}, u32[]{:S(2)}, u32[]{:S(2)}) %collective-permute-start.8) | collective-permute-done | bytes 12320 | tf_op jit(solution)/shard_map/ppermute | solution.py:265
  61.5 10.7 %coronal.1 = f32[12,8,256]{2,1,0:T(8,128)} custom-call(f32[3]{0:T(128)S(1)} %pad_maximum_fusion.scale_ref, f32[8,16,256]{2,1,0:T(8,128)S(1)} %get-tuple-element.8.corrected_ref, bf16[8,32,256]{2,1,0:T(8,128)(2,1)S(1)} %concatenate.14.entry_ref, bf16[1024,96]{1,0:T(8,128)(2,1)S(1)} %bitcast.80, bf16[192,192]{1,0:T(8,128)(2,1)S(1)} %reshape.97.middle_ref, ...), custom_call_target="tpu_custom_call" | custom-call | tf_op jit(solution)/shard_map/coronal/pallas_call | solution.py:373
  (55 shorter events, 5.2 us)
Async XLA Ops:
  0.6 45.9 %copy-start.2 = (bf16[128,1024]{1,0:T(8,128)(2,1)S(1)}, bf16[128,1024]{1,0:T(8,128)(2,1)}, u32[]{:S(2)}) copy-start(bf16[128,1024]{1,0:T(8,128)(2,1)} %constant.139.clone.unfold_ref) | copy-start | bytes 786436
  0.6 41.7 %copy-start.5 = (bf16[9,1,64]{2,0,1:T(8,128)(2,1)S(1)}, bf16[9,1,64]{2,0,1:T(8,128)(2,1)}, u32[]{:S(2)}) copy-start(bf16[9,1,64]{2,0,1:T(8,128)(2,1)} %param.35) | copy-start | bytes 3460
  2.3 11.5 %collective-permute-start = (bf16[12,3,256]{2,1,0:T(4,128)(2,1)S(1)}, bf16[12,3,256]{2,1,0:T(4,128)(2,1)S(1)}, u32[]{:S(2)}, u32[]{:S(2)}) collective-permute-start(bf16[12,3,256]{2,1,0:T(4,128)(2,1)S(1)} %get-tuple-element.16), channel_id=1, source_target_pairs={{0,1},{1,0},{2,3},{3,2},{4,5},{5,4},{6,7},{7,6},{8,9},{9,8},{10,11... | collective-permute-start | bytes 55304 | tf_op jit(solution)/shard_map/ppermute | solution.py:266
  2.4 11.4 %collective-permute-start.1 = (bf16[12,3,256]{2,1,0:T(4,128)(2,1)S(1)}, bf16[12,3,256]{2,1,0:T(4,128)(2,1)S(1)}, u32[]{:S(2)}, u32[]{:S(2)}) collective-permute-start(bf16[12,3,256]{2,1,0:T(4,128)(2,1)S(1)} %get-tuple-element.17), channel_id=1, source_target_pairs={{1,2},{3,4},{5,6},{7,8},{9,10},{11,12},{13,14},{2,1},{4,3},{6,5},{... | collective-permute-start | bytes 55304 | tf_op jit(solution)/shard_map/ppermute | solution.py:265
  14.7 0.9 %copy-start = (f32[12,8,256]{2,1,0:T(8,128)S(1)}, f32[12,8,256]{2,1,0:T(8,128)}, u32[]{:S(2)}) copy-start(f32[12,8,256]{2,1,0:T(8,128)} %volume_ref.1) | copy-start | bytes 294916
  15.6 0.9 %copy-start.1 = (bf16[1024,128]{1,0:T(8,128)(2,1)S(1)}, bf16[1024,128]{1,0:T(8,128)(2,1)}, u32[]{:S(2)}) copy-start(bf16[1024,128]{1,0:T(8,128)(2,1)} %constant.138.clone.fold_ref) | copy-start | bytes 786436
  16.5 40.4 %copy-start.4 = (bf16[16,14,3,1]{0,2,3,1:T(4,128)(2,1)S(1)}, bf16[16,14,3,1]{0,2,3,1:T(4,128)(2,1)}, u32[]{:S(2)}) copy-start(bf16[16,14,3,1]{0,2,3,1:T(4,128)(2,1)} %constant.146) | copy-start | bytes 4036
  16.5 40.9 %copy-start.3 = (bf16[9,64,64]{2,1,0:T(8,128)(2,1)S(1)}, bf16[9,64,64]{2,1,0:T(8,128)(2,1)}, u32[]{:S(2)}) copy-start(bf16[9,64,64]{2,1,0:T(8,128)(2,1)} %param.33) | copy-start | bytes 221188
  16.5 44.9 %copy-start.6 = (f32[64]{0:T(128)S(1)}, f32[64]{0:T(128)}, u32[]{:S(2)}) copy-start(f32[64]{0:T(128)} %param.34) | copy-start | bytes 772
  31.5 2.0 %collective-permute-start.2 = (bf16[128,128]{1,0:T(8,128)(2,1)S(1)}, bf16[128,128]{1,0:T(8,128)(2,1)S(1)}, u32[]{:S(2)}, u32[]{:S(2)}) collective-permute-start(bf16[128,128]{1,0:T(8,128)(2,1)S(1)} %convert_element_type.121), channel_id=1, source_target_pairs={{0,1},{1,0},{2,3},{3,2},{4,5},{5,4},{6,7},{7,6},{8,9},{9,8},{10,11... | collective-permute-start | bytes 98312 | tf_op jit(solution)/shard_map/ppermute | solution.py:272
  33.5 4.0 %collective-permute-start.3 = (bf16[128,128]{1,0:T(8,128)(2,1)S(1)}, bf16[128,128]{1,0:T(8,128)(2,1)S(1)}, u32[]{:S(2)}, u32[]{:S(2)}) collective-permute-start(bf16[128,128]{1,0:T(8,128)(2,1)S(1)} %fusion.11), channel_id=1, source_target_pairs={{0,2},{1,3},{2,0},{3,1},{4,6},{5,7},{6,4},{7,5},{8,10},{9,11},{10,... | collective-permute-start | bytes 98312 | tf_op jit(solution)/shard_map/ppermute | solution.py:272
  37.5 4.9 %collective-permute-start.4 = (bf16[128,128]{1,0:T(8,128)(2,1)S(1)}, bf16[128,128]{1,0:T(8,128)(2,1)S(1)}, u32[]{:S(2)}, u32[]{:S(2)}) collective-permute-start(bf16[128,128]{1,0:T(8,128)(2,1)S(1)} %fusion.12), channel_id=1, source_target_pairs={{0,4},{1,5},{2,6},{3,7},{4,0},{5,1},{6,2},{7,3},{8,12},{9,13},{10,... | collective-permute-start | bytes 98312 | tf_op jit(solution)/shard_map/ppermute | solution.py:272
  39.2 5.4 %collective-permute-start.5 = (bf16[128,128]{1,0:T(8,128)(2,1)S(1)}, bf16[128,128]{1,0:T(8,128)(2,1)S(1)}, u32[]{:S(2)}, u32[]{:S(2)}) collective-permute-start(bf16[128,128]{1,0:T(8,128)(2,1)S(1)} %fusion.12), channel_id=1, source_target_pairs={{0,8},{1,9},{2,10},{3,11},{4,12},{5,13},{6,14},{7,15},{8,0},{9,1},... | collective-permute-start | bytes 98312 | tf_op jit(solution)/shard_map/ppermute | solution.py:272
  41.4 5.1 %collective-permute-start.6 = (bf16[128,128]{1,0:T(8,128)(2,1)S(1)}, bf16[128,128]{1,0:T(8,128)(2,1)S(1)}, u32[]{:S(2)}, u32[]{:S(2)}) collective-permute-start(bf16[128,128]{1,0:T(8,128)(2,1)S(1)} %fusion.12), channel_id=1, source_target_pairs={{0,12},{1,13},{2,14},{3,15},{4,8},{5,9},{6,10},{7,11},{8,4},{9,5},... | collective-permute-start | bytes 98312 | tf_op jit(solution)/shard_map/ppermute | solution.py:272
  50.0 8.5 %collective-permute-start.7 = (bf16[8,3,256]{2,1,0:T(4,128)(2,1)S(1)}, bf16[8,3,256]{2,1,0:T(4,128)(2,1)S(1)}, u32[]{:S(2)}, u32[]{:S(2)}) collective-permute-start(bf16[8,3,256]{2,1,0:T(4,128)(2,1)S(1)} %get-tuple-element.15), channel_id=1, source_target_pairs={{0,16},{16,0},{32,48},{48,32},{64,80},{80,64},{96,112},{112,96},{1... | collective-permute-start | bytes 36872 | tf_op jit(solution)/shard_map/ppermute | solution.py:266
  52.0 9.2 %collective-permute-start.8 = (bf16[8,3,256]{2,1,0:T(4,128)(2,1)S(1)}, bf16[8,3,256]{2,1,0:T(4,128)(2,1)S(1)}, u32[]{:S(2)}, u32[]{:S(2)}) collective-permute-start(bf16[8,3,256]{2,1,0:T(4,128)(2,1)S(1)} %get-tuple-element.14), channel_id=1, source_target_pairs={{16,32},{48,64},{80,96},{32,16},{64,48},{96,80},{17,33},{49,65},{8... | collective-permute-start | bytes 36872 | tf_op jit(solution)/shard_map/ppermute | solution.py:265

commit v2 on v1

v2 whole, which is shorter than its diff:
```python
import jax
import jax.numpy as jnp
from jax import lax
from jax.experimental import pallas as pl
from jax.experimental.pallas import tpu as pltpu
from jax.sharding import PartitionSpec as P

SUBSETS = 4
SIGMA_STEP = 0.002
RELAX_TOP = 4.0
HALO = 3
PLANES = 4
BF = jnp.bfloat16
F32 = jnp.float32
AXIAL = (8, 8, 11, 14, 16)
CORONAL = (12, 16, 19, 22, 24)


def noise_scales(timestep_ref):
    sigma = jnp.full((1, 256), timestep_ref[0], jnp.int32).astype(F32) * SIGMA_STEP
    scale_in = 1.0 / jnp.sqrt(1.0 + sigma * sigma)
    return (scale_in, sigma * scale_in)


def relaxation(subset_ref):
    epoch = jnp.full((1, 256), subset_ref[0] // SUBSETS, jnp.int32).astype(F32)
    return RELAX_TOP / (1.0 + epoch / 64.0)


def iota(shape, dim):
    return lax.broadcasted_iota(jnp.int32, shape, dim)


def last_rows(own):
    return -(-3 * (-(-own // 8) * 8) // 16) * 16


def build_weights(layout, index, count, first_taps, first_bias, middle_bias, last_taps, middle_taps_ref, outs):
    own, first, second, ones, slots = layout
    one_ref, middle_ref, bias_ref, last_ref = outs
    rows_one, rows_two = own + 4, own + 2
    total = count * own
    odd = index % 2 == 1
    before = jnp.where(odd, first, second)
    after = jnp.where(odd, second, first)

    def keep(row):
        place = index * own + row
        return jnp.where((place >= 0) & (place < total), 1.0, 0.0).astype(F32)

    def slot(row):
        if row < HALO:
            return before + row
        if row < own + HALO:
            return row - HALO
        return after + row - own - HALO

    rows = jnp.concatenate([first_taps, first_bias, middle_bias, jnp.zeros((5, 64), F32)], axis=0)
    high = rows.astype(BF)
    rest = rows - high.astype(F32)
    middle = rest.astype(BF)
    low = (rest - middle.astype(F32)).astype(BF)
    stack = jnp.concatenate([high, middle, low], axis=0)
    picks = jnp.where(iota((48, 11 * 128), 0) % 16 == iota((48, 11 * 128), 1) // 128, 1.0, 0.0)
    spread = lax.dot_general(
        stack, picks.astype(BF), (((0,), (0,)), ((), ())), preferred_element_type=F32
    )
    columns = [spread[:, k * 128 : (k + 1) * 128] for k in range(11)]
    bias_ref[:, 0:128] = columns[10]
    bias_ref[:, 128:256] = columns[10]
    bias_high = columns[9].astype(BF).astype(F32)
    bias_low = columns[9] - bias_high
    lane = iota((64, 128), 1)
    for row in range(rows_one):
        block = jnp.where(lane == slots + ones, bias_high, 0.0)
        block = jnp.where(lane == slots + ones + 1, bias_low, block)
        for a in range(3):
            for b in range(3):
                block = jnp.where(lane == b * slots + slot(row + a), columns[3 * a + b], block)
        one_ref[row * 64 : (row + 1) * 64, :] = (block * keep(row - 2)).astype(BF)
    padded = last_rows(own)
    band = -(-own // 8) * 8
    sublane = iota((padded, 64), 0)
    for row in range(rows_two):
        block = jnp.zeros((padded, 64), F32)
        for a in range(3):
            if 0 <= row - a < own:
                for b in range(3):
                    tap = last_taps[3 * a + b : 3 * a + b + 1, :]
                    block = jnp.where(sublane == b * band + row - a, tap, block)
        last_ref[:, row * 64 : (row + 1) * 64] = (block * keep(row - 1)).astype(BF)
    middle_ref[...] = jnp.zeros_like(middle_ref)
    for out in range(2):
        for a in range(3):
            for b in range(3):
                column = (out + a) * 192 + b * 64
                middle_ref[out * 64 : (out + 1) * 64, column : column + 64] = middle_taps_ref[3 * a + b]


def build_from(layout, index, count, raw, outs):
    first_taps, first_bias, middle_bias, last_taps, middle_taps_ref = raw
    build_weights(
        layout,
        index,
        count,
        first_taps[...].astype(F32),
        first_bias[...],
        middle_bias[...],
        last_taps[...].astype(F32),
        middle_taps_ref,
        outs,
    )


def prepare_kernel(*refs):
    raw, measured_ref, outs, turned_ref = refs[0:5], refs[5], refs[6:10], refs[10]
    build_from(CORONAL, lax.axis_index("gz"), 8, raw, outs)
    turned_ref[...] = jnp.zeros_like(turned_ref)
    for part in range(8):
        turned_ref[part * 16 : part * 16 + 12, :] = measured_ref[:, part * 128 : (part + 1) * 128]


def weight_shapes(own):
    return [
        (((own + 4) * 64, 128), BF),
        ((128, 768), BF),
        ((64, 256), F32),
        ((last_rows(own), (own + 2) * 64), BF),
    ]


def shifted(block):
    lane = lax.broadcasted_iota(jnp.int32, block.shape, 1)
    zero = jnp.zeros((), block.dtype)
    across = block.shape[1]
    left = jnp.where(lane == 0, zero, pltpu.roll(block, 1, 1))
    right = jnp.where(lane == across - 1, zero, pltpu.roll(block, across - 1, 1))
    return left, right


def spread_entry(own, first, second):
    rows = [own, first, second, jnp.ones((2, own.shape[1]), F32)]
    entry = jnp.concatenate(rows, axis=0)
    left, right = shifted(entry)
    return jnp.concatenate([left, entry, right], axis=0).astype(BF)


def layer_one(spread, rows_one, one_ref, taps_ref):
    depth = spread.shape[0]
    for row in range(rows_one):
        hidden = jnp.dot(
            one_ref[row * 64 : (row + 1) * 64, 0:depth], spread, preferred_element_type=F32
        )
        hidden = jnp.maximum(hidden, 0.0).astype(BF)
        left, right = shifted(hidden)
        taps_ref[row * 192 : row * 192 + 64, :] = left
        taps_ref[row * 192 + 64 : row * 192 + 128, :] = hidden
        taps_ref[row * 192 + 128 : row * 192 + 192, :] = right


def layer_two(rows_two, middle_ref, bias_ref, taps_ref, hidden_ref):
    bias = bias_ref[...]
    for row in range(0, rows_two, 2):
        summed = jnp.dot(
            middle_ref[...], taps_ref[row * 192 : (row + 4) * 192, :], preferred_element_type=F32
        )
        for k in range(2):
            value = jnp.maximum(summed[k * 64 : (k + 1) * 64] + bias, 0.0)
            hidden_ref[(row + k) * 64 : (row + k + 1) * 64, :] = value.astype(BF)


def layer_three(rows, last_ref, hidden_ref):
    last = jnp.dot(last_ref[...], hidden_ref[...], preferred_element_type=F32)
    left, _ = shifted(last[0:rows])
    _, right = shifted(last[2 * rows : 3 * rows])
    return left + last[rows : 2 * rows] + right


def networks(entries, own, weights, scratch):
    one_ref, middle_ref, bias_ref, last_ref = weights
    taps, hidden = scratch[0:PLANES], scratch[PLANES : 2 * PLANES]
    for k in range(PLANES):
        layer_one(spread_entry(*entries[k]), own + 4, one_ref, taps[k])
    for k in range(PLANES):
        layer_two(own + 2, middle_ref, bias_ref, taps[k], hidden[k])
    return [layer_three(-(-own // 8) * 8, last_ref, hidden[k]) for k in range(PLANES)]


def network_scratch(own):
    return [pltpu.VMEM(((own + 4) * 192, 256), BF)] * PLANES + [
        pltpu.VMEM(((own + 2) * 64, 256), BF)
    ] * PLANES


def axial_kernel(
    subset_ref,
    timestep_ref,
    volume_ref,
    first_ref,
    second_ref,
    taps_in_ref,
    bias_in_ref,
    bias_mid_ref,
    taps_out_ref,
    taps_mid_ref,
    projector_ref,
    axial_ref,
    partial_ref,
    sent_ref,
    chosen_ref,
    picked_ref,
    sem,
    *scratch,
):
    copy = pltpu.make_async_copy(projector_ref.at[subset_ref[0] % SUBSETS], chosen_ref, sem)
    copy.start()
    weights, scratch = scratch[0:4], scratch[4:]
    raw = (taps_in_ref, bias_in_ref, bias_mid_ref, taps_out_ref, taps_mid_ref)
    build_from(AXIAL, lax.axis_index("gy"), 16, raw, weights)
    axial_ref[...] = jnp.zeros_like(axial_ref)
    scale_in, scale_out = noise_scales(timestep_ref)

    def planes(step, carry):
        entries = []
        for k in range(PLANES):
            p = step * PLANES + k
            entries.append((volume_ref[p] * scale_in, first_ref[p] * scale_in, second_ref[p] * scale_in))
        nets = networks(entries, 8, weights, scratch)
        for k in range(PLANES):
            p = step * PLANES + k
            value = volume_ref[p] + scale_out * nets[k]
            for y in range(8):
                axial_ref[y, pl.ds(p, 1), :] = value[y : y + 1, :]
        return carry

    lax.fori_loop(0, 12 // PLANES, planes, 0)
    copy.wait()
    flat = axial_ref[...].reshape(128, 256).astype(BF)
    lane = lax.broadcasted_iota(jnp.int32, (16, 256), 1) % 8
    for part in range(32):
        product = lax.dot_general(
            flat,
            chosen_ref[part * 256 : (part + 1) * 256, :],
            (((1,), (1,)), ((), ())),
            preferred_element_type=F32,
        )
        picked = product[0:16]
        for y in range(1, 8):
            picked = jnp.where(lane == y, product[y * 16 : (y + 1) * 16], picked)
        row, column = (part // 4) * 16, (part % 4) * 256
        picked_ref[row : row + 16, column : column + 256] = picked
    picked = picked_ref[...]
    high = picked.astype(BF)
    low = (picked - high.astype(F32)).astype(BF)
    fold = jnp.where(iota((1024, 128), 0) // 8 == iota((1024, 128), 1), 1.0, 0.0).astype(BF)
    partial = jnp.dot(high, fold, preferred_element_type=F32) + jnp.dot(
        low, fold, preferred_element_type=F32
    )
    partial_ref[...] = partial
    sent_ref[...] = partial.astype(BF)


def back_kernel(
    subset_ref,
    measured_ref,
    sinogram_ref,
    axial_ref,
    projector_ref,
    corrected_ref,
    residual_ref,
    chosen_ref,
    held_ref,
    sems,
):
    copies = []
    for part in range(8):
        rows = pl.ds(part * 1024, 1024)
        copies.append(
            pltpu.make_async_copy(
                projector_ref.at[subset_ref[0] % SUBSETS, rows], chosen_ref.at[rows], sems.at[part]
            )
        )
        copies[-1].start()
    residual = measured_ref[...] - sinogram_ref[...]
    held_ref[...] = residual
    unfold = jnp.where(iota((128, 1024), 1) // 8 == iota((128, 1024), 0), 1.0, 0.0).astype(BF)
    wide = jnp.dot(residual.astype(BF), unfold, preferred_element_type=F32).astype(BF)
    lane = lax.broadcasted_iota(jnp.int32, (16, 1024), 1) % 8
    zero = jnp.zeros((), BF)
    total = jnp.zeros((128, 256), F32)
    for part in range(8):
        rays = wide[part * 16 : (part + 1) * 16]
        spread = jnp.concatenate([jnp.where(lane == y, rays, zero) for y in range(8)], axis=0)
        copies[part].wait()
        total = total + jnp.dot(
            spread, chosen_ref[part * 1024 : (part + 1) * 1024, :], preferred_element_type=F32
        )
    corrected_ref[...] = axial_ref[...] + (relaxation(subset_ref) * total).reshape(8, 16, 256)
    index = lax.axis_index("gy")
    block = held_ref[pl.ds(pl.multiple_of((index // 2) * 16, 16), 16), :]
    residual_ref[...] = jnp.where(index % 2 == 1, block[0:12, 64:128], block[0:12, 0:64])


def coronal_kernel(
    timestep_ref,
    corrected_ref,
    first_ref,
    second_ref,
    one_ref,
    middle_ref,
    bias_ref,
    last_ref,
    restored_ref,
    *scratch,
):
    scale_in, scale_out = noise_scales(timestep_ref)
    weights = (one_ref, middle_ref, bias_ref, last_ref)

    def planes(step, carry):
        entries = []
        for k in range(PLANES):
            p = step * PLANES + k
            entries.append((corrected_ref[p] * scale_in, first_ref[p] * scale_in, second_ref[p] * scale_in))
        nets = networks(entries, 12, weights, scratch)
        for k in range(PLANES):
            p = step * PLANES + k
            value = corrected_ref[p] + scale_out * nets[k]
            for z in range(12):
                restored_ref[z, pl.ds(p, 1), :] = value[z : z + 1, :]
        return carry

    lax.fori_loop(0, 8 // PLANES, planes, 0)


def vmem():
    return pl.BlockSpec(memory_space=pltpu.VMEM)


def hbm():
    return pl.BlockSpec(memory_space=pltpu.HBM)


def smem():
    return pl.BlockSpec(memory_space=pltpu.SMEM)


def params(limit):
    return pltpu.CompilerParams(vmem_limit_bytes=limit << 20)


def inner_pairs(size):
    return [(i, i ^ 1) for i in range(size)]


def outer_pairs(size):
    ups = [(i, i + 1) for i in range(1, size - 1, 2)]
    return ups + [(j, i) for i, j in ups]


def exchange(leading, trailing, axis, ordered):
    size = lax.axis_size(axis)
    odd = lax.axis_index(axis) % 2 == 1
    inner = jnp.where(odd, leading, trailing)
    outer = jnp.where(odd, trailing, leading)
    first = lax.ppermute(inner, axis, inner_pairs(size))
    if ordered:
        first, outer = lax.optimization_barrier((first, outer))
    second = lax.ppermute(outer, axis, outer_pairs(size))
    return first, second


def sum_over_gy(partial, sent, axial):
    def partner(value, bits):
        return lax.ppermute(value, "gy", [(i, i ^ bits) for i in range(16)]).astype(F32)

    total = partial + partner(sent, 1)
    total = total + partner(total.astype(BF), 2)
    sent, axial = lax.optimization_barrier((total.astype(BF), axial))
    total = total + partner(sent, 4)
    return total + partner(total.astype(BF), 8), axial


def per_device(
    volume,
    projector,
    measured,
    subset,
    timestep,
    axial_in,
    axial_bias_in,
    axial_mid,
    axial_bias_mid,
    axial_out,
    coronal_in,
    coronal_bias_in,
    coronal_mid,
    coronal_bias_mid,
    coronal_out,
):
    first, second = exchange(volume[:, :HALO], volume[:, -HALO:], "gy", False)
    prepared = pl.pallas_call(
        prepare_kernel,
        name="prepare",
        out_shape=tuple(jax.ShapeDtypeStruct(*shape) for shape in weight_shapes(12))
        + (jax.ShapeDtypeStruct((128, 128), F32),),
        in_specs=[vmem()] * 6,
        out_specs=(vmem(),) * 5,
        compiler_params=params(48),
        cost_estimate=pl.CostEstimate(flops=1000000, bytes_accessed=3000000, transcendentals=0),
    )(
        coronal_in[:, :, 0],
        coronal_bias_in[None],
        coronal_bias_mid[None],
        coronal_out[:, 0, :],
        coronal_mid,
        measured.T,
    )
    coronal_weights, turned = prepared[0:4], prepared[4]
    flat_projector = projector.reshape(4, 8192, 256)
    axial, partial, sent = pl.pallas_call(
        axial_kernel,
        name="axial",
        out_shape=(
            jax.ShapeDtypeStruct((8, 16, 256), F32),
            jax.ShapeDtypeStruct((128, 128), F32),
            jax.ShapeDtypeStruct((128, 128), BF),
        ),
        in_specs=[smem()] * 2 + [vmem()] * 8 + [hbm()],
        out_specs=(vmem(),) * 3,
        scratch_shapes=[
            pltpu.VMEM((8192, 256), BF),
            pltpu.VMEM((128, 1024), F32),
            pltpu.SemaphoreType.DMA,
        ]
        + [pltpu.VMEM(*shape) for shape in weight_shapes(8)]
        + network_scratch(8),
        compiler_params=params(60),
    )(
        subset,
        timestep,
        volume,
        first,
        second,
        axial_in[:, :, 0],
        axial_bias_in[None],
        axial_bias_mid[None],
        axial_out[:, 0, :],
        axial_mid,
        flat_projector,
    )
    zero = timestep[0].astype(F32) * 0.0
    partial = lax.optimization_barrier(partial + zero)
    sinogram, axial = sum_over_gy(partial, sent, axial)
    axial = lax.optimization_barrier(axial + zero)
    corrected, residual = pl.pallas_call(
        back_kernel,
        name="back",
        out_shape=(
            jax.ShapeDtypeStruct((8, 16, 256), F32),
            jax.ShapeDtypeStruct((12, 64), F32),
        ),
        in_specs=[smem()] + [vmem()] * 3 + [hbm()],
        out_specs=(vmem(), vmem()),
        scratch_shapes=[
            pltpu.VMEM((8192, 256), BF),
            pltpu.VMEM((128, 128), F32),
            pltpu.SemaphoreType.DMA((8,)),
        ],
        compiler_params=params(48),
    )(subset, turned, sinogram, axial, flat_projector)
    first, second = exchange(corrected[:, :HALO], corrected[:, 12 - HALO : 12], "gz", False)
    restored = pl.pallas_call(
        coronal_kernel,
        name="coronal",
        out_shape=jax.ShapeDtypeStruct((12, 8, 256), F32),
        in_specs=[smem()] + [vmem()] * 7,
        out_specs=vmem(),
        scratch_shapes=network_scratch(12),
        compiler_params=params(48),
    )(timestep, corrected, first, second, *coronal_weights)
    return (restored, residual.T)


def solution(mesh):
    in_specs = (
        P("gz", "gy", None),
        P(None, None, "gy", None),
        P(None, "gz"),
    ) + (P(),) * 12
    out_specs = (P("gz", "gy", None), P("gy", "gz"))
    return jax.shard_map(
        per_device, mesh=mesh, in_specs=in_specs, out_specs=out_specs, check_vma=False
    )
```

time: 73.2 us -> 53.9 us (0.74); the launches traced: 72.2 us -> 53.6 us
  Pallas kernels: 29 us -> 19.7 us
  local copies, waits for them, and re-layouts: 7.23 us -> 0.67 us
  matrix products: 3.33 us -> 0 us
  starting transfers between devices: 16 us -> 17 us
    pallas_call x1, Pallas kernels: 15 us -> 9.88 us  [per_device(): pl.pallas_call(axial_kernel, name='axial', out_shape=(jax.ShapeDtypeStruc...]
    pallas_call x1, Pallas kernels: 10.7 us -> 5.91 us  [per_device(): pl.pallas_call(coronal_kernel, name='coronal', out_shape=jax.ShapeDtypeSt...]
    dot_general x4 -> x0, matrix products: 3.33 us -> none  [the longest x2 2.17 us: layer_weights(): one = jnp.einsum('ko,ikq->ioq', stack, chosen, preferred_element_type=F32)]
    unnamed x16, local copies, waits for them, and re-layouts: 3.4 us -> 0.67 us
    reshape x10 -> x0, local copies, waits for them, and re-layouts: 2.52 us -> none  [the longest x4 1.5 us: layer_weights(): middle_taps.reshape(3, 3, 64, 64).transpose(0, 2, 1, 3).reshape(192, 192)]
    add x1 -> x3, other arithmetic: 0.03 us -> 1.78 us  [the longest x1 0.91 us: per_device(): axial = lax.optimization_barrier(axial + zero)]
    broadcast_in_dim x2 -> x0, other arithmetic: 1.47 us -> none  [layer_weights(): high[None]]
    ppermute x5 -> x4, waiting for transfers between devices: 8.66 us -> 7.2 us  [partner(): lax.ppermute(value, 'gy', [(i, i ^ bits) for i in range(16)]).astype(F32)]
  transfers between devices with their start and end apart: 9 -> 8, of which waited for: 5 -> 7; matrix products, arithmetic and copies ran while one was open for 13% -> 3% of each run, Pallas kernels for 0% -> 1%
where the time goes in v2:
time: 53.9 us; the launch traced here: 53.6 us
  Pallas kernels  19.7 us (37%)
  starting transfers between devices  17 us (32%)
  waiting for transfers between devices  11.3 us (21%)
  other arithmetic  2.89 us (5%)
  between operations  2.1 us (4%)
  local copies, waits for them, and re-layouts  0.67 us (1%)
    pallas_call x1, Pallas kernels, per_device(): pl.pallas_call(axial_kernel, name='axial', out_shape=(jax.ShapeDtypeStruc...  9.88 us
    ppermute x2, starting transfers between devices, exchange(): second = lax.ppermute(outer, axis, outer_pairs(size))  8.97 us
    ppermute x4, waiting for transfers between devices, partner(): lax.ppermute(value, 'gy', [(i, i ^ bits) for i in range(16)]).astype(F32)  7.2 us
    ppermute x4, starting transfers between devices, partner(): lax.ppermute(value, 'gy', [(i, i ^ bits) for i in range(16)]).astype(F32)  6.16 us
    pallas_call x1, Pallas kernels, per_device(): pl.pallas_call(coronal_kernel, name='coronal', out_shape=jax.ShapeDtypeSt...  5.91 us
    pallas_call x1, Pallas kernels, per_device(): pl.pallas_call(back_kernel, name='back', out_shape=(jax.ShapeDtypeStruct(...  3.3 us
    ppermute x2, waiting for transfers between devices, exchange(): second = lax.ppermute(outer, axis, outer_pairs(size))  2.68 us
    ppermute x2, starting transfers between devices, exchange(): first = lax.ppermute(inner, axis, inner_pairs(size))  1.85 us
  transfers between devices with their start and end apart: 8, of which 7 were waited for; matrix products, arithmetic and copies ran while one was open for 3% of the time, Pallas kernels for 1%

profile of v2, /device:TPU:6, one launch (start us, length us, event | category | flops | bytes accessed | tf_op | source)
XLA Modules:
  0.0 53.6 jit_solution(16572464175432594419)
XLA Ops:
  0.7 1.1 %slice_select_fusion = (f32[12,3,256]{2,1,0:T(4,128)S(1)}, f32[12,3,256]{2,1,0:T(4,128)S(1)}) fusion(f32[12,8,256]{2,1,0:T(8,128)} %volume_ref.1, pred[]{:T(512)S(6)} %eq.9), kind=kLoop, calls=%fused_computation.7 | loop fusion | flops 18432 | bytes 147457 | tf_op jit(solution)/shard_map/jit(_where)/select_n | solution.py:364
  1.8 2.2 %collective-permute-start.1 = (f32[12,3,256]{2,1,0:T(4,128)S(1)}, f32[12,3,256]{2,1,0:T(4,128)S(1)}, u32[]{:S(2)}, u32[]{:S(2)}) collective-permute-start(f32[12,3,256]{2,1,0:T(4,128)S(1)} %get-tuple-element.28), channel_id=1, source_target_pairs={{1,2},{3,4},{5,6},{7,8},{9,10},{11,12},{13,14},{2,1},{4,3},{6,5},{... | collective-permute-start | bytes 110600 | tf_op jit(solution)/shard_map/ppermute | solution.py:368
  3.9 1.8 %collective-permute-start = (f32[12,3,256]{2,1,0:T(4,128)S(1)}, f32[12,3,256]{2,1,0:T(4,128)S(1)}, u32[]{:S(2)}, u32[]{:S(2)}) collective-permute-start(f32[12,3,256]{2,1,0:T(4,128)S(1)} %get-tuple-element.29), channel_id=1, source_target_pairs={{0,1},{1,0},{2,3},{3,2},{4,5},{5,4},{6,7},{7,6},{8,9},{9,8},{10,11... | collective-permute-start | bytes 110600 | tf_op jit(solution)/shard_map/ppermute | solution.py:365
  7.0 0.2 collective-permute-done.1.second_ref
  7.2 0.6 %copy-done.6 = f32[12,3,256]{2,1,0:T(4,128)} copy-done((f32[12,3,256]{2,1,0:T(4,128)}, f32[12,3,256]{2,1,0:T(4,128)S(1)}, u32[]{:S(2)}) %copy-start.6) | copy-done | bytes 36888
  7.8 0.0 copy-done.7
  7.8 9.9 %axial.1 = (f32[8,16,256]{2,1,0:T(8,128)}, f32[128,128]{1,0:T(8,128)}, bf16[128,128]{1,0:T(8,128)(2,1)}) custom-call(s32[1]{0:T(128)S(6)} %copy.17.subset_ref, s32[1]{0:T(128)S(6)} %copy.18.timestep_ref, f32[12,8,256]{2,1,0:T(8,128)} %volume_ref.1, f32[12,3,256]{2,1,0:T(4,128)} %copy-done.7, f32[12,3,256]{2,1,0:T(4,128)} %copy-done.6, ...), custom_call_target="tpu_custom_call" | custom-call | tf_op jit(solution)/shard_map/axial/pallas_call | solution.py:420
  17.7 1.2 %collective-permute-start.2 = (bf16[128,128]{1,0:T(8,128)(2,1)}, bf16[128,128]{1,0:T(8,128)(2,1)S(1)}, u32[]{:S(2)}, u32[]{:S(2)}) collective-permute-start(bf16[128,128]{1,0:T(8,128)(2,1)} %get-tuple-element.16), channel_id=1, source_target_pairs={{0,1},{1,0},{2,3},{3,2},{4,5},{5,4},{6,7},{7,6},{8,9},{9,8},{10,11... | collective-permute-start | bytes 98312 | tf_op jit(solution)/shard_map/ppermute | solution.py:374
  18.9 0.8 %broadcast_add_fusion.1 = f32[128,128]{1,0:T(8,128)S(1)} fusion(f32[128,128]{1,0:T(8,128)} %get-tuple-element.15, f32[]{:T(128)} %bitcast.10), kind=kLoop, calls=%fused_computation.9 | loop fusion | flops 16384 | bytes 131076 | tf_op jit(solution)/shard_map/add | solution.py:452
  19.8 0.2 collective-permute-done.2
  20.0 0.1 collective-permute-start.3
  20.1 3.9 %collective-permute-done.3 = bf16[128,128]{1,0:T(8,128)(2,1)S(1)} collective-permute-done((bf16[128,128]{1,0:T(8,128)(2,1)S(1)}, bf16[128,128]{1,0:T(8,128)(2,1)S(1)}, u32[]{:S(2)}, u32[]{:S(2)}) %collective-permute-start.3) | collective-permute-done | bytes 32800 | tf_op jit(solution)/shard_map/ppermute | solution.py:374
  24.0 1.7 %collective-permute-start.4 = (bf16[128,128]{1,0:T(8,128)(2,1)S(1)}, bf16[128,128]{1,0:T(8,128)(2,1)S(1)}, u32[]{:S(2)}, u32[]{:S(2)}) collective-permute-start(bf16[128,128]{1,0:T(8,128)(2,1)S(1)} %fusion.2), channel_id=1, source_target_pairs={{0,4},{1,5},{2,6},{3,7},{4,0},{5,1},{6,2},{7,3},{8,12},{9,13},{10,... | collective-permute-start | bytes 98312 | tf_op jit(solution)/shard_map/ppermute | solution.py:374
  25.7 0.6 %prepare.1 = (bf16[1024,128]{1,0:T(8,128)(2,1)S(1)}, bf16[128,768]{1,0:T(8,128)(2,1)S(1)}, f32[64,256]{1,0:T(8,128)S(1)}, bf16[48,896]{1,0:T(8,128)(2,1)S(1)}, f32[128,128]{1,0:T(8,128)S(1)}) custom-call(bf16[9,64]{1,0:T(8,128)(2,1)S(1)} %bitcast.13, f32[1,64]{1,0:T(1,128)S(1)} %bitcast.15, f32[1,64]{1,0:T(1,128)S(1)} %bitcast.16, ...), custom_call_target="tpu_custom_call" | custom-call | flops 1000000 | bytes 3000000 | tf_op jit(solution)/shard_map/prepare/pallas_call | solution.py:401
  26.3 1.7 %collective-permute-done.4 = bf16[128,128]{1,0:T(8,128)(2,1)S(1)} collective-permute-done((bf16[128,128]{1,0:T(8,128)(2,1)S(1)}, bf16[128,128]{1,0:T(8,128)(2,1)S(1)}, u32[]{:S(2)}, u32[]{:S(2)}) %collective-permute-start.4) | collective-permute-done | bytes 32800 | tf_op jit(solution)/shard_map/ppermute | solution.py:374
  28.1 3.2 %collective-permute-start.5 = (bf16[128,128]{1,0:T(8,128)(2,1)S(1)}, bf16[128,128]{1,0:T(8,128)(2,1)S(1)}, u32[]{:S(2)}, u32[]{:S(2)}) collective-permute-start(bf16[128,128]{1,0:T(8,128)(2,1)S(1)} %fusion.1), channel_id=1, source_target_pairs={{0,8},{1,9},{2,10},{3,11},{4,12},{5,13},{6,14},{7,15},{8,0},{9,1},... | collective-permute-start | bytes 98312 | tf_op jit(solution)/shard_map/ppermute | solution.py:374
  31.2 0.9 %broadcast_add_fusion.axial_ref = f32[8,16,256]{2,1,0:T(8,128)S(1)} fusion(f32[8,16,256]{2,1,0:T(8,128)} %get-tuple-element.19, f32[]{:T(128)} %bitcast.10), kind=kLoop, calls=%fused_computation | loop fusion | flops 32768 | bytes 262148 | tf_op jit(solution)/shard_map/add | solution.py:454
  32.2 1.4 %collective-permute-done.5 = bf16[128,128]{1,0:T(8,128)(2,1)S(1)} collective-permute-done((bf16[128,128]{1,0:T(8,128)(2,1)S(1)}, bf16[128,128]{1,0:T(8,128)(2,1)S(1)}, u32[]{:S(2)}, u32[]{:S(2)}) %collective-permute-start.5) | collective-permute-done | bytes 32800 | tf_op jit(solution)/shard_map/ppermute | solution.py:374
  33.6 3.3 %back.1 = (f32[8,16,256]{2,1,0:T(8,128)S(1)}, f32[12,64]{1,0:T(8,128)}) custom-call(s32[1]{0:T(128)S(6)} %copy.17.subset_ref, f32[128,128]{1,0:T(8,128)S(1)} %get-tuple-element.14.measured_ref, f32[128,128]{1,0:T(8,128)S(1)} %convert_add_fusion.sinogram_ref, f32[8,16,256]{2,1,0:T(8,128)S(1)} %broadcast_add_fusion.axial_ref, bf16[4,8192,256]{2,1,0:T(8,128)(2,1)} %bitcast.18), custom_call_target="tpu_custom_call" | custom-call | tf_op jit(solution)/shard_map/back/pallas_call | solution.py:455
  36.9 6.8 %collective-permute-start.7 = (f32[8,3,256]{2,1,0:T(4,128)S(1)}, f32[8,3,256]{2,1,0:T(4,128)S(1)}, u32[]{:S(2)}, u32[]{:S(2)}) collective-permute-start(f32[8,3,256]{2,1,0:T(4,128)S(1)} %get-tuple-element.26), channel_id=1, source_target_pairs={{16,32},{48,64},{80,96},{32,16},{64,48},{96,80},{17,33},{49,65},{8... | collective-permute-start | bytes 73736 | tf_op jit(solution)/shard_map/ppermute | solution.py:368
  43.7 0.1 collective-permute-start.6
  43.8 2.5 %collective-permute-done.7.second_ref = f32[8,3,256]{2,1,0:T(4,128)S(1)} collective-permute-done((f32[8,3,256]{2,1,0:T(4,128)S(1)}, f32[8,3,256]{2,1,0:T(4,128)S(1)}, u32[]{:S(2)}, u32[]{:S(2)}) %collective-permute-start.7) | collective-permute-done | bytes 24608 | tf_op jit(solution)/shard_map/ppermute | solution.py:368
  46.3 1.4 %collective-permute-done.6.first_ref = f32[8,3,256]{2,1,0:T(4,128)S(1)} collective-permute-done((f32[8,3,256]{2,1,0:T(4,128)S(1)}, f32[8,3,256]{2,1,0:T(4,128)S(1)}, u32[]{:S(2)}, u32[]{:S(2)}) %collective-permute-start.6) | collective-permute-done | bytes 24608 | tf_op jit(solution)/shard_map/ppermute | solution.py:365
  47.7 5.9 %coronal.1 = f32[12,8,256]{2,1,0:T(8,128)} custom-call(s32[1]{0:T(128)S(6)} %copy.18.timestep_ref, f32[8,16,256]{2,1,0:T(8,128)S(1)} %get-tuple-element.20.corrected_ref, f32[8,3,256]{2,1,0:T(4,128)S(1)} %collective-permute-done.6.first_ref, f32[8,3,256]{2,1,0:T(4,128)S(1)} %collective-permute-done.7.second_ref, ...), custom_call_target="tpu_custom_call" | custom-call | tf_op jit(solution)/shard_map/coronal/pallas_call | solution.py:472
  (20 shorter events, 0.1 us)
Async XLA Ops:
  0.6 25.1 %copy-start.3 = (bf16[9,1,64]{2,0,1:T(8,128)(2,1)S(1)}, bf16[9,1,64]{2,0,1:T(8,128)(2,1)}, u32[]{:S(2)}) copy-start(bf16[9,1,64]{2,0,1:T(8,128)(2,1)} %param.29) | copy-start | bytes 3460
  0.6 25.1 %copy-start.5 = (f32[64]{0:T(128)S(1)}, f32[64]{0:T(128)}, u32[]{:S(2)}) copy-start(f32[64]{0:T(128)} %param.28) | copy-start | bytes 772
  0.7 25.0 %copy-start = (bf16[9,64,64]{2,1,0:T(8,128)(2,1)S(1)}, bf16[9,64,64]{2,1,0:T(8,128)(2,1)}, u32[]{:S(2)}) copy-start(bf16[9,64,64]{2,1,0:T(8,128)(2,1)} %refs_4_.1) | copy-start | bytes 221188
  0.7 25.0 %copy-start.4 = (f32[64]{0:T(128)S(1)}, f32[64]{0:T(128)}, u32[]{:S(2)}) copy-start(f32[64]{0:T(128)} %param.26) | copy-start | bytes 772
  0.7 25.0 %copy-start.2 = (bf16[9,64,1]{1,0,2:T(8,128)(2,1)S(1)}, bf16[9,64,1]{1,0,2:T(8,128)(2,1)}, u32[]{:S(2)}) copy-start(bf16[9,64,1]{1,0,2:T(8,128)(2,1)} %param.25) | copy-start | bytes 3460
  0.7 25.0 %copy-start.1 = (f32[1024,12]{0,1:T(8,128)S(1)}, f32[1024,12]{0,1:T(8,128)}, u32[]{:S(2)}) copy-start(f32[1024,12]{0,1:T(8,128)} %param.17) | copy-start | bytes 147460
  1.8 5.4 %collective-permute-start.1 = (f32[12,3,256]{2,1,0:T(4,128)S(1)}, f32[12,3,256]{2,1,0:T(4,128)S(1)}, u32[]{:S(2)}, u32[]{:S(2)}) collective-permute-start(f32[12,3,256]{2,1,0:T(4,128)S(1)} %get-tuple-element.28), channel_id=1, source_target_pairs={{1,2},{3,4},{5,6},{7,8},{9,10},{11,12},{13,14},{2,1},{4,3},{6,5},{... | collective-permute-start | bytes 110600 | tf_op jit(solution)/shard_map/ppermute | solution.py:368
  3.9 3.2 %collective-permute-start = (f32[12,3,256]{2,1,0:T(4,128)S(1)}, f32[12,3,256]{2,1,0:T(4,128)S(1)}, u32[]{:S(2)}, u32[]{:S(2)}) collective-permute-start(f32[12,3,256]{2,1,0:T(4,128)S(1)} %get-tuple-element.29), channel_id=1, source_target_pairs={{0,1},{1,0},{2,3},{3,2},{4,5},{5,4},{6,7},{7,6},{8,9},{9,8},{10,11... | collective-permute-start | bytes 110600 | tf_op jit(solution)/shard_map/ppermute | solution.py:365
  7.2 0.6 %copy-start.6 = (f32[12,3,256]{2,1,0:T(4,128)}, f32[12,3,256]{2,1,0:T(4,128)S(1)}, u32[]{:S(2)}) copy-start(f32[12,3,256]{2,1,0:T(4,128)S(1)} %collective-permute-done.1.second_ref) | copy-start | bytes 110596
  7.2 0.6 %copy-start.7 = (f32[12,3,256]{2,1,0:T(4,128)}, f32[12,3,256]{2,1,0:T(4,128)S(1)}, u32[]{:S(2)}) copy-start(f32[12,3,256]{2,1,0:T(4,128)S(1)} %collective-permute-done.first_ref) | copy-start | bytes 110596
  17.7 2.3 %collective-permute-start.2 = (bf16[128,128]{1,0:T(8,128)(2,1)}, bf16[128,128]{1,0:T(8,128)(2,1)S(1)}, u32[]{:S(2)}, u32[]{:S(2)}) collective-permute-start(bf16[128,128]{1,0:T(8,128)(2,1)} %get-tuple-element.16), channel_id=1, source_target_pairs={{0,1},{1,0},{2,3},{3,2},{4,5},{5,4},{6,7},{7,6},{8,9},{9,8},{10,11... | collective-permute-start | bytes 98312 | tf_op jit(solution)/shard_map/ppermute | solution.py:374
  20.0 4.0 %collective-permute-start.3 = (bf16[128,128]{1,0:T(8,128)(2,1)S(1)}, bf16[128,128]{1,0:T(8,128)(2,1)S(1)}, u32[]{:S(2)}, u32[]{:S(2)}) collective-permute-start(bf16[128,128]{1,0:T(8,128)(2,1)S(1)} %fusion), channel_id=1, source_target_pairs={{0,2},{1,3},{2,0},{3,1},{4,6},{5,7},{6,4},{7,5},{8,10},{9,11},{10,... | collective-permute-start | bytes 98312 | tf_op jit(solution)/shard_map/ppermute | solution.py:374
  24.0 4.0 %collective-permute-start.4 = (bf16[128,128]{1,0:T(8,128)(2,1)S(1)}, bf16[128,128]{1,0:T(8,128)(2,1)S(1)}, u32[]{:S(2)}, u32[]{:S(2)}) collective-permute-start(bf16[128,128]{1,0:T(8,128)(2,1)S(1)} %fusion.2), channel_id=1, source_target_pairs={{0,4},{1,5},{2,6},{3,7},{4,0},{5,1},{6,2},{7,3},{8,12},{9,13},{10,... | collective-permute-start | bytes 98312 | tf_op jit(solution)/shard_map/ppermute | solution.py:374
  28.1 5.5 %collective-permute-start.5 = (bf16[128,128]{1,0:T(8,128)(2,1)S(1)}, bf16[128,128]{1,0:T(8,128)(2,1)S(1)}, u32[]{:S(2)}, u32[]{:S(2)}) collective-permute-start(bf16[128,128]{1,0:T(8,128)(2,1)S(1)} %fusion.1), channel_id=1, source_target_pairs={{0,8},{1,9},{2,10},{3,11},{4,12},{5,13},{6,14},{7,15},{8,0},{9,1},... | collective-permute-start | bytes 98312 | tf_op jit(solution)/shard_map/ppermute | solution.py:374
  36.9 9.4 %collective-permute-start.7 = (f32[8,3,256]{2,1,0:T(4,128)S(1)}, f32[8,3,256]{2,1,0:T(4,128)S(1)}, u32[]{:S(2)}, u32[]{:S(2)}) collective-permute-start(f32[8,3,256]{2,1,0:T(4,128)S(1)} %get-tuple-element.26), channel_id=1, source_target_pairs={{16,32},{48,64},{80,96},{32,16},{64,48},{96,80},{17,33},{49,65},{8... | collective-permute-start | bytes 73736 | tf_op jit(solution)/shard_map/ppermute | solution.py:368
  43.7 4.0 %collective-permute-start.6 = (f32[8,3,256]{2,1,0:T(4,128)S(1)}, f32[8,3,256]{2,1,0:T(4,128)S(1)}, u32[]{:S(2)}, u32[]{:S(2)}) collective-permute-start(f32[8,3,256]{2,1,0:T(4,128)S(1)} %get-tuple-element.27), channel_id=1, source_target_pairs={{0,16},{16,0},{32,48},{48,32},{64,80},{80,64},{96,112},{112,96},{1... | collective-permute-start | bytes 73736 | tf_op jit(solution)/shard_map/ppermute | solution.py:365

commit v3 on v2

--- a/solution.py
+++ b/solution.py
@@ -260,27 +260,22 @@
     sent_ref[...] = partial.astype(BF)
 
 
+def choose_kernel(subset_ref, _, projector_ref, chosen_ref, sem):
+    copy = pltpu.make_async_copy(projector_ref.at[subset_ref[0] % SUBSETS], chosen_ref, sem)
+    copy.start()
+    copy.wait()
+
+
 def back_kernel(
     subset_ref,
     measured_ref,
     sinogram_ref,
     axial_ref,
-    projector_ref,
+    chosen_ref,
     corrected_ref,
     residual_ref,
-    chosen_ref,
     held_ref,
-    sems,
 ):
-    copies = []
-    for part in range(8):
-        rows = pl.ds(part * 1024, 1024)
-        copies.append(
-            pltpu.make_async_copy(
-                projector_ref.at[subset_ref[0] % SUBSETS, rows], chosen_ref.at[rows], sems.at[part]
-            )
-        )
-        copies[-1].start()
     residual = measured_ref[...] - sinogram_ref[...]
     held_ref[...] = residual
     unfold = jnp.where(iota((128, 1024), 1) // 8 == iota((128, 1024), 0), 1.0, 0.0).astype(BF)
@@ -291,7 +286,6 @@
     for part in range(8):
         rays = wide[part * 16 : (part + 1) * 16]
         spread = jnp.concatenate([jnp.where(lane == y, rays, zero) for y in range(8)], axis=0)
-        copies[part].wait()
         total = total + jnp.dot(
             spread, chosen_ref[part * 1024 : (part + 1) * 1024, :], preferred_element_type=F32
         )
@@ -369,15 +363,15 @@
     return first, second
 
 
-def sum_over_gy(partial, sent, axial):
+def sum_over_gy(partial, sent, later):
     def partner(value, bits):
         return lax.ppermute(value, "gy", [(i, i ^ bits) for i in range(16)]).astype(F32)
 
     total = partial + partner(sent, 1)
-    total = total + partner(total.astype(BF), 2)
-    sent, axial = lax.optimization_barrier((total.astype(BF), axial))
-    total = total + partner(sent, 4)
-    return total + partner(total.astype(BF), 8), axial
+    sent = total.astype(BF)
+    total = total + partner(sent, 2) + partner(sent, 4) + partner(sent, 6)
+    sent, later = lax.optimization_barrier((total.astype(BF), later))
+    return total + partner(sent, 8), later, sent
 
 
 def per_device(
@@ -405,7 +399,7 @@
         + (jax.ShapeDtypeStruct((128, 128), F32),),
         in_specs=[vmem()] * 6,
         out_specs=(vmem(),) * 5,
-        compiler_params=params(48),
+        compiler_params=params(40),
         cost_estimate=pl.CostEstimate(flops=1000000, bytes_accessed=3000000, transcendentals=0),
     )(
         coronal_in[:, :, 0],
@@ -450,7 +444,17 @@
     )
     zero = timestep[0].astype(F32) * 0.0
     partial = lax.optimization_barrier(partial + zero)
-    sinogram, axial = sum_over_gy(partial, sent, axial)
+    sinogram, axial, sent = sum_over_gy(partial, sent, axial)
+    chosen = pl.pallas_call(
+        choose_kernel,
+        name="choose",
+        out_shape=jax.ShapeDtypeStruct((8192, 256), BF),
+        in_specs=[smem(), vmem(), hbm()],
+        out_specs=vmem(),
+        scratch_shapes=[pltpu.SemaphoreType.DMA],
+        compiler_params=params(46),
+        cost_estimate=pl.CostEstimate(flops=0, bytes_accessed=8 << 20, transcendentals=0),
+    )(subset, sent, flat_projector)
     axial = lax.optimization_barrier(axial + zero)
     corrected, residual = pl.pallas_call(
         back_kernel,
@@ -459,15 +463,11 @@
             jax.ShapeDtypeStruct((8, 16, 256), F32),
             jax.ShapeDtypeStruct((12, 64), F32),
         ),
-        in_specs=[smem()] + [vmem()] * 3 + [hbm()],
+        in_specs=[smem()] + [vmem()] * 4,
         out_specs=(vmem(), vmem()),
-        scratch_shapes=[
-            pltpu.VMEM((8192, 256), BF),
-            pltpu.VMEM((128, 128), F32),
-            pltpu.SemaphoreType.DMA((8,)),
-        ],
-        compiler_params=params(48),
-    )(subset, turned, sinogram, axial, flat_projector)
+        scratch_shapes=[pltpu.VMEM((128, 128), F32)],
+        compiler_params=params(40),
+    )(subset, turned, sinogram, axial, chosen)
     first, second = exchange(corrected[:, :HALO], corrected[:, 12 - HALO : 12], "gz", False)
     restored = pl.pallas_call(
         coronal_kernel,

time: 53.9 us -> 51 us (0.946)
  waiting for transfers between devices: 11.3 us -> 6.01 us
  starting transfers between devices: 17 us -> 19 us
    ppermute x4 -> x5, waiting for transfers between devices: 7.2 us -> 1.95 us  [partner(): lax.ppermute(value, 'gy', [(i, i ^ bits) for i in range(16)]).astype(F32)]
    ppermute x4 -> x5, starting transfers between devices: 6.16 us -> 8.5 us  [partner(): lax.ppermute(value, 'gy', [(i, i ^ bits) for i in range(16)]).astype(F32)]
    pallas_call x0 -> x1, Pallas kernels: none -> 2.21 us  [per_device(): pl.pallas_call(choose_kernel, name='choose', out_shape=jax.ShapeDtypeStru...]
    pallas_call x1, Pallas kernels: 3.3 us -> 1.45 us  [per_device(): pl.pallas_call(back_kernel, name='back', out_shape=(jax.ShapeDtypeStruct(...]
  transfers between devices with their start and end apart: 8 -> 9, of which waited for: 7 -> 6; matrix products, arithmetic and copies ran while one was open for 3% -> 3% of each run, Pallas kernels for 1% -> 6%
where the time goes in v3:
time: 51 us; the launch traced here: 50.7 us
  Pallas kernels  20 us (39%)
  starting transfers between devices  19 us (37%)
  waiting for transfers between devices  6.01 us (12%)
  other arithmetic  2.89 us (6%)
  between operations  2.1 us (4%)
  local copies, waits for them, and re-layouts  0.65 us (1%)
    pallas_call x1, Pallas kernels, per_device(): pl.pallas_call(axial_kernel, name='axial', out_shape=(jax.ShapeDtypeStruc...  9.87 us
    ppermute x2, starting transfers between devices, exchange(): second = lax.ppermute(outer, axis, outer_pairs(size))  8.67 us
    ppermute x5, starting transfers between devices, partner(): lax.ppermute(value, 'gy', [(i, i ^ bits) for i in range(16)]).astype(F32)  8.5 us
    pallas_call x1, Pallas kernels, per_device(): pl.pallas_call(coronal_kernel, name='coronal', out_shape=jax.ShapeDtypeSt...  5.9 us
    ppermute x2, waiting for transfers between devices, exchange(): second = lax.ppermute(outer, axis, outer_pairs(size))  2.98 us
    pallas_call x1, Pallas kernels, per_device(): pl.pallas_call(choose_kernel, name='choose', out_shape=jax.ShapeDtypeStru...  2.21 us
    ppermute x5, waiting for transfers between devices, partner(): lax.ppermute(value, 'gy', [(i, i ^ bits) for i in range(16)]).astype(F32)  1.95 us
    ppermute x2, starting transfers between devices, exchange(): first = lax.ppermute(inner, axis, inner_pairs(size))  1.85 us
  transfers between devices with their start and end apart: 9, of which 6 were waited for; matrix products, arithmetic and copies ran while one was open for 3% of the time, Pallas kernels for 6%

profile of v3, /device:TPU:6, one launch (start us, length us, event | category | flops | bytes accessed | tf_op | source)
XLA Modules:
  0.0 50.7 jit_solution(11145833045630809147)
XLA Ops:
  0.7 1.1 %slice_select_fusion = (f32[12,3,256]{2,1,0:T(4,128)S(1)}, f32[12,3,256]{2,1,0:T(4,128)S(1)}) fusion(f32[12,8,256]{2,1,0:T(8,128)} %volume_ref.1, pred[]{:T(512)S(6)} %eq.9), kind=kLoop, calls=%fused_computation.5 | loop fusion | flops 18432 | bytes 147457 | tf_op jit(solution)/shard_map/jit(_where)/select_n | solution.py:358
  1.8 2.2 %collective-permute-start.1 = (f32[12,3,256]{2,1,0:T(4,128)S(1)}, f32[12,3,256]{2,1,0:T(4,128)S(1)}, u32[]{:S(2)}, u32[]{:S(2)}) collective-permute-start(f32[12,3,256]{2,1,0:T(4,128)S(1)} %get-tuple-element.28), channel_id=1, source_target_pairs={{1,2},{3,4},{5,6},{7,8},{9,10},{11,12},{13,14},{2,1},{4,3},{6,5},{... | collective-permute-start | bytes 110600 | tf_op jit(solution)/shard_map/ppermute | solution.py:362
  3.9 1.8 %collective-permute-start = (f32[12,3,256]{2,1,0:T(4,128)S(1)}, f32[12,3,256]{2,1,0:T(4,128)S(1)}, u32[]{:S(2)}, u32[]{:S(2)}) collective-permute-start(f32[12,3,256]{2,1,0:T(4,128)S(1)} %get-tuple-element.29), channel_id=1, source_target_pairs={{0,1},{1,0},{2,3},{3,2},{4,5},{5,4},{6,7},{7,6},{8,9},{9,8},{10,11... | collective-permute-start | bytes 110600 | tf_op jit(solution)/shard_map/ppermute | solution.py:359
  7.0 0.2 collective-permute-done.1.second_ref
  7.2 0.6 %copy-done.6 = f32[12,3,256]{2,1,0:T(4,128)} copy-done((f32[12,3,256]{2,1,0:T(4,128)}, f32[12,3,256]{2,1,0:T(4,128)S(1)}, u32[]{:S(2)}) %copy-start.6) | copy-done | bytes 36888
  7.8 0.0 copy-done.7
  7.8 9.9 %axial.1 = (f32[8,16,256]{2,1,0:T(8,128)}, f32[128,128]{1,0:T(8,128)}, bf16[128,128]{1,0:T(8,128)(2,1)}) custom-call(s32[1]{0:T(128)S(6)} %copy.17.subset_ref, s32[1]{0:T(128)S(6)} %copy.18.timestep_ref, f32[12,8,256]{2,1,0:T(8,128)} %volume_ref.1, f32[12,3,256]{2,1,0:T(4,128)} %copy-done.7, f32[12,3,256]{2,1,0:T(4,128)} %copy-done.6, ...), custom_call_target="tpu_custom_call" | custom-call | tf_op jit(solution)/shard_map/axial/pallas_call | solution.py:414
  17.7 1.2 %collective-permute-start.2 = (bf16[128,128]{1,0:T(8,128)(2,1)}, bf16[128,128]{1,0:T(8,128)(2,1)S(1)}, u32[]{:S(2)}, u32[]{:S(2)}) collective-permute-start(bf16[128,128]{1,0:T(8,128)(2,1)} %get-tuple-element.16), channel_id=1, source_target_pairs={{0,1},{1,0},{2,3},{3,2},{4,5},{5,4},{6,7},{7,6},{8,9},{9,8},{10,11... | collective-permute-start | bytes 98312 | tf_op jit(solution)/shard_map/ppermute | solution.py:368
  18.9 0.8 %broadcast_add_fusion.1 = f32[128,128]{1,0:T(8,128)S(1)} fusion(f32[128,128]{1,0:T(8,128)} %get-tuple-element.15, f32[]{:T(128)} %bitcast.10), kind=kLoop, calls=%fused_computation.7 | loop fusion | flops 16384 | bytes 131076 | tf_op jit(solution)/shard_map/add | solution.py:446
  19.7 0.2 collective-permute-done.2
  20.0 2.0 %collective-permute-start.5 = (bf16[128,128]{1,0:T(8,128)(2,1)S(1)}, bf16[128,128]{1,0:T(8,128)(2,1)S(1)}, u32[]{:S(2)}, u32[]{:S(2)}) collective-permute-start(bf16[128,128]{1,0:T(8,128)(2,1)S(1)} %fusion), channel_id=1, source_target_pairs={{0,6},{1,7},{2,4},{3,5},{4,2},{5,3},{6,0},{7,1},{8,14},{9,15},{10,... | collective-permute-start | bytes 98312 | tf_op jit(solution)/shard_map/ppermute | solution.py:368
  22.0 1.5 %collective-permute-start.3 = (bf16[128,128]{1,0:T(8,128)(2,1)S(1)}, bf16[128,128]{1,0:T(8,128)(2,1)S(1)}, u32[]{:S(2)}, u32[]{:S(2)}) collective-permute-start(bf16[128,128]{1,0:T(8,128)(2,1)S(1)} %fusion), channel_id=1, source_target_pairs={{0,2},{1,3},{2,0},{3,1},{4,6},{5,7},{6,4},{7,5},{8,10},{9,11},{10,... | collective-permute-start | bytes 98312 | tf_op jit(solution)/shard_map/ppermute | solution.py:368
  23.6 0.6 %prepare.1 = (bf16[1024,128]{1,0:T(8,128)(2,1)S(1)}, bf16[128,768]{1,0:T(8,128)(2,1)S(1)}, f32[64,256]{1,0:T(8,128)S(1)}, bf16[48,896]{1,0:T(8,128)(2,1)S(1)}, f32[128,128]{1,0:T(8,128)S(1)}) custom-call(bf16[9,64]{1,0:T(8,128)(2,1)S(1)} %bitcast.13, f32[1,64]{1,0:T(1,128)S(1)} %bitcast.15, f32[1,64]{1,0:T(1,128)S(1)} %bitcast.16, ...), custom_call_target="tpu_custom_call" | custom-call | flops 1000000 | bytes 3000000 | tf_op jit(solution)/shard_map/prepare/pallas_call | solution.py:395
  24.2 0.8 %collective-permute-done.5 = bf16[128,128]{1,0:T(8,128)(2,1)S(1)} collective-permute-done((bf16[128,128]{1,0:T(8,128)(2,1)S(1)}, bf16[128,128]{1,0:T(8,128)(2,1)S(1)}, u32[]{:S(2)}, u32[]{:S(2)}) %collective-permute-start.5) | collective-permute-done | bytes 32800 | tf_op jit(solution)/shard_map/ppermute | solution.py:368
  25.0 0.9 %collective-permute-done.4 = bf16[128,128]{1,0:T(8,128)(2,1)S(1)} collective-permute-done((bf16[128,128]{1,0:T(8,128)(2,1)S(1)}, bf16[128,128]{1,0:T(8,128)(2,1)S(1)}, u32[]{:S(2)}, u32[]{:S(2)}) %collective-permute-start.4) | collective-permute-done | bytes 32800 | tf_op jit(solution)/shard_map/ppermute | solution.py:368
  26.0 3.7 %collective-permute-start.6 = (bf16[128,128]{1,0:T(8,128)(2,1)S(1)}, bf16[128,128]{1,0:T(8,128)(2,1)S(1)}, u32[]{:S(2)}, u32[]{:S(2)}) collective-permute-start(bf16[128,128]{1,0:T(8,128)(2,1)S(1)} %fusion.1._), channel_id=1, source_target_pairs={{0,8},{1,9},{2,10},{3,11},{4,12},{5,13},{6,14},{7,15},{8,0},{9,1},... | collective-permute-start | bytes 98312 | tf_op jit(solution)/shard_map/ppermute | solution.py:368
  29.7 0.9 %broadcast_add_fusion.axial_ref = f32[8,16,256]{2,1,0:T(8,128)S(1)} fusion(f32[8,16,256]{2,1,0:T(8,128)} %get-tuple-element.19, f32[]{:T(128)} %bitcast.10), kind=kLoop, calls=%fused_computation | loop fusion | flops 32768 | bytes 262148 | tf_op jit(solution)/shard_map/add | solution.py:458
  30.6 2.2 %choose.1.chosen_ref = bf16[8192,256]{1,0:T(8,128)(2,1)S(1)} custom-call(s32[1]{0:T(128)S(6)} %copy.17.subset_ref, bf16[128,128]{1,0:T(8,128)(2,1)S(1)} %fusion.1._, bf16[4,8192,256]{2,1,0:T(8,128)(2,1)} %bitcast.18), custom_call_target="tpu_custom_call" | custom-call | bytes 8388608 | tf_op jit(solution)/shard_map/choose/pallas_call | solution.py:448
  32.8 1.5 %back.1 = (f32[8,16,256]{2,1,0:T(8,128)S(1)}, f32[12,64]{1,0:T(8,128)}) custom-call(s32[1]{0:T(128)S(6)} %copy.17.subset_ref, f32[128,128]{1,0:T(8,128)S(1)} %get-tuple-element.14.measured_ref, f32[128,128]{1,0:T(8,128)S(1)} %convert_add_fusion.sinogram_ref, f32[8,16,256]{2,1,0:T(8,128)S(1)} %broadcast_add_fusion.axial_ref, ...), custom_call_target="tpu_custom_call" | custom-call | tf_op jit(solution)/shard_map/back/pallas_call | solution.py:459
  34.3 6.5 %collective-permute-start.8 = (f32[8,3,256]{2,1,0:T(4,128)S(1)}, f32[8,3,256]{2,1,0:T(4,128)S(1)}, u32[]{:S(2)}, u32[]{:S(2)}) collective-permute-start(f32[8,3,256]{2,1,0:T(4,128)S(1)} %get-tuple-element.26), channel_id=1, source_target_pairs={{16,32},{48,64},{80,96},{32,16},{64,48},{96,80},{17,33},{49,65},{8... | collective-permute-start | bytes 73736 | tf_op jit(solution)/shard_map/ppermute | solution.py:362
  40.8 0.1 collective-permute-start.7
  40.9 2.8 %collective-permute-done.8.second_ref = f32[8,3,256]{2,1,0:T(4,128)S(1)} collective-permute-done((f32[8,3,256]{2,1,0:T(4,128)S(1)}, f32[8,3,256]{2,1,0:T(4,128)S(1)}, u32[]{:S(2)}, u32[]{:S(2)}) %collective-permute-start.8) | collective-permute-done | bytes 24608 | tf_op jit(solution)/shard_map/ppermute | solution.py:362
  43.7 1.1 %collective-permute-done.7.first_ref = f32[8,3,256]{2,1,0:T(4,128)S(1)} collective-permute-done((f32[8,3,256]{2,1,0:T(4,128)S(1)}, f32[8,3,256]{2,1,0:T(4,128)S(1)}, u32[]{:S(2)}, u32[]{:S(2)}) %collective-permute-start.7) | collective-permute-done | bytes 24608 | tf_op jit(solution)/shard_map/ppermute | solution.py:359
  44.8 5.9 %coronal.1 = f32[12,8,256]{2,1,0:T(8,128)} custom-call(s32[1]{0:T(128)S(6)} %copy.18.timestep_ref, f32[8,16,256]{2,1,0:T(8,128)S(1)} %get-tuple-element.20.corrected_ref, f32[8,3,256]{2,1,0:T(4,128)S(1)} %collective-permute-done.7.first_ref, f32[8,3,256]{2,1,0:T(4,128)S(1)} %collective-permute-done.8.second_ref, ...), custom_call_target="tpu_custom_call" | custom-call | tf_op jit(solution)/shard_map/coronal/pallas_call | solution.py:472
  (22 shorter events, 0.1 us)
Async XLA Ops:
  0.6 22.9 %copy-start.3 = (bf16[9,1,64]{2,0,1:T(8,128)(2,1)S(1)}, bf16[9,1,64]{2,0,1:T(8,128)(2,1)}, u32[]{:S(2)}) copy-start(bf16[9,1,64]{2,0,1:T(8,128)(2,1)} %param.29) | copy-start | bytes 3460
  0.6 22.9 %copy-start.5 = (f32[64]{0:T(128)S(1)}, f32[64]{0:T(128)}, u32[]{:S(2)}) copy-start(f32[64]{0:T(128)} %param.28) | copy-start | bytes 772
  0.7 22.9 %copy-start = (bf16[9,64,64]{2,1,0:T(8,128)(2,1)S(1)}, bf16[9,64,64]{2,1,0:T(8,128)(2,1)}, u32[]{:S(2)}) copy-start(bf16[9,64,64]{2,1,0:T(8,128)(2,1)} %refs_4_.1) | copy-start | bytes 221188
  0.7 22.9 %copy-start.4 = (f32[64]{0:T(128)S(1)}, f32[64]{0:T(128)}, u32[]{:S(2)}) copy-start(f32[64]{0:T(128)} %param.26) | copy-start | bytes 772
  0.7 22.9 %copy-start.2 = (bf16[9,64,1]{1,0,2:T(8,128)(2,1)S(1)}, bf16[9,64,1]{1,0,2:T(8,128)(2,1)}, u32[]{:S(2)}) copy-start(bf16[9,64,1]{1,0,2:T(8,128)(2,1)} %param.25) | copy-start | bytes 3460
  0.7 22.9 %copy-start.1 = (f32[1024,12]{0,1:T(8,128)S(1)}, f32[1024,12]{0,1:T(8,128)}, u32[]{:S(2)}) copy-start(f32[1024,12]{0,1:T(8,128)} %param.17) | copy-start | bytes 147460
  1.8 5.4 %collective-permute-start.1 = (f32[12,3,256]{2,1,0:T(4,128)S(1)}, f32[12,3,256]{2,1,0:T(4,128)S(1)}, u32[]{:S(2)}, u32[]{:S(2)}) collective-permute-start(f32[12,3,256]{2,1,0:T(4,128)S(1)} %get-tuple-element.28), channel_id=1, source_target_pairs={{1,2},{3,4},{5,6},{7,8},{9,10},{11,12},{13,14},{2,1},{4,3},{6,5},{... | collective-permute-start | bytes 110600 | tf_op jit(solution)/shard_map/ppermute | solution.py:362
  3.9 3.2 %collective-permute-start = (f32[12,3,256]{2,1,0:T(4,128)S(1)}, f32[12,3,256]{2,1,0:T(4,128)S(1)}, u32[]{:S(2)}, u32[]{:S(2)}) collective-permute-start(f32[12,3,256]{2,1,0:T(4,128)S(1)} %get-tuple-element.29), channel_id=1, source_target_pairs={{0,1},{1,0},{2,3},{3,2},{4,5},{5,4},{6,7},{7,6},{8,9},{9,8},{10,11... | collective-permute-start | bytes 110600 | tf_op jit(solution)/shard_map/ppermute | solution.py:359
  7.2 0.6 %copy-start.6 = (f32[12,3,256]{2,1,0:T(4,128)}, f32[12,3,256]{2,1,0:T(4,128)S(1)}, u32[]{:S(2)}) copy-start(f32[12,3,256]{2,1,0:T(4,128)S(1)} %collective-permute-done.1.second_ref) | copy-start | bytes 110596
  7.2 0.6 %copy-start.7 = (f32[12,3,256]{2,1,0:T(4,128)}, f32[12,3,256]{2,1,0:T(4,128)S(1)}, u32[]{:S(2)}) copy-start(f32[12,3,256]{2,1,0:T(4,128)S(1)} %collective-permute-done.first_ref) | copy-start | bytes 110596
  17.7 2.3 %collective-permute-start.2 = (bf16[128,128]{1,0:T(8,128)(2,1)}, bf16[128,128]{1,0:T(8,128)(2,1)S(1)}, u32[]{:S(2)}, u32[]{:S(2)}) collective-permute-start(bf16[128,128]{1,0:T(8,128)(2,1)} %get-tuple-element.16), channel_id=1, source_target_pairs={{0,1},{1,0},{2,3},{3,2},{4,5},{5,4},{6,7},{7,6},{8,9},{9,8},{10,11... | collective-permute-start | bytes 98312 | tf_op jit(solution)/shard_map/ppermute | solution.py:368
  20.0 5.0 %collective-permute-start.5 = (bf16[128,128]{1,0:T(8,128)(2,1)S(1)}, bf16[128,128]{1,0:T(8,128)(2,1)S(1)}, u32[]{:S(2)}, u32[]{:S(2)}) collective-permute-start(bf16[128,128]{1,0:T(8,128)(2,1)S(1)} %fusion), channel_id=1, source_target_pairs={{0,6},{1,7},{2,4},{3,5},{4,2},{5,3},{6,0},{7,1},{8,14},{9,15},{10,... | collective-permute-start | bytes 98312 | tf_op jit(solution)/shard_map/ppermute | solution.py:368
  22.0 3.9 %collective-permute-start.4 = (bf16[128,128]{1,0:T(8,128)(2,1)S(1)}, bf16[128,128]{1,0:T(8,128)(2,1)S(1)}, u32[]{:S(2)}, u32[]{:S(2)}) collective-permute-start(bf16[128,128]{1,0:T(8,128)(2,1)S(1)} %fusion), channel_id=1, source_target_pairs={{0,4},{1,5},{2,6},{3,7},{4,0},{5,1},{6,2},{7,3},{8,12},{9,13},{10,... | collective-permute-start | bytes 98312 | tf_op jit(solution)/shard_map/ppermute | solution.py:368
  22.0 3.9 %collective-permute-start.3 = (bf16[128,128]{1,0:T(8,128)(2,1)S(1)}, bf16[128,128]{1,0:T(8,128)(2,1)S(1)}, u32[]{:S(2)}, u32[]{:S(2)}) collective-permute-start(bf16[128,128]{1,0:T(8,128)(2,1)S(1)} %fusion), channel_id=1, source_target_pairs={{0,2},{1,3},{2,0},{3,1},{4,6},{5,7},{6,4},{7,5},{8,10},{9,11},{10,... | collective-permute-start | bytes 98312 | tf_op jit(solution)/shard_map/ppermute | solution.py:368
  26.0 6.8 %collective-permute-start.6 = (bf16[128,128]{1,0:T(8,128)(2,1)S(1)}, bf16[128,128]{1,0:T(8,128)(2,1)S(1)}, u32[]{:S(2)}, u32[]{:S(2)}) collective-permute-start(bf16[128,128]{1,0:T(8,128)(2,1)S(1)} %fusion.1._), channel_id=1, source_target_pairs={{0,8},{1,9},{2,10},{3,11},{4,12},{5,13},{6,14},{7,15},{8,0},{9,1},... | collective-permute-start | bytes 98312 | tf_op jit(solution)/shard_map/ppermute | solution.py:368
  34.3 9.4 %collective-permute-start.8 = (f32[8,3,256]{2,1,0:T(4,128)S(1)}, f32[8,3,256]{2,1,0:T(4,128)S(1)}, u32[]{:S(2)}, u32[]{:S(2)}) collective-permute-start(f32[8,3,256]{2,1,0:T(4,128)S(1)} %get-tuple-element.26), channel_id=1, source_target_pairs={{16,32},{48,64},{80,96},{32,16},{64,48},{96,80},{17,33},{49,65},{8... | collective-permute-start | bytes 73736 | tf_op jit(solution)/shard_map/ppermute | solution.py:362
  40.8 4.0 %collective-permute-start.7 = (f32[8,3,256]{2,1,0:T(4,128)S(1)}, f32[8,3,256]{2,1,0:T(4,128)S(1)}, u32[]{:S(2)}, u32[]{:S(2)}) collective-permute-start(f32[8,3,256]{2,1,0:T(4,128)S(1)} %get-tuple-element.27), channel_id=1, source_target_pairs={{0,16},{16,0},{32,48},{48,32},{64,80},{80,64},{96,112},{112,96},{1... | collective-permute-start | bytes 73736 | tf_op jit(solution)/shard_map/ppermute | solution.py:359

commit v4 on v3

--- a/solution.py
+++ b/solution.py
@@ -145,9 +145,9 @@
     return jnp.concatenate([left, entry, right], axis=0).astype(BF)
 
 
-def layer_one(spread, rows_one, one_ref, taps_ref):
+def layer_one(spread, rows, one_ref, taps_ref):
     depth = spread.shape[0]
-    for row in range(rows_one):
+    for row in rows:
         hidden = jnp.dot(
             one_ref[row * 64 : (row + 1) * 64, 0:depth], spread, preferred_element_type=F32
         )
@@ -158,19 +158,19 @@
         taps_ref[row * 192 + 128 : row * 192 + 192, :] = right
 
 
-def layer_two(rows_two, middle_ref, bias_ref, taps_ref, hidden_ref):
+def layer_two(pairs, middle_ref, bias_ref, taps_ref, hidden_ref, base=0):
     bias = bias_ref[...]
-    for row in range(0, rows_two, 2):
+    for row in pairs:
         summed = jnp.dot(
             middle_ref[...], taps_ref[row * 192 : (row + 4) * 192, :], preferred_element_type=F32
         )
         for k in range(2):
             value = jnp.maximum(summed[k * 64 : (k + 1) * 64] + bias, 0.0)
-            hidden_ref[(row + k) * 64 : (row + k + 1) * 64, :] = value.astype(BF)
-
-
-def layer_three(rows, last_ref, hidden_ref):
-    last = jnp.dot(last_ref[...], hidden_ref[...], preferred_element_type=F32)
+            place = (row + k - base) * 64
+            hidden_ref[place : place + 64, :] = value.astype(BF)
+
+
+def layer_three(rows, last):
     left, _ = shifted(last[0:rows])
     _, right = shifted(last[2 * rows : 3 * rows])
     return left + last[rows : 2 * rows] + right
@@ -180,10 +180,11 @@
     one_ref, middle_ref, bias_ref, last_ref = weights
     taps, hidden = scratch[0:PLANES], scratch[PLANES : 2 * PLANES]
     for k in range(PLANES):
-        layer_one(spread_entry(*entries[k]), own + 4, one_ref, taps[k])
+        layer_one(spread_entry(*entries[k]), range(own + 4), one_ref, taps[k])
     for k in range(PLANES):
-        layer_two(own + 2, middle_ref, bias_ref, taps[k], hidden[k])
-    return [layer_three(-(-own // 8) * 8, last_ref, hidden[k]) for k in range(PLANES)]
+        layer_two(range(0, own + 2, 2), middle_ref, bias_ref, taps[k], hidden[k])
+    last = [jnp.dot(last_ref[...], hidden[k][...], preferred_element_type=F32) for k in range(PLANES)]
+    return [layer_three(-(-own // 8) * 8, last[k]) for k in range(PLANES)]
 
 
 def network_scratch(own):
@@ -295,11 +296,34 @@
     residual_ref[...] = jnp.where(index % 2 == 1, block[0:12, 64:128], block[0:12, 0:64])
 
 
+def inner_kernel(
+    timestep_ref, corrected_ref, one_ref, middle_ref, bias_ref, last_ref, inner_ref, *scratch
+):
+    taps, hidden = scratch[0:PLANES], scratch[PLANES:]
+    scale_in, _ = noise_scales(timestep_ref)
+    absent = jnp.zeros((HALO, 256), F32)
+
+    def planes(step, carry):
+        for k in range(PLANES):
+            entry = corrected_ref[step * PLANES + k] * scale_in
+            layer_one(spread_entry(entry, absent, absent), range(4, 12), one_ref, taps[k])
+        for k in range(PLANES):
+            layer_two((4, 6, 8), middle_ref, bias_ref, taps[k], hidden[k], 4)
+        for k in range(PLANES):
+            inner_ref[step * PLANES + k] = jnp.dot(
+                last_ref[:, 256:640], hidden[k][...], preferred_element_type=F32
+            )
+        return carry
+
+    lax.fori_loop(0, 8 // PLANES, planes, 0)
+
+
 def coronal_kernel(
     timestep_ref,
     corrected_ref,
     first_ref,
     second_ref,
+    inner_ref,
     one_ref,
     middle_ref,
     bias_ref,
@@ -308,17 +332,23 @@
     *scratch,
 ):
     scale_in, scale_out = noise_scales(timestep_ref)
-    weights = (one_ref, middle_ref, bias_ref, last_ref)
+    taps, low, high = scratch[0:PLANES], scratch[PLANES : 2 * PLANES], scratch[2 * PLANES :]
+    edges = (*range(0, 6), *range(10, 16))
 
     def planes(step, carry):
-        entries = []
         for k in range(PLANES):
             p = step * PLANES + k
-            entries.append((corrected_ref[p] * scale_in, first_ref[p] * scale_in, second_ref[p] * scale_in))
-        nets = networks(entries, 12, weights, scratch)
+            rows = [ref[p] * scale_in for ref in (corrected_ref, first_ref, second_ref)]
+            layer_one(spread_entry(*rows), edges, one_ref, taps[k])
+        for k in range(PLANES):
+            layer_two((0, 2), middle_ref, bias_ref, taps[k], low[k])
+            layer_two((10, 12), middle_ref, bias_ref, taps[k], high[k], 10)
         for k in range(PLANES):
             p = step * PLANES + k
-            value = corrected_ref[p] + scale_out * nets[k]
+            last = inner_ref[p]
+            last = last + jnp.dot(last_ref[:, 0:256], low[k][...], preferred_element_type=F32)
+            last = last + jnp.dot(last_ref[:, 640:896], high[k][...], preferred_element_type=F32)
+            value = corrected_ref[p] + scale_out * layer_three(16, last)
             for z in range(12):
                 restored_ref[z, pl.ds(p, 1), :] = value[z : z + 1, :]
         return carry
@@ -469,15 +499,26 @@
         compiler_params=params(40),
     )(subset, turned, sinogram, axial, chosen)
     first, second = exchange(corrected[:, :HALO], corrected[:, 12 - HALO : 12], "gz", False)
+    taps_scratch = [pltpu.VMEM((16 * 192, 256), BF)] * PLANES
+    inner = pl.pallas_call(
+        inner_kernel,
+        name="inner",
+        out_shape=jax.ShapeDtypeStruct((8, 48, 256), F32),
+        in_specs=[smem()] + [vmem()] * 5,
+        out_specs=vmem(),
+        scratch_shapes=taps_scratch + [pltpu.VMEM((6 * 64, 256), BF)] * PLANES,
+        compiler_params=params(40),
+        cost_estimate=pl.CostEstimate(flops=2000000000, bytes_accessed=2 << 20, transcendentals=0),
+    )(timestep, corrected, *coronal_weights)
     restored = pl.pallas_call(
         coronal_kernel,
         name="coronal",
         out_shape=jax.ShapeDtypeStruct((12, 8, 256), F32),
-        in_specs=[smem()] + [vmem()] * 7,
+        in_specs=[smem()] + [vmem()] * 8,
         out_specs=vmem(),
-        scratch_shapes=network_scratch(12),
-        compiler_params=params(48),
-    )(timestep, corrected, first, second, *coronal_weights)
+        scratch_shapes=taps_scratch + [pltpu.VMEM((256, 256), BF)] * (2 * PLANES),
+        compiler_params=params(40),
+    )(timestep, corrected, first, second, inner, *coronal_weights)
     return (restored, residual.T)
 
 

time: 51 us -> 49.3 us (0.967)
  waiting for transfers between devices: 6.01 us -> 3.36 us
  Pallas kernels: 20 us -> 20.9 us
    ppermute x2, waiting for transfers between devices: 2.98 us -> 0.33 us  [exchange(): second = lax.ppermute(outer, axis, outer_pairs(size))]
    pallas_call x0 -> x1, Pallas kernels: none -> 2.65 us  [per_device(): pl.pallas_call(inner_kernel, name='inner', out_shape=jax.ShapeDtypeStruct...]
    pallas_call x1, Pallas kernels: 5.9 us -> 4.16 us  [per_device(): pl.pallas_call(coronal_kernel, name='coronal', out_shape=jax.ShapeDtypeSt...]
  transfers between devices with their start and end apart: 9 -> 9, of which waited for: 6 -> 6; matrix products, arithmetic and copies ran while one was open for 3% -> 4% of each run, Pallas kernels for 6% -> 11%
where the time goes in v4:
time: 49.3 us; the launch traced here: 49 us
  Pallas kernels  20.9 us (42%)
  starting transfers between devices  19 us (39%)
  waiting for transfers between devices  3.36 us (7%)
  other arithmetic  2.89 us (6%)
  between operations  2.1 us (4%)
  local copies, waits for them, and re-layouts  0.65 us (1%)
    pallas_call x1, Pallas kernels, per_device(): pl.pallas_call(axial_kernel, name='axial', out_shape=(jax.ShapeDtypeStruc...  9.87 us
    ppermute x2, starting transfers between devices, exchange(): second = lax.ppermute(outer, axis, outer_pairs(size))  8.67 us
    ppermute x5, starting transfers between devices, partner(): lax.ppermute(value, 'gy', [(i, i ^ bits) for i in range(16)]).astype(F32)  8.5 us
    pallas_call x1, Pallas kernels, per_device(): pl.pallas_call(coronal_kernel, name='coronal', out_shape=jax.ShapeDtypeSt...  4.16 us
    pallas_call x1, Pallas kernels, per_device(): pl.pallas_call(inner_kernel, name='inner', out_shape=jax.ShapeDtypeStruct...  2.65 us
    pallas_call x1, Pallas kernels, per_device(): pl.pallas_call(choose_kernel, name='choose', out_shape=jax.ShapeDtypeStru...  2.21 us
    ppermute x5, waiting for transfers between devices, partner(): lax.ppermute(value, 'gy', [(i, i ^ bits) for i in range(16)]).astype(F32)  1.95 us
    ppermute x2, starting transfers between devices, exchange(): first = lax.ppermute(inner, axis, inner_pairs(size))  1.85 us
  transfers between devices with their start and end apart: 9, of which 6 were waited for; matrix products, arithmetic and copies ran while one was open for 4% of the time, Pallas kernels for 11%

profile of v4, /device:TPU:6, one launch (start us, length us, event | category | flops | bytes accessed | tf_op | source)
XLA Modules:
  0.0 49.0 jit_solution(4635134427244535459)
XLA Ops:
  0.7 1.1 %slice_select_fusion = (f32[12,3,256]{2,1,0:T(4,128)S(1)}, f32[12,3,256]{2,1,0:T(4,128)S(1)}) fusion(f32[12,8,256]{2,1,0:T(8,128)} %volume_ref.1, pred[]{:T(512)S(6)} %eq.9), kind=kLoop, calls=%fused_computation.5 | loop fusion | flops 18432 | bytes 147457 | tf_op jit(solution)/shard_map/jit(_where)/select_n | solution.py:388
  1.8 2.2 %collective-permute-start.1 = (f32[12,3,256]{2,1,0:T(4,128)S(1)}, f32[12,3,256]{2,1,0:T(4,128)S(1)}, u32[]{:S(2)}, u32[]{:S(2)}) collective-permute-start(f32[12,3,256]{2,1,0:T(4,128)S(1)} %get-tuple-element.28), channel_id=1, source_target_pairs={{1,2},{3,4},{5,6},{7,8},{9,10},{11,12},{13,14},{2,1},{4,3},{6,5},{... | collective-permute-start | bytes 110600 | tf_op jit(solution)/shard_map/ppermute | solution.py:392
  3.9 1.8 %collective-permute-start = (f32[12,3,256]{2,1,0:T(4,128)S(1)}, f32[12,3,256]{2,1,0:T(4,128)S(1)}, u32[]{:S(2)}, u32[]{:S(2)}) collective-permute-start(f32[12,3,256]{2,1,0:T(4,128)S(1)} %get-tuple-element.29), channel_id=1, source_target_pairs={{0,1},{1,0},{2,3},{3,2},{4,5},{5,4},{6,7},{7,6},{8,9},{9,8},{10,11... | collective-permute-start | bytes 110600 | tf_op jit(solution)/shard_map/ppermute | solution.py:389
  7.0 0.2 collective-permute-done.1.second_ref
  7.2 0.6 %copy-done.6 = f32[12,3,256]{2,1,0:T(4,128)} copy-done((f32[12,3,256]{2,1,0:T(4,128)}, f32[12,3,256]{2,1,0:T(4,128)S(1)}, u32[]{:S(2)}) %copy-start.6) | copy-done | bytes 36888
  7.8 9.9 %axial.1 = (f32[8,16,256]{2,1,0:T(8,128)}, f32[128,128]{1,0:T(8,128)}, bf16[128,128]{1,0:T(8,128)(2,1)}) custom-call(s32[1]{0:T(128)S(6)} %copy.17.subset_ref, s32[1]{0:T(128)S(6)} %copy.18.timestep_ref, f32[12,8,256]{2,1,0:T(8,128)} %volume_ref.1, f32[12,3,256]{2,1,0:T(4,128)} %copy-done.7, f32[12,3,256]{2,1,0:T(4,128)} %copy-done.6, ...), custom_call_target="tpu_custom_call" | custom-call | tf_op jit(solution)/shard_map/axial/pallas_call | solution.py:444
  17.7 1.2 %collective-permute-start.2 = (bf16[128,128]{1,0:T(8,128)(2,1)}, bf16[128,128]{1,0:T(8,128)(2,1)S(1)}, u32[]{:S(2)}, u32[]{:S(2)}) collective-permute-start(bf16[128,128]{1,0:T(8,128)(2,1)} %get-tuple-element.16), channel_id=1, source_target_pairs={{0,1},{1,0},{2,3},{3,2},{4,5},{5,4},{6,7},{7,6},{8,9},{9,8},{10,11... | collective-permute-start | bytes 98312 | tf_op jit(solution)/shard_map/ppermute | solution.py:398
  18.9 0.8 %broadcast_add_fusion.1 = f32[128,128]{1,0:T(8,128)S(1)} fusion(f32[128,128]{1,0:T(8,128)} %get-tuple-element.15, f32[]{:T(128)} %bitcast.10), kind=kLoop, calls=%fused_computation.7 | loop fusion | flops 16384 | bytes 131076 | tf_op jit(solution)/shard_map/add | solution.py:476
  19.7 0.2 collective-permute-done.2
  20.0 2.0 %collective-permute-start.5 = (bf16[128,128]{1,0:T(8,128)(2,1)S(1)}, bf16[128,128]{1,0:T(8,128)(2,1)S(1)}, u32[]{:S(2)}, u32[]{:S(2)}) collective-permute-start(bf16[128,128]{1,0:T(8,128)(2,1)S(1)} %fusion), channel_id=1, source_target_pairs={{0,6},{1,7},{2,4},{3,5},{4,2},{5,3},{6,0},{7,1},{8,14},{9,15},{10,... | collective-permute-start | bytes 98312 | tf_op jit(solution)/shard_map/ppermute | solution.py:398
  22.0 1.5 %collective-permute-start.3 = (bf16[128,128]{1,0:T(8,128)(2,1)S(1)}, bf16[128,128]{1,0:T(8,128)(2,1)S(1)}, u32[]{:S(2)}, u32[]{:S(2)}) collective-permute-start(bf16[128,128]{1,0:T(8,128)(2,1)S(1)} %fusion), channel_id=1, source_target_pairs={{0,2},{1,3},{2,0},{3,1},{4,6},{5,7},{6,4},{7,5},{8,10},{9,11},{10,... | collective-permute-start | bytes 98312 | tf_op jit(solution)/shard_map/ppermute | solution.py:398
  23.6 0.6 %prepare.1 = (bf16[1024,128]{1,0:T(8,128)(2,1)S(1)}, bf16[128,768]{1,0:T(8,128)(2,1)S(1)}, f32[64,256]{1,0:T(8,128)S(1)}, bf16[48,896]{1,0:T(8,128)(2,1)S(1)}, f32[128,128]{1,0:T(8,128)S(1)}) custom-call(bf16[9,64]{1,0:T(8,128)(2,1)S(1)} %bitcast.13, f32[1,64]{1,0:T(1,128)S(1)} %bitcast.15, f32[1,64]{1,0:T(1,128)S(1)} %bitcast.16, ...), custom_call_target="tpu_custom_call" | custom-call | flops 1000000 | bytes 3000000 | tf_op jit(solution)/shard_map/prepare/pallas_call | solution.py:425
  24.2 0.8 %collective-permute-done.5 = bf16[128,128]{1,0:T(8,128)(2,1)S(1)} collective-permute-done((bf16[128,128]{1,0:T(8,128)(2,1)S(1)}, bf16[128,128]{1,0:T(8,128)(2,1)S(1)}, u32[]{:S(2)}, u32[]{:S(2)}) %collective-permute-start.5) | collective-permute-done | bytes 32800 | tf_op jit(solution)/shard_map/ppermute | solution.py:398
  25.0 0.9 %collective-permute-done.4 = bf16[128,128]{1,0:T(8,128)(2,1)S(1)} collective-permute-done((bf16[128,128]{1,0:T(8,128)(2,1)S(1)}, bf16[128,128]{1,0:T(8,128)(2,1)S(1)}, u32[]{:S(2)}, u32[]{:S(2)}) %collective-permute-start.4) | collective-permute-done | bytes 32800 | tf_op jit(solution)/shard_map/ppermute | solution.py:398
  26.0 3.7 %collective-permute-start.6 = (bf16[128,128]{1,0:T(8,128)(2,1)S(1)}, bf16[128,128]{1,0:T(8,128)(2,1)S(1)}, u32[]{:S(2)}, u32[]{:S(2)}) collective-permute-start(bf16[128,128]{1,0:T(8,128)(2,1)S(1)} %fusion.1._), channel_id=1, source_target_pairs={{0,8},{1,9},{2,10},{3,11},{4,12},{5,13},{6,14},{7,15},{8,0},{9,1},... | collective-permute-start | bytes 98312 | tf_op jit(solution)/shard_map/ppermute | solution.py:398
  29.7 0.9 %broadcast_add_fusion.axial_ref = f32[8,16,256]{2,1,0:T(8,128)S(1)} fusion(f32[8,16,256]{2,1,0:T(8,128)} %get-tuple-element.19, f32[]{:T(128)} %bitcast.10), kind=kLoop, calls=%fused_computation | loop fusion | flops 32768 | bytes 262148 | tf_op jit(solution)/shard_map/add | solution.py:488
  30.6 2.2 %choose.1.chosen_ref = bf16[8192,256]{1,0:T(8,128)(2,1)S(1)} custom-call(s32[1]{0:T(128)S(6)} %copy.17.subset_ref, bf16[128,128]{1,0:T(8,128)(2,1)S(1)} %fusion.1._, bf16[4,8192,256]{2,1,0:T(8,128)(2,1)} %bitcast.18), custom_call_target="tpu_custom_call" | custom-call | bytes 8388608 | tf_op jit(solution)/shard_map/choose/pallas_call | solution.py:478
  32.8 1.5 %back.1 = (f32[8,16,256]{2,1,0:T(8,128)S(1)}, f32[12,64]{1,0:T(8,128)}) custom-call(s32[1]{0:T(128)S(6)} %copy.17.subset_ref, f32[128,128]{1,0:T(8,128)S(1)} %get-tuple-element.14.measured_ref, f32[128,128]{1,0:T(8,128)S(1)} %convert_add_fusion.sinogram_ref, f32[8,16,256]{2,1,0:T(8,128)S(1)} %broadcast_add_fusion.axial_ref, ...), custom_call_target="tpu_custom_call" | custom-call | tf_op jit(solution)/shard_map/back/pallas_call | solution.py:489
  34.3 6.5 %collective-permute-start.8 = (f32[8,3,256]{2,1,0:T(4,128)S(1)}, f32[8,3,256]{2,1,0:T(4,128)S(1)}, u32[]{:S(2)}, u32[]{:S(2)}) collective-permute-start(f32[8,3,256]{2,1,0:T(4,128)S(1)} %get-tuple-element.26), channel_id=1, source_target_pairs={{16,32},{48,64},{80,96},{32,16},{64,48},{96,80},{17,33},{49,65},{8... | collective-permute-start | bytes 73736 | tf_op jit(solution)/shard_map/ppermute | solution.py:392
  40.8 0.1 collective-permute-start.7
  40.9 2.7 %inner.1.inner_ref = f32[8,48,256]{2,1,0:T(8,128)S(1)} custom-call(s32[1]{0:T(128)S(6)} %copy.18.timestep_ref, f32[8,16,256]{2,1,0:T(8,128)S(1)} %get-tuple-element.20.corrected_ref, bf16[1024,128]{1,0:T(8,128)(2,1)S(1)} %get-tuple-element.21.one_ref, bf16[128,768]{1,0:T(8,128)(2,1)S(1)} %get-tuple-element.22.middle_ref, ...), custom_call_target="tpu_custom_call" | custom-call | flops 2000000000 | bytes 2097152 | tf_op jit(solution)/shard_map/inner/pallas_call | solution.py:503
  43.6 0.2 collective-permute-done.8.second_ref
  43.7 1.1 %collective-permute-done.7.first_ref = f32[8,3,256]{2,1,0:T(4,128)S(1)} collective-permute-done((f32[8,3,256]{2,1,0:T(4,128)S(1)}, f32[8,3,256]{2,1,0:T(4,128)S(1)}, u32[]{:S(2)}, u32[]{:S(2)}) %collective-permute-start.7) | collective-permute-done | bytes 24608 | tf_op jit(solution)/shard_map/ppermute | solution.py:389
  44.8 4.2 %coronal.1 = f32[12,8,256]{2,1,0:T(8,128)} custom-call(s32[1]{0:T(128)S(6)} %copy.18.timestep_ref, f32[8,16,256]{2,1,0:T(8,128)S(1)} %get-tuple-element.20.corrected_ref, f32[8,3,256]{2,1,0:T(4,128)S(1)} %collective-permute-done.7.first_ref, f32[8,3,256]{2,1,0:T(4,128)S(1)} %collective-permute-done.8.second_ref, f32[8,48,256]{2,1,0:T(8,128)S(1)} %inner.1.inner_ref, ...), custom_call_target="tpu_custom_call" | custom-call | tf_op jit(solution)/shard_map/coronal/pallas_call | solution.py:513
  (23 shorter events, 0.1 us)
Async XLA Ops:
  0.6 22.9 %copy-start.3 = (bf16[9,1,64]{2,0,1:T(8,128)(2,1)S(1)}, bf16[9,1,64]{2,0,1:T(8,128)(2,1)}, u32[]{:S(2)}) copy-start(bf16[9,1,64]{2,0,1:T(8,128)(2,1)} %param.29) | copy-start | bytes 3460
  0.6 22.9 %copy-start.5 = (f32[64]{0:T(128)S(1)}, f32[64]{0:T(128)}, u32[]{:S(2)}) copy-start(f32[64]{0:T(128)} %param.28) | copy-start | bytes 772
  0.7 22.9 %copy-start = (bf16[9,64,64]{2,1,0:T(8,128)(2,1)S(1)}, bf16[9,64,64]{2,1,0:T(8,128)(2,1)}, u32[]{:S(2)}) copy-start(bf16[9,64,64]{2,1,0:T(8,128)(2,1)} %refs_4_.1) | copy-start | bytes 221188
  0.7 22.9 %copy-start.4 = (f32[64]{0:T(128)S(1)}, f32[64]{0:T(128)}, u32[]{:S(2)}) copy-start(f32[64]{0:T(128)} %param.26) | copy-start | bytes 772
  0.7 22.9 %copy-start.2 = (bf16[9,64,1]{1,0,2:T(8,128)(2,1)S(1)}, bf16[9,64,1]{1,0,2:T(8,128)(2,1)}, u32[]{:S(2)}) copy-start(bf16[9,64,1]{1,0,2:T(8,128)(2,1)} %param.25) | copy-start | bytes 3460
  0.7 22.9 %copy-start.1 = (f32[1024,12]{0,1:T(8,128)S(1)}, f32[1024,12]{0,1:T(8,128)}, u32[]{:S(2)}) copy-start(f32[1024,12]{0,1:T(8,128)} %param.17) | copy-start | bytes 147460
  1.8 5.4 %collective-permute-start.1 = (f32[12,3,256]{2,1,0:T(4,128)S(1)}, f32[12,3,256]{2,1,0:T(4,128)S(1)}, u32[]{:S(2)}, u32[]{:S(2)}) collective-permute-start(f32[12,3,256]{2,1,0:T(4,128)S(1)} %get-tuple-element.28), channel_id=1, source_target_pairs={{1,2},{3,4},{5,6},{7,8},{9,10},{11,12},{13,14},{2,1},{4,3},{6,5},{... | collective-permute-start | bytes 110600 | tf_op jit(solution)/shard_map/ppermute | solution.py:392
  3.9 3.2 %collective-permute-start = (f32[12,3,256]{2,1,0:T(4,128)S(1)}, f32[12,3,256]{2,1,0:T(4,128)S(1)}, u32[]{:S(2)}, u32[]{:S(2)}) collective-permute-start(f32[12,3,256]{2,1,0:T(4,128)S(1)} %get-tuple-element.29), channel_id=1, source_target_pairs={{0,1},{1,0},{2,3},{3,2},{4,5},{5,4},{6,7},{7,6},{8,9},{9,8},{10,11... | collective-permute-start | bytes 110600 | tf_op jit(solution)/shard_map/ppermute | solution.py:389
  7.2 0.6 %copy-start.6 = (f32[12,3,256]{2,1,0:T(4,128)}, f32[12,3,256]{2,1,0:T(4,128)S(1)}, u32[]{:S(2)}) copy-start(f32[12,3,256]{2,1,0:T(4,128)S(1)} %collective-permute-done.1.second_ref) | copy-start | bytes 110596
  7.2 0.6 %copy-start.7 = (f32[12,3,256]{2,1,0:T(4,128)}, f32[12,3,256]{2,1,0:T(4,128)S(1)}, u32[]{:S(2)}) copy-start(f32[12,3,256]{2,1,0:T(4,128)S(1)} %collective-permute-done.first_ref) | copy-start | bytes 110596
  17.7 2.3 %collective-permute-start.2 = (bf16[128,128]{1,0:T(8,128)(2,1)}, bf16[128,128]{1,0:T(8,128)(2,1)S(1)}, u32[]{:S(2)}, u32[]{:S(2)}) collective-permute-start(bf16[128,128]{1,0:T(8,128)(2,1)} %get-tuple-element.16), channel_id=1, source_target_pairs={{0,1},{1,0},{2,3},{3,2},{4,5},{5,4},{6,7},{7,6},{8,9},{9,8},{10,11... | collective-permute-start | bytes 98312 | tf_op jit(solution)/shard_map/ppermute | solution.py:398
  20.0 5.0 %collective-permute-start.5 = (bf16[128,128]{1,0:T(8,128)(2,1)S(1)}, bf16[128,128]{1,0:T(8,128)(2,1)S(1)}, u32[]{:S(2)}, u32[]{:S(2)}) collective-permute-start(bf16[128,128]{1,0:T(8,128)(2,1)S(1)} %fusion), channel_id=1, source_target_pairs={{0,6},{1,7},{2,4},{3,5},{4,2},{5,3},{6,0},{7,1},{8,14},{9,15},{10,... | collective-permute-start | bytes 98312 | tf_op jit(solution)/shard_map/ppermute | solution.py:398
  22.0 3.9 %collective-permute-start.4 = (bf16[128,128]{1,0:T(8,128)(2,1)S(1)}, bf16[128,128]{1,0:T(8,128)(2,1)S(1)}, u32[]{:S(2)}, u32[]{:S(2)}) collective-permute-start(bf16[128,128]{1,0:T(8,128)(2,1)S(1)} %fusion), channel_id=1, source_target_pairs={{0,4},{1,5},{2,6},{3,7},{4,0},{5,1},{6,2},{7,3},{8,12},{9,13},{10,... | collective-permute-start | bytes 98312 | tf_op jit(solution)/shard_map/ppermute | solution.py:398
  22.0 3.9 %collective-permute-start.3 = (bf16[128,128]{1,0:T(8,128)(2,1)S(1)}, bf16[128,128]{1,0:T(8,128)(2,1)S(1)}, u32[]{:S(2)}, u32[]{:S(2)}) collective-permute-start(bf16[128,128]{1,0:T(8,128)(2,1)S(1)} %fusion), channel_id=1, source_target_pairs={{0,2},{1,3},{2,0},{3,1},{4,6},{5,7},{6,4},{7,5},{8,10},{9,11},{10,... | collective-permute-start | bytes 98312 | tf_op jit(solution)/shard_map/ppermute | solution.py:398
  26.0 6.8 %collective-permute-start.6 = (bf16[128,128]{1,0:T(8,128)(2,1)S(1)}, bf16[128,128]{1,0:T(8,128)(2,1)S(1)}, u32[]{:S(2)}, u32[]{:S(2)}) collective-permute-start(bf16[128,128]{1,0:T(8,128)(2,1)S(1)} %fusion.1._), channel_id=1, source_target_pairs={{0,8},{1,9},{2,10},{3,11},{4,12},{5,13},{6,14},{7,15},{8,0},{9,1},... | collective-permute-start | bytes 98312 | tf_op jit(solution)/shard_map/ppermute | solution.py:398
  34.3 9.4 %collective-permute-start.8 = (f32[8,3,256]{2,1,0:T(4,128)S(1)}, f32[8,3,256]{2,1,0:T(4,128)S(1)}, u32[]{:S(2)}, u32[]{:S(2)}) collective-permute-start(f32[8,3,256]{2,1,0:T(4,128)S(1)} %get-tuple-element.26), channel_id=1, source_target_pairs={{16,32},{48,64},{80,96},{32,16},{64,48},{96,80},{17,33},{49,65},{8... | collective-permute-start | bytes 73736 | tf_op jit(solution)/shard_map/ppermute | solution.py:392
  40.8 4.0 %collective-permute-start.7 = (f32[8,3,256]{2,1,0:T(4,128)S(1)}, f32[8,3,256]{2,1,0:T(4,128)S(1)}, u32[]{:S(2)}, u32[]{:S(2)}) collective-permute-start(f32[8,3,256]{2,1,0:T(4,128)S(1)} %get-tuple-element.27), channel_id=1, source_target_pairs={{0,16},{16,0},{32,48},{48,32},{64,80},{80,64},{96,112},{112,96},{1... | collective-permute-start | bytes 73736 | tf_op jit(solution)/shard_map/ppermute | solution.py:389

commit v5 on v4

--- a/solution.py
+++ b/solution.py
@@ -9,7 +9,8 @@
 SIGMA_STEP = 0.002
 RELAX_TOP = 4.0
 HALO = 3
-PLANES = 4
+AXIAL_PLANES = 6
+CORONAL_PLANES = 8
 BF = jnp.bfloat16
 F32 = jnp.float32
 AXIAL = (8, 8, 11, 14, 16)
@@ -178,19 +179,19 @@
 
 def networks(entries, own, weights, scratch):
     one_ref, middle_ref, bias_ref, last_ref = weights
-    taps, hidden = scratch[0:PLANES], scratch[PLANES : 2 * PLANES]
-    for k in range(PLANES):
+    taps, hidden = scratch[0:AXIAL_PLANES], scratch[AXIAL_PLANES : 2 * AXIAL_PLANES]
+    for k in range(AXIAL_PLANES):
         layer_one(spread_entry(*entries[k]), range(own + 4), one_ref, taps[k])
-    for k in range(PLANES):
+    for k in range(AXIAL_PLANES):
         layer_two(range(0, own + 2, 2), middle_ref, bias_ref, taps[k], hidden[k])
-    last = [jnp.dot(last_ref[...], hidden[k][...], preferred_element_type=F32) for k in range(PLANES)]
-    return [layer_three(-(-own // 8) * 8, last[k]) for k in range(PLANES)]
+    last = [jnp.dot(last_ref[...], hidden[k][...], preferred_element_type=F32) for k in range(AXIAL_PLANES)]
+    return [layer_three(-(-own // 8) * 8, last[k]) for k in range(AXIAL_PLANES)]
 
 
 def network_scratch(own):
-    return [pltpu.VMEM(((own + 4) * 192, 256), BF)] * PLANES + [
+    return [pltpu.VMEM(((own + 4) * 192, 256), BF)] * AXIAL_PLANES + [
         pltpu.VMEM(((own + 2) * 64, 256), BF)
-    ] * PLANES
+    ] * AXIAL_PLANES
 
 
 def axial_kernel(
@@ -223,18 +224,18 @@
 
     def planes(step, carry):
         entries = []
-        for k in range(PLANES):
-            p = step * PLANES + k
+        for k in range(AXIAL_PLANES):
+            p = step * AXIAL_PLANES + k
             entries.append((volume_ref[p] * scale_in, first_ref[p] * scale_in, second_ref[p] * scale_in))
         nets = networks(entries, 8, weights, scratch)
-        for k in range(PLANES):
-            p = step * PLANES + k
+        for k in range(AXIAL_PLANES):
+            p = step * AXIAL_PLANES + k
             value = volume_ref[p] + scale_out * nets[k]
             for y in range(8):
                 axial_ref[y, pl.ds(p, 1), :] = value[y : y + 1, :]
         return carry
 
-    lax.fori_loop(0, 12 // PLANES, planes, 0)
+    lax.fori_loop(0, 12 // AXIAL_PLANES, planes, 0)
     copy.wait()
     flat = axial_ref[...].reshape(128, 256).astype(BF)
     lane = lax.broadcasted_iota(jnp.int32, (16, 256), 1) % 8
@@ -299,23 +300,23 @@
 def inner_kernel(
     timestep_ref, corrected_ref, one_ref, middle_ref, bias_ref, last_ref, inner_ref, *scratch
 ):
-    taps, hidden = scratch[0:PLANES], scratch[PLANES:]
+    taps, hidden = scratch[0:CORONAL_PLANES], scratch[CORONAL_PLANES:]
     scale_in, _ = noise_scales(timestep_ref)
     absent = jnp.zeros((HALO, 256), F32)
 
     def planes(step, carry):
-        for k in range(PLANES):
-            entry = corrected_ref[step * PLANES + k] * scale_in
+        for k in range(CORONAL_PLANES):
+            entry = corrected_ref[step * CORONAL_PLANES + k] * scale_in
             layer_one(spread_entry(entry, absent, absent), range(4, 12), one_ref, taps[k])
-        for k in range(PLANES):
+        for k in range(CORONAL_PLANES):
             layer_two((4, 6, 8), middle_ref, bias_ref, taps[k], hidden[k], 4)
-        for k in range(PLANES):
-            inner_ref[step * PLANES + k] = jnp.dot(
+        for k in range(CORONAL_PLANES):
+            inner_ref[step * CORONAL_PLANES + k] = jnp.dot(
                 last_ref[:, 256:640], hidden[k][...], preferred_element_type=F32
             )
         return carry
 
-    lax.fori_loop(0, 8 // PLANES, planes, 0)
+    lax.fori_loop(0, 8 // CORONAL_PLANES, planes, 0)
 
 
 def coronal_kernel(
@@ -332,19 +333,19 @@
     *scratch,
 ):
     scale_in, scale_out = noise_scales(timestep_ref)
-    taps, low, high = scratch[0:PLANES], scratch[PLANES : 2 * PLANES], scratch[2 * PLANES :]
+    taps, low, high = scratch[0:CORONAL_PLANES], scratch[CORONAL_PLANES : 2 * CORONAL_PLANES], scratch[2 * CORONAL_PLANES :]
     edges = (*range(0, 6), *range(10, 16))
 
     def planes(step, carry):
-        for k in range(PLANES):
-            p = step * PLANES + k
+        for k in range(CORONAL_PLANES):
+            p = step * CORONAL_PLANES + k
             rows = [ref[p] * scale_in for ref in (corrected_ref, first_ref, second_ref)]
             layer_one(spread_entry(*rows), edges, one_ref, taps[k])
-        for k in range(PLANES):
+        for k in range(CORONAL_PLANES):
             layer_two((0, 2), middle_ref, bias_ref, taps[k], low[k])
             layer_two((10, 12), middle_ref, bias_ref, taps[k], high[k], 10)
-        for k in range(PLANES):
-            p = step * PLANES + k
+        for k in range(CORONAL_PLANES):
+            p = step * CORONAL_PLANES + k
             last = inner_ref[p]
             last = last + jnp.dot(last_ref[:, 0:256], low[k][...], preferred_element_type=F32)
             last = last + jnp.dot(last_ref[:, 640:896], high[k][...], preferred_element_type=F32)
@@ -353,7 +354,7 @@
                 restored_ref[z, pl.ds(p, 1), :] = value[z : z + 1, :]
         return carry
 
-    lax.fori_loop(0, 8 // PLANES, planes, 0)
+    lax.fori_loop(0, 8 // CORONAL_PLANES, planes, 0)
 
 
 def vmem():
@@ -499,14 +500,14 @@
         compiler_params=params(40),
     )(subset, turned, sinogram, axial, chosen)
     first, second = exchange(corrected[:, :HALO], corrected[:, 12 - HALO : 12], "gz", False)
-    taps_scratch = [pltpu.VMEM((16 * 192, 256), BF)] * PLANES
+    taps_scratch = [pltpu.VMEM((16 * 192, 256), BF)] * CORONAL_PLANES
     inner = pl.pallas_call(
         inner_kernel,
         name="inner",
         out_shape=jax.ShapeDtypeStruct((8, 48, 256), F32),
         in_specs=[smem()] + [vmem()] * 5,
         out_specs=vmem(),
-        scratch_shapes=taps_scratch + [pltpu.VMEM((6 * 64, 256), BF)] * PLANES,
+        scratch_shapes=taps_scratch + [pltpu.VMEM((6 * 64, 256), BF)] * CORONAL_PLANES,
         compiler_params=params(40),
         cost_estimate=pl.CostEstimate(flops=2000000000, bytes_accessed=2 << 20, transcendentals=0),
     )(timestep, corrected, *coronal_weights)
@@ -516,7 +517,7 @@
         out_shape=jax.ShapeDtypeStruct((12, 8, 256), F32),
         in_specs=[smem()] + [vmem()] * 8,
         out_specs=vmem(),
-        scratch_shapes=taps_scratch + [pltpu.VMEM((256, 256), BF)] * (2 * PLANES),
+        scratch_shapes=taps_scratch + [pltpu.VMEM((256, 256), BF)] * (2 * CORONAL_PLANES),
         compiler_params=params(40),
     )(timestep, corrected, first, second, inner, *coronal_weights)
     return (restored, residual.T)

time: 49.3 us -> 48.8 us (0.990)
  Pallas kernels: 20.9 us -> 20 us
where the time goes in v5:
time: 48.8 us; the launch traced here: 48.5 us
  Pallas kernels  20 us (41%)
  starting transfers between devices  19.2 us (39%)
  waiting for transfers between devices  3.71 us (8%)
  other arithmetic  2.89 us (6%)
  between operations  2.11 us (4%)
  local copies, waits for them, and re-layouts  0.65 us (1%)
    pallas_call x1, Pallas kernels, per_device(): pl.pallas_call(axial_kernel, name='axial', out_shape=(jax.ShapeDtypeStruc...  9.57 us
    ppermute x2, starting transfers between devices, exchange(): second = lax.ppermute(outer, axis, outer_pairs(size))  8.67 us
    ppermute x5, starting transfers between devices, partner(): lax.ppermute(value, 'gy', [(i, i ^ bits) for i in range(16)]).astype(F32)  8.52 us
    pallas_call x1, Pallas kernels, per_device(): pl.pallas_call(coronal_kernel, name='coronal', out_shape=jax.ShapeDtypeSt...  3.83 us
    pallas_call x1, Pallas kernels, per_device(): pl.pallas_call(inner_kernel, name='inner', out_shape=jax.ShapeDtypeStruct...  2.29 us
    pallas_call x1, Pallas kernels, per_device(): pl.pallas_call(choose_kernel, name='choose', out_shape=jax.ShapeDtypeStru...  2.21 us
    ppermute x2, starting transfers between devices, exchange(): first = lax.ppermute(inner, axis, inner_pairs(size))  2.03 us
    ppermute x5, waiting for transfers between devices, partner(): lax.ppermute(value, 'gy', [(i, i ^ bits) for i in range(16)]).astype(F32)  1.94 us
  transfers between devices with their start and end apart: 9, of which 6 were waited for; matrix products, arithmetic and copies ran while one was open for 4% of the time, Pallas kernels for 11%

profile of v5, /device:TPU:6, one launch (start us, length us, event | category | flops | bytes accessed | tf_op | source)
XLA Modules:
  0.0 48.5 jit_solution(6018729130588737554)
XLA Ops:
  0.7 1.1 %slice_select_fusion = (f32[12,3,256]{2,1,0:T(4,128)S(1)}, f32[12,3,256]{2,1,0:T(4,128)S(1)}) fusion(f32[12,8,256]{2,1,0:T(8,128)} %volume_ref.1, pred[]{:T(512)S(6)} %eq.9), kind=kLoop, calls=%fused_computation.5 | loop fusion | flops 18432 | bytes 147457 | tf_op jit(solution)/shard_map/jit(_where)/select_n | solution.py:389
  1.8 2.2 %collective-permute-start.1 = (f32[12,3,256]{2,1,0:T(4,128)S(1)}, f32[12,3,256]{2,1,0:T(4,128)S(1)}, u32[]{:S(2)}, u32[]{:S(2)}) collective-permute-start(f32[12,3,256]{2,1,0:T(4,128)S(1)} %get-tuple-element.28), channel_id=1, source_target_pairs={{1,2},{3,4},{5,6},{7,8},{9,10},{11,12},{13,14},{2,1},{4,3},{6,5},{... | collective-permute-start | bytes 110600 | tf_op jit(solution)/shard_map/ppermute | solution.py:393
  3.9 1.8 %collective-permute-start = (f32[12,3,256]{2,1,0:T(4,128)S(1)}, f32[12,3,256]{2,1,0:T(4,128)S(1)}, u32[]{:S(2)}, u32[]{:S(2)}) collective-permute-start(f32[12,3,256]{2,1,0:T(4,128)S(1)} %get-tuple-element.29), channel_id=1, source_target_pairs={{0,1},{1,0},{2,3},{3,2},{4,5},{5,4},{6,7},{7,6},{8,9},{9,8},{10,11... | collective-permute-start | bytes 110600 | tf_op jit(solution)/shard_map/ppermute | solution.py:390
  7.0 0.2 collective-permute-done.1.second_ref
  7.2 0.6 %copy-done.6 = f32[12,3,256]{2,1,0:T(4,128)} copy-done((f32[12,3,256]{2,1,0:T(4,128)}, f32[12,3,256]{2,1,0:T(4,128)S(1)}, u32[]{:S(2)}) %copy-start.6) | copy-done | bytes 36888
  7.8 9.6 %axial.1 = (f32[8,16,256]{2,1,0:T(8,128)}, f32[128,128]{1,0:T(8,128)}, bf16[128,128]{1,0:T(8,128)(2,1)}) custom-call(s32[1]{0:T(128)S(6)} %copy.17.subset_ref, s32[1]{0:T(128)S(6)} %copy.18.timestep_ref, f32[12,8,256]{2,1,0:T(8,128)} %volume_ref.1, f32[12,3,256]{2,1,0:T(4,128)} %copy-done.7, f32[12,3,256]{2,1,0:T(4,128)} %copy-done.6, ...), custom_call_target="tpu_custom_call" | custom-call | tf_op jit(solution)/shard_map/axial/pallas_call | solution.py:445
  17.4 1.2 %collective-permute-start.2 = (bf16[128,128]{1,0:T(8,128)(2,1)}, bf16[128,128]{1,0:T(8,128)(2,1)S(1)}, u32[]{:S(2)}, u32[]{:S(2)}) collective-permute-start(bf16[128,128]{1,0:T(8,128)(2,1)} %get-tuple-element.16), channel_id=1, source_target_pairs={{0,1},{1,0},{2,3},{3,2},{4,5},{5,4},{6,7},{7,6},{8,9},{9,8},{10,11... | collective-permute-start | bytes 98312 | tf_op jit(solution)/shard_map/ppermute | solution.py:399
  18.6 0.8 %broadcast_add_fusion.1 = f32[128,128]{1,0:T(8,128)S(1)} fusion(f32[128,128]{1,0:T(8,128)} %get-tuple-element.15, f32[]{:T(128)} %bitcast.10), kind=kLoop, calls=%fused_computation.7 | loop fusion | flops 16384 | bytes 131076 | tf_op jit(solution)/shard_map/add | solution.py:477
  19.5 0.2 collective-permute-done.2
  19.7 2.0 %collective-permute-start.5 = (bf16[128,128]{1,0:T(8,128)(2,1)S(1)}, bf16[128,128]{1,0:T(8,128)(2,1)S(1)}, u32[]{:S(2)}, u32[]{:S(2)}) collective-permute-start(bf16[128,128]{1,0:T(8,128)(2,1)S(1)} %fusion), channel_id=1, source_target_pairs={{0,6},{1,7},{2,4},{3,5},{4,2},{5,3},{6,0},{7,1},{8,14},{9,15},{10,... | collective-permute-start | bytes 98312 | tf_op jit(solution)/shard_map/ppermute | solution.py:399
  21.7 1.5 %collective-permute-start.3 = (bf16[128,128]{1,0:T(8,128)(2,1)S(1)}, bf16[128,128]{1,0:T(8,128)(2,1)S(1)}, u32[]{:S(2)}, u32[]{:S(2)}) collective-permute-start(bf16[128,128]{1,0:T(8,128)(2,1)S(1)} %fusion), channel_id=1, source_target_pairs={{0,2},{1,3},{2,0},{3,1},{4,6},{5,7},{6,4},{7,5},{8,10},{9,11},{10,... | collective-permute-start | bytes 98312 | tf_op jit(solution)/shard_map/ppermute | solution.py:399
  23.3 0.6 %prepare.1 = (bf16[1024,128]{1,0:T(8,128)(2,1)S(1)}, bf16[128,768]{1,0:T(8,128)(2,1)S(1)}, f32[64,256]{1,0:T(8,128)S(1)}, bf16[48,896]{1,0:T(8,128)(2,1)S(1)}, f32[128,128]{1,0:T(8,128)S(1)}) custom-call(bf16[9,64]{1,0:T(8,128)(2,1)S(1)} %bitcast.13, f32[1,64]{1,0:T(1,128)S(1)} %bitcast.15, f32[1,64]{1,0:T(1,128)S(1)} %bitcast.16, ...), custom_call_target="tpu_custom_call" | custom-call | flops 1000000 | bytes 3000000 | tf_op jit(solution)/shard_map/prepare/pallas_call | solution.py:426
  23.9 0.8 %collective-permute-done.5 = bf16[128,128]{1,0:T(8,128)(2,1)S(1)} collective-permute-done((bf16[128,128]{1,0:T(8,128)(2,1)S(1)}, bf16[128,128]{1,0:T(8,128)(2,1)S(1)}, u32[]{:S(2)}, u32[]{:S(2)}) %collective-permute-start.5) | collective-permute-done | bytes 32800 | tf_op jit(solution)/shard_map/ppermute | solution.py:399
  24.7 0.9 %collective-permute-done.4 = bf16[128,128]{1,0:T(8,128)(2,1)S(1)} collective-permute-done((bf16[128,128]{1,0:T(8,128)(2,1)S(1)}, bf16[128,128]{1,0:T(8,128)(2,1)S(1)}, u32[]{:S(2)}, u32[]{:S(2)}) %collective-permute-start.4) | collective-permute-done | bytes 32800 | tf_op jit(solution)/shard_map/ppermute | solution.py:399
  25.7 3.7 %collective-permute-start.6 = (bf16[128,128]{1,0:T(8,128)(2,1)S(1)}, bf16[128,128]{1,0:T(8,128)(2,1)S(1)}, u32[]{:S(2)}, u32[]{:S(2)}) collective-permute-start(bf16[128,128]{1,0:T(8,128)(2,1)S(1)} %fusion.1._), channel_id=1, source_target_pairs={{0,8},{1,9},{2,10},{3,11},{4,12},{5,13},{6,14},{7,15},{8,0},{9,1},... | collective-permute-start | bytes 98312 | tf_op jit(solution)/shard_map/ppermute | solution.py:399
  29.4 0.9 %broadcast_add_fusion.axial_ref = f32[8,16,256]{2,1,0:T(8,128)S(1)} fusion(f32[8,16,256]{2,1,0:T(8,128)} %get-tuple-element.19, f32[]{:T(128)} %bitcast.10), kind=kLoop, calls=%fused_computation | loop fusion | flops 32768 | bytes 262148 | tf_op jit(solution)/shard_map/add | solution.py:489
  30.3 2.2 %choose.1.chosen_ref = bf16[8192,256]{1,0:T(8,128)(2,1)S(1)} custom-call(s32[1]{0:T(128)S(6)} %copy.17.subset_ref, bf16[128,128]{1,0:T(8,128)(2,1)S(1)} %fusion.1._, bf16[4,8192,256]{2,1,0:T(8,128)(2,1)} %bitcast.18), custom_call_target="tpu_custom_call" | custom-call | bytes 8388608 | tf_op jit(solution)/shard_map/choose/pallas_call | solution.py:479
  32.6 1.5 %back.1 = (f32[8,16,256]{2,1,0:T(8,128)S(1)}, f32[12,64]{1,0:T(8,128)}) custom-call(s32[1]{0:T(128)S(6)} %copy.17.subset_ref, f32[128,128]{1,0:T(8,128)S(1)} %get-tuple-element.14.measured_ref, f32[128,128]{1,0:T(8,128)S(1)} %convert_add_fusion.sinogram_ref, f32[8,16,256]{2,1,0:T(8,128)S(1)} %broadcast_add_fusion.axial_ref, ...), custom_call_target="tpu_custom_call" | custom-call | tf_op jit(solution)/shard_map/back/pallas_call | solution.py:490
  34.0 6.5 %collective-permute-start.8 = (f32[8,3,256]{2,1,0:T(4,128)S(1)}, f32[8,3,256]{2,1,0:T(4,128)S(1)}, u32[]{:S(2)}, u32[]{:S(2)}) collective-permute-start(f32[8,3,256]{2,1,0:T(4,128)S(1)} %get-tuple-element.26), channel_id=1, source_target_pairs={{16,32},{48,64},{80,96},{32,16},{64,48},{96,80},{17,33},{49,65},{8... | collective-permute-start | bytes 73736 | tf_op jit(solution)/shard_map/ppermute | solution.py:393
  40.5 0.3 collective-permute-start.7
  40.8 2.3 %inner.1.inner_ref = f32[8,48,256]{2,1,0:T(8,128)S(1)} custom-call(s32[1]{0:T(128)S(6)} %copy.18.timestep_ref, f32[8,16,256]{2,1,0:T(8,128)S(1)} %get-tuple-element.20.corrected_ref, bf16[1024,128]{1,0:T(8,128)(2,1)S(1)} %get-tuple-element.21.one_ref, bf16[128,768]{1,0:T(8,128)(2,1)S(1)} %get-tuple-element.22.middle_ref, ...), custom_call_target="tpu_custom_call" | custom-call | flops 2000000000 | bytes 2097152 | tf_op jit(solution)/shard_map/inner/pallas_call | solution.py:504
  43.1 0.3 collective-permute-done.8.second_ref
  43.4 1.3 %collective-permute-done.7.first_ref = f32[8,3,256]{2,1,0:T(4,128)S(1)} collective-permute-done((f32[8,3,256]{2,1,0:T(4,128)S(1)}, f32[8,3,256]{2,1,0:T(4,128)S(1)}, u32[]{:S(2)}, u32[]{:S(2)}) %collective-permute-start.7) | collective-permute-done | bytes 24608 | tf_op jit(solution)/shard_map/ppermute | solution.py:390
  44.7 3.8 %coronal.1 = f32[12,8,256]{2,1,0:T(8,128)} custom-call(s32[1]{0:T(128)S(6)} %copy.18.timestep_ref, f32[8,16,256]{2,1,0:T(8,128)S(1)} %get-tuple-element.20.corrected_ref, f32[8,3,256]{2,1,0:T(4,128)S(1)} %collective-permute-done.7.first_ref, f32[8,3,256]{2,1,0:T(4,128)S(1)} %collective-permute-done.8.second_ref, f32[8,48,256]{2,1,0:T(8,128)S(1)} %inner.1.inner_ref, ...), custom_call_target="tpu_custom_call" | custom-call | tf_op jit(solution)/shard_map/coronal/pallas_call | solution.py:514
  (23 shorter events, 0.1 us)
Async XLA Ops:
  0.6 22.6 %copy-start.3 = (bf16[9,1,64]{2,0,1:T(8,128)(2,1)S(1)}, bf16[9,1,64]{2,0,1:T(8,128)(2,1)}, u32[]{:S(2)}) copy-start(bf16[9,1,64]{2,0,1:T(8,128)(2,1)} %param.29) | copy-start | bytes 3460
  0.6 22.6 %copy-start.5 = (f32[64]{0:T(128)S(1)}, f32[64]{0:T(128)}, u32[]{:S(2)}) copy-start(f32[64]{0:T(128)} %param.28) | copy-start | bytes 772
  0.7 22.6 %copy-start = (bf16[9,64,64]{2,1,0:T(8,128)(2,1)S(1)}, bf16[9,64,64]{2,1,0:T(8,128)(2,1)}, u32[]{:S(2)}) copy-start(bf16[9,64,64]{2,1,0:T(8,128)(2,1)} %refs_4_.1) | copy-start | bytes 221188
  0.7 22.6 %copy-start.4 = (f32[64]{0:T(128)S(1)}, f32[64]{0:T(128)}, u32[]{:S(2)}) copy-start(f32[64]{0:T(128)} %param.26) | copy-start | bytes 772
  0.7 22.6 %copy-start.2 = (bf16[9,64,1]{1,0,2:T(8,128)(2,1)S(1)}, bf16[9,64,1]{1,0,2:T(8,128)(2,1)}, u32[]{:S(2)}) copy-start(bf16[9,64,1]{1,0,2:T(8,128)(2,1)} %param.25) | copy-start | bytes 3460
  0.7 22.6 %copy-start.1 = (f32[1024,12]{0,1:T(8,128)S(1)}, f32[1024,12]{0,1:T(8,128)}, u32[]{:S(2)}) copy-start(f32[1024,12]{0,1:T(8,128)} %param.17) | copy-start | bytes 147460
  1.8 5.4 %collective-permute-start.1 = (f32[12,3,256]{2,1,0:T(4,128)S(1)}, f32[12,3,256]{2,1,0:T(4,128)S(1)}, u32[]{:S(2)}, u32[]{:S(2)}) collective-permute-start(f32[12,3,256]{2,1,0:T(4,128)S(1)} %get-tuple-element.28), channel_id=1, source_target_pairs={{1,2},{3,4},{5,6},{7,8},{9,10},{11,12},{13,14},{2,1},{4,3},{6,5},{... | collective-permute-start | bytes 110600 | tf_op jit(solution)/shard_map/ppermute | solution.py:393
  3.9 3.2 %collective-permute-start = (f32[12,3,256]{2,1,0:T(4,128)S(1)}, f32[12,3,256]{2,1,0:T(4,128)S(1)}, u32[]{:S(2)}, u32[]{:S(2)}) collective-permute-start(f32[12,3,256]{2,1,0:T(4,128)S(1)} %get-tuple-element.29), channel_id=1, source_target_pairs={{0,1},{1,0},{2,3},{3,2},{4,5},{5,4},{6,7},{7,6},{8,9},{9,8},{10,11... | collective-permute-start | bytes 110600 | tf_op jit(solution)/shard_map/ppermute | solution.py:390
  7.2 0.6 %copy-start.6 = (f32[12,3,256]{2,1,0:T(4,128)}, f32[12,3,256]{2,1,0:T(4,128)S(1)}, u32[]{:S(2)}) copy-start(f32[12,3,256]{2,1,0:T(4,128)S(1)} %collective-permute-done.1.second_ref) | copy-start | bytes 110596
  7.2 0.6 %copy-start.7 = (f32[12,3,256]{2,1,0:T(4,128)}, f32[12,3,256]{2,1,0:T(4,128)S(1)}, u32[]{:S(2)}) copy-start(f32[12,3,256]{2,1,0:T(4,128)S(1)} %collective-permute-done.first_ref) | copy-start | bytes 110596
  17.4 2.3 %collective-permute-start.2 = (bf16[128,128]{1,0:T(8,128)(2,1)}, bf16[128,128]{1,0:T(8,128)(2,1)S(1)}, u32[]{:S(2)}, u32[]{:S(2)}) collective-permute-start(bf16[128,128]{1,0:T(8,128)(2,1)} %get-tuple-element.16), channel_id=1, source_target_pairs={{0,1},{1,0},{2,3},{3,2},{4,5},{5,4},{6,7},{7,6},{8,9},{9,8},{10,11... | collective-permute-start | bytes 98312 | tf_op jit(solution)/shard_map/ppermute | solution.py:399
  19.7 5.0 %collective-permute-start.5 = (bf16[128,128]{1,0:T(8,128)(2,1)S(1)}, bf16[128,128]{1,0:T(8,128)(2,1)S(1)}, u32[]{:S(2)}, u32[]{:S(2)}) collective-permute-start(bf16[128,128]{1,0:T(8,128)(2,1)S(1)} %fusion), channel_id=1, source_target_pairs={{0,6},{1,7},{2,4},{3,5},{4,2},{5,3},{6,0},{7,1},{8,14},{9,15},{10,... | collective-permute-start | bytes 98312 | tf_op jit(solution)/shard_map/ppermute | solution.py:399
  21.7 3.9 %collective-permute-start.4 = (bf16[128,128]{1,0:T(8,128)(2,1)S(1)}, bf16[128,128]{1,0:T(8,128)(2,1)S(1)}, u32[]{:S(2)}, u32[]{:S(2)}) collective-permute-start(bf16[128,128]{1,0:T(8,128)(2,1)S(1)} %fusion), channel_id=1, source_target_pairs={{0,4},{1,5},{2,6},{3,7},{4,0},{5,1},{6,2},{7,3},{8,12},{9,13},{10,... | collective-permute-start | bytes 98312 | tf_op jit(solution)/shard_map/ppermute | solution.py:399
  21.7 3.9 %collective-permute-start.3 = (bf16[128,128]{1,0:T(8,128)(2,1)S(1)}, bf16[128,128]{1,0:T(8,128)(2,1)S(1)}, u32[]{:S(2)}, u32[]{:S(2)}) collective-permute-start(bf16[128,128]{1,0:T(8,128)(2,1)S(1)} %fusion), channel_id=1, source_target_pairs={{0,2},{1,3},{2,0},{3,1},{4,6},{5,7},{6,4},{7,5},{8,10},{9,11},{10,... | collective-permute-start | bytes 98312 | tf_op jit(solution)/shard_map/ppermute | solution.py:399
  25.7 6.9 %collective-permute-start.6 = (bf16[128,128]{1,0:T(8,128)(2,1)S(1)}, bf16[128,128]{1,0:T(8,128)(2,1)S(1)}, u32[]{:S(2)}, u32[]{:S(2)}) collective-permute-start(bf16[128,128]{1,0:T(8,128)(2,1)S(1)} %fusion.1._), channel_id=1, source_target_pairs={{0,8},{1,9},{2,10},{3,11},{4,12},{5,13},{6,14},{7,15},{8,0},{9,1},... | collective-permute-start | bytes 98312 | tf_op jit(solution)/shard_map/ppermute | solution.py:399
  34.0 9.4 %collective-permute-start.8 = (f32[8,3,256]{2,1,0:T(4,128)S(1)}, f32[8,3,256]{2,1,0:T(4,128)S(1)}, u32[]{:S(2)}, u32[]{:S(2)}) collective-permute-start(f32[8,3,256]{2,1,0:T(4,128)S(1)} %get-tuple-element.26), channel_id=1, source_target_pairs={{16,32},{48,64},{80,96},{32,16},{64,48},{96,80},{17,33},{49,65},{8... | collective-permute-start | bytes 73736 | tf_op jit(solution)/shard_map/ppermute | solution.py:393
  40.5 4.2 %collective-permute-start.7 = (f32[8,3,256]{2,1,0:T(4,128)S(1)}, f32[8,3,256]{2,1,0:T(4,128)S(1)}, u32[]{:S(2)}, u32[]{:S(2)}) collective-permute-start(f32[8,3,256]{2,1,0:T(4,128)S(1)} %get-tuple-element.27), channel_id=1, source_target_pairs={{0,16},{16,0},{32,48},{48,32},{64,80},{80,64},{96,112},{112,96},{1... | collective-permute-start | bytes 73736 | tf_op jit(solution)/shard_map/ppermute | solution.py:390

commit v6 on v5

--- a/solution.py
+++ b/solution.py
@@ -262,10 +262,15 @@
     sent_ref[...] = partial.astype(BF)
 
 
-def choose_kernel(subset_ref, _, projector_ref, chosen_ref, sem):
-    copy = pltpu.make_async_copy(projector_ref.at[subset_ref[0] % SUBSETS], chosen_ref, sem)
-    copy.start()
-    copy.wait()
+def choose_kernel(subset_ref, _, projector_ref, chosen_ref, sems):
+    copies = []
+    for part in range(8):
+        rows = pl.ds(part * 1024, 1024)
+        source = projector_ref.at[subset_ref[0] % SUBSETS, rows]
+        copies.append(pltpu.make_async_copy(source, chosen_ref.at[rows], sems.at[part]))
+        copies[-1].start()
+    for copy in copies:
+        copy.wait()
 
 
 def back_kernel(
@@ -482,7 +487,7 @@
         out_shape=jax.ShapeDtypeStruct((8192, 256), BF),
         in_specs=[smem(), vmem(), hbm()],
         out_specs=vmem(),
-        scratch_shapes=[pltpu.SemaphoreType.DMA],
+        scratch_shapes=[pltpu.SemaphoreType.DMA((8,))],
         compiler_params=params(46),
         cost_estimate=pl.CostEstimate(flops=0, bytes_accessed=8 << 20, transcendentals=0),
     )(subset, sent, flat_projector)

time: 48.8 us -> 48.8 us (level)
  no operation moved by 1% of the time
where the time goes in v6:
time: 48.8 us; the launch traced here: 48.5 us
  Pallas kernels  20 us (41%)
  starting transfers between devices  19.2 us (39%)
  waiting for transfers between devices  3.71 us (8%)
  other arithmetic  2.89 us (6%)
  between operations  2.11 us (4%)
  local copies, waits for them, and re-layouts  0.65 us (1%)
    pallas_call x1, Pallas kernels, per_device(): pl.pallas_call(axial_kernel, name='axial', out_shape=(jax.ShapeDtypeStruc...  9.57 us
    ppermute x2, starting transfers between devices, exchange(): second = lax.ppermute(outer, axis, outer_pairs(size))  8.67 us
    ppermute x5, starting transfers between devices, partner(): lax.ppermute(value, 'gy', [(i, i ^ bits) for i in range(16)]).astype(F32)  8.52 us
    pallas_call x1, Pallas kernels, per_device(): pl.pallas_call(coronal_kernel, name='coronal', out_shape=jax.ShapeDtypeSt...  3.82 us
    pallas_call x1, Pallas kernels, per_device(): pl.pallas_call(inner_kernel, name='inner', out_shape=jax.ShapeDtypeStruct...  2.29 us
    pallas_call x1, Pallas kernels, per_device(): pl.pallas_call(choose_kernel, name='choose', out_shape=jax.ShapeDtypeStru...  2.22 us
    ppermute x2, starting transfers between devices, exchange(): first = lax.ppermute(inner, axis, inner_pairs(size))  2.03 us
    ppermute x5, waiting for transfers between devices, partner(): lax.ppermute(value, 'gy', [(i, i ^ bits) for i in range(16)]).astype(F32)  1.94 us
  transfers between devices with their start and end apart: 9, of which 6 were waited for; matrix products, arithmetic and copies ran while one was open for 4% of the time, Pallas kernels for 11%

profile of v6, /device:TPU:6, one launch (start us, length us, event | category | flops | bytes accessed | tf_op | source)
XLA Modules:
  0.0 48.5 jit_solution(18072413561095996615)
XLA Ops:
  0.7 1.1 %slice_select_fusion = (f32[12,3,256]{2,1,0:T(4,128)S(1)}, f32[12,3,256]{2,1,0:T(4,128)S(1)}) fusion(f32[12,8,256]{2,1,0:T(8,128)} %volume_ref.1, pred[]{:T(512)S(6)} %eq.9), kind=kLoop, calls=%fused_computation.5 | loop fusion | flops 18432 | bytes 147457 | tf_op jit(solution)/shard_map/jit(_where)/select_n | solution.py:394
  1.8 2.2 %collective-permute-start.1 = (f32[12,3,256]{2,1,0:T(4,128)S(1)}, f32[12,3,256]{2,1,0:T(4,128)S(1)}, u32[]{:S(2)}, u32[]{:S(2)}) collective-permute-start(f32[12,3,256]{2,1,0:T(4,128)S(1)} %get-tuple-element.28), channel_id=1, source_target_pairs={{1,2},{3,4},{5,6},{7,8},{9,10},{11,12},{13,14},{2,1},{4,3},{6,5},{... | collective-permute-start | bytes 110600 | tf_op jit(solution)/shard_map/ppermute | solution.py:398
  3.9 1.8 %collective-permute-start = (f32[12,3,256]{2,1,0:T(4,128)S(1)}, f32[12,3,256]{2,1,0:T(4,128)S(1)}, u32[]{:S(2)}, u32[]{:S(2)}) collective-permute-start(f32[12,3,256]{2,1,0:T(4,128)S(1)} %get-tuple-element.29), channel_id=1, source_target_pairs={{0,1},{1,0},{2,3},{3,2},{4,5},{5,4},{6,7},{7,6},{8,9},{9,8},{10,11... | collective-permute-start | bytes 110600 | tf_op jit(solution)/shard_map/ppermute | solution.py:395
  7.0 0.2 collective-permute-done.1.second_ref
  7.2 0.6 %copy-done.6 = f32[12,3,256]{2,1,0:T(4,128)} copy-done((f32[12,3,256]{2,1,0:T(4,128)}, f32[12,3,256]{2,1,0:T(4,128)S(1)}, u32[]{:S(2)}) %copy-start.6) | copy-done | bytes 36888
  7.8 9.6 %axial.1 = (f32[8,16,256]{2,1,0:T(8,128)}, f32[128,128]{1,0:T(8,128)}, bf16[128,128]{1,0:T(8,128)(2,1)}) custom-call(s32[1]{0:T(128)S(6)} %copy.17.subset_ref, s32[1]{0:T(128)S(6)} %copy.18.timestep_ref, f32[12,8,256]{2,1,0:T(8,128)} %volume_ref.1, f32[12,3,256]{2,1,0:T(4,128)} %copy-done.7, f32[12,3,256]{2,1,0:T(4,128)} %copy-done.6, ...), custom_call_target="tpu_custom_call" | custom-call | tf_op jit(solution)/shard_map/axial/pallas_call | solution.py:450
  17.4 1.2 %collective-permute-start.2 = (bf16[128,128]{1,0:T(8,128)(2,1)}, bf16[128,128]{1,0:T(8,128)(2,1)S(1)}, u32[]{:S(2)}, u32[]{:S(2)}) collective-permute-start(bf16[128,128]{1,0:T(8,128)(2,1)} %get-tuple-element.16), channel_id=1, source_target_pairs={{0,1},{1,0},{2,3},{3,2},{4,5},{5,4},{6,7},{7,6},{8,9},{9,8},{10,11... | collective-permute-start | bytes 98312 | tf_op jit(solution)/shard_map/ppermute | solution.py:404
  18.6 0.8 %broadcast_add_fusion.1 = f32[128,128]{1,0:T(8,128)S(1)} fusion(f32[128,128]{1,0:T(8,128)} %get-tuple-element.15, f32[]{:T(128)} %bitcast.10), kind=kLoop, calls=%fused_computation.7 | loop fusion | flops 16384 | bytes 131076 | tf_op jit(solution)/shard_map/add | solution.py:482
  19.5 0.2 collective-permute-done.2
  19.7 2.0 %collective-permute-start.5 = (bf16[128,128]{1,0:T(8,128)(2,1)S(1)}, bf16[128,128]{1,0:T(8,128)(2,1)S(1)}, u32[]{:S(2)}, u32[]{:S(2)}) collective-permute-start(bf16[128,128]{1,0:T(8,128)(2,1)S(1)} %fusion), channel_id=1, source_target_pairs={{0,6},{1,7},{2,4},{3,5},{4,2},{5,3},{6,0},{7,1},{8,14},{9,15},{10,... | collective-permute-start | bytes 98312 | tf_op jit(solution)/shard_map/ppermute | solution.py:404
  21.7 1.5 %collective-permute-start.3 = (bf16[128,128]{1,0:T(8,128)(2,1)S(1)}, bf16[128,128]{1,0:T(8,128)(2,1)S(1)}, u32[]{:S(2)}, u32[]{:S(2)}) collective-permute-start(bf16[128,128]{1,0:T(8,128)(2,1)S(1)} %fusion), channel_id=1, source_target_pairs={{0,2},{1,3},{2,0},{3,1},{4,6},{5,7},{6,4},{7,5},{8,10},{9,11},{10,... | collective-permute-start | bytes 98312 | tf_op jit(solution)/shard_map/ppermute | solution.py:404
  23.3 0.6 %prepare.1 = (bf16[1024,128]{1,0:T(8,128)(2,1)S(1)}, bf16[128,768]{1,0:T(8,128)(2,1)S(1)}, f32[64,256]{1,0:T(8,128)S(1)}, bf16[48,896]{1,0:T(8,128)(2,1)S(1)}, f32[128,128]{1,0:T(8,128)S(1)}) custom-call(bf16[9,64]{1,0:T(8,128)(2,1)S(1)} %bitcast.13, f32[1,64]{1,0:T(1,128)S(1)} %bitcast.15, f32[1,64]{1,0:T(1,128)S(1)} %bitcast.16, ...), custom_call_target="tpu_custom_call" | custom-call | flops 1000000 | bytes 3000000 | tf_op jit(solution)/shard_map/prepare/pallas_call | solution.py:431
  23.9 0.8 %collective-permute-done.5 = bf16[128,128]{1,0:T(8,128)(2,1)S(1)} collective-permute-done((bf16[128,128]{1,0:T(8,128)(2,1)S(1)}, bf16[128,128]{1,0:T(8,128)(2,1)S(1)}, u32[]{:S(2)}, u32[]{:S(2)}) %collective-permute-start.5) | collective-permute-done | bytes 32800 | tf_op jit(solution)/shard_map/ppermute | solution.py:404
  24.7 0.9 %collective-permute-done.4 = bf16[128,128]{1,0:T(8,128)(2,1)S(1)} collective-permute-done((bf16[128,128]{1,0:T(8,128)(2,1)S(1)}, bf16[128,128]{1,0:T(8,128)(2,1)S(1)}, u32[]{:S(2)}, u32[]{:S(2)}) %collective-permute-start.4) | collective-permute-done | bytes 32800 | tf_op jit(solution)/shard_map/ppermute | solution.py:404
  25.7 3.7 %collective-permute-start.6 = (bf16[128,128]{1,0:T(8,128)(2,1)S(1)}, bf16[128,128]{1,0:T(8,128)(2,1)S(1)}, u32[]{:S(2)}, u32[]{:S(2)}) collective-permute-start(bf16[128,128]{1,0:T(8,128)(2,1)S(1)} %fusion.1._), channel_id=1, source_target_pairs={{0,8},{1,9},{2,10},{3,11},{4,12},{5,13},{6,14},{7,15},{8,0},{9,1},... | collective-permute-start | bytes 98312 | tf_op jit(solution)/shard_map/ppermute | solution.py:404
  29.4 0.9 %broadcast_add_fusion.axial_ref = f32[8,16,256]{2,1,0:T(8,128)S(1)} fusion(f32[8,16,256]{2,1,0:T(8,128)} %get-tuple-element.19, f32[]{:T(128)} %bitcast.10), kind=kLoop, calls=%fused_computation | loop fusion | flops 32768 | bytes 262148 | tf_op jit(solution)/shard_map/add | solution.py:494
  30.3 2.2 %choose.1.chosen_ref = bf16[8192,256]{1,0:T(8,128)(2,1)S(1)} custom-call(s32[1]{0:T(128)S(6)} %copy.17.subset_ref, bf16[128,128]{1,0:T(8,128)(2,1)S(1)} %fusion.1._, bf16[4,8192,256]{2,1,0:T(8,128)(2,1)} %bitcast.18), custom_call_target="tpu_custom_call" | custom-call | bytes 8388608 | tf_op jit(solution)/shard_map/choose/pallas_call | solution.py:484
  32.6 1.5 %back.1 = (f32[8,16,256]{2,1,0:T(8,128)S(1)}, f32[12,64]{1,0:T(8,128)}) custom-call(s32[1]{0:T(128)S(6)} %copy.17.subset_ref, f32[128,128]{1,0:T(8,128)S(1)} %get-tuple-element.14.measured_ref, f32[128,128]{1,0:T(8,128)S(1)} %convert_add_fusion.sinogram_ref, f32[8,16,256]{2,1,0:T(8,128)S(1)} %broadcast_add_fusion.axial_ref, ...), custom_call_target="tpu_custom_call" | custom-call | tf_op jit(solution)/shard_map/back/pallas_call | solution.py:495
  34.0 6.5 %collective-permute-start.8 = (f32[8,3,256]{2,1,0:T(4,128)S(1)}, f32[8,3,256]{2,1,0:T(4,128)S(1)}, u32[]{:S(2)}, u32[]{:S(2)}) collective-permute-start(f32[8,3,256]{2,1,0:T(4,128)S(1)} %get-tuple-element.26), channel_id=1, source_target_pairs={{16,32},{48,64},{80,96},{32,16},{64,48},{96,80},{17,33},{49,65},{8... | collective-permute-start | bytes 73736 | tf_op jit(solution)/shard_map/ppermute | solution.py:398
  40.5 0.3 collective-permute-start.7
  40.8 2.3 %inner.1.inner_ref = f32[8,48,256]{2,1,0:T(8,128)S(1)} custom-call(s32[1]{0:T(128)S(6)} %copy.18.timestep_ref, f32[8,16,256]{2,1,0:T(8,128)S(1)} %get-tuple-element.20.corrected_ref, bf16[1024,128]{1,0:T(8,128)(2,1)S(1)} %get-tuple-element.21.one_ref, bf16[128,768]{1,0:T(8,128)(2,1)S(1)} %get-tuple-element.22.middle_ref, ...), custom_call_target="tpu_custom_call" | custom-call | flops 2000000000 | bytes 2097152 | tf_op jit(solution)/shard_map/inner/pallas_call | solution.py:509
  43.1 0.3 collective-permute-done.8.second_ref
  43.5 1.3 %collective-permute-done.7.first_ref = f32[8,3,256]{2,1,0:T(4,128)S(1)} collective-permute-done((f32[8,3,256]{2,1,0:T(4,128)S(1)}, f32[8,3,256]{2,1,0:T(4,128)S(1)}, u32[]{:S(2)}, u32[]{:S(2)}) %collective-permute-start.7) | collective-permute-done | bytes 24608 | tf_op jit(solution)/shard_map/ppermute | solution.py:395
  44.7 3.8 %coronal.1 = f32[12,8,256]{2,1,0:T(8,128)} custom-call(s32[1]{0:T(128)S(6)} %copy.18.timestep_ref, f32[8,16,256]{2,1,0:T(8,128)S(1)} %get-tuple-element.20.corrected_ref, f32[8,3,256]{2,1,0:T(4,128)S(1)} %collective-permute-done.7.first_ref, f32[8,3,256]{2,1,0:T(4,128)S(1)} %collective-permute-done.8.second_ref, f32[8,48,256]{2,1,0:T(8,128)S(1)} %inner.1.inner_ref, ...), custom_call_target="tpu_custom_call" | custom-call | tf_op jit(solution)/shard_map/coronal/pallas_call | solution.py:519
  (23 shorter events, 0.1 us)
Async XLA Ops:
  0.6 22.6 %copy-start.3 = (bf16[9,1,64]{2,0,1:T(8,128)(2,1)S(1)}, bf16[9,1,64]{2,0,1:T(8,128)(2,1)}, u32[]{:S(2)}) copy-start(bf16[9,1,64]{2,0,1:T(8,128)(2,1)} %param.29) | copy-start | bytes 3460
  0.6 22.6 %copy-start.5 = (f32[64]{0:T(128)S(1)}, f32[64]{0:T(128)}, u32[]{:S(2)}) copy-start(f32[64]{0:T(128)} %param.28) | copy-start | bytes 772
  0.7 22.6 %copy-start = (bf16[9,64,64]{2,1,0:T(8,128)(2,1)S(1)}, bf16[9,64,64]{2,1,0:T(8,128)(2,1)}, u32[]{:S(2)}) copy-start(bf16[9,64,64]{2,1,0:T(8,128)(2,1)} %refs_4_.1) | copy-start | bytes 221188
  0.7 22.6 %copy-start.4 = (f32[64]{0:T(128)S(1)}, f32[64]{0:T(128)}, u32[]{:S(2)}) copy-start(f32[64]{0:T(128)} %param.26) | copy-start | bytes 772
  0.7 22.6 %copy-start.2 = (bf16[9,64,1]{1,0,2:T(8,128)(2,1)S(1)}, bf16[9,64,1]{1,0,2:T(8,128)(2,1)}, u32[]{:S(2)}) copy-start(bf16[9,64,1]{1,0,2:T(8,128)(2,1)} %param.25) | copy-start | bytes 3460
  0.7 22.6 %copy-start.1 = (f32[1024,12]{0,1:T(8,128)S(1)}, f32[1024,12]{0,1:T(8,128)}, u32[]{:S(2)}) copy-start(f32[1024,12]{0,1:T(8,128)} %param.17) | copy-start | bytes 147460
  1.8 5.4 %collective-permute-start.1 = (f32[12,3,256]{2,1,0:T(4,128)S(1)}, f32[12,3,256]{2,1,0:T(4,128)S(1)}, u32[]{:S(2)}, u32[]{:S(2)}) collective-permute-start(f32[12,3,256]{2,1,0:T(4,128)S(1)} %get-tuple-element.28), channel_id=1, source_target_pairs={{1,2},{3,4},{5,6},{7,8},{9,10},{11,12},{13,14},{2,1},{4,3},{6,5},{... | collective-permute-start | bytes 110600 | tf_op jit(solution)/shard_map/ppermute | solution.py:398
  3.9 3.2 %collective-permute-start = (f32[12,3,256]{2,1,0:T(4,128)S(1)}, f32[12,3,256]{2,1,0:T(4,128)S(1)}, u32[]{:S(2)}, u32[]{:S(2)}) collective-permute-start(f32[12,3,256]{2,1,0:T(4,128)S(1)} %get-tuple-element.29), channel_id=1, source_target_pairs={{0,1},{1,0},{2,3},{3,2},{4,5},{5,4},{6,7},{7,6},{8,9},{9,8},{10,11... | collective-permute-start | bytes 110600 | tf_op jit(solution)/shard_map/ppermute | solution.py:395
  7.2 0.6 %copy-start.6 = (f32[12,3,256]{2,1,0:T(4,128)}, f32[12,3,256]{2,1,0:T(4,128)S(1)}, u32[]{:S(2)}) copy-start(f32[12,3,256]{2,1,0:T(4,128)S(1)} %collective-permute-done.1.second_ref) | copy-start | bytes 110596
  7.2 0.6 %copy-start.7 = (f32[12,3,256]{2,1,0:T(4,128)}, f32[12,3,256]{2,1,0:T(4,128)S(1)}, u32[]{:S(2)}) copy-start(f32[12,3,256]{2,1,0:T(4,128)S(1)} %collective-permute-done.first_ref) | copy-start | bytes 110596
  17.4 2.3 %collective-permute-start.2 = (bf16[128,128]{1,0:T(8,128)(2,1)}, bf16[128,128]{1,0:T(8,128)(2,1)S(1)}, u32[]{:S(2)}, u32[]{:S(2)}) collective-permute-start(bf16[128,128]{1,0:T(8,128)(2,1)} %get-tuple-element.16), channel_id=1, source_target_pairs={{0,1},{1,0},{2,3},{3,2},{4,5},{5,4},{6,7},{7,6},{8,9},{9,8},{10,11... | collective-permute-start | bytes 98312 | tf_op jit(solution)/shard_map/ppermute | solution.py:404
  19.7 5.0 %collective-permute-start.5 = (bf16[128,128]{1,0:T(8,128)(2,1)S(1)}, bf16[128,128]{1,0:T(8,128)(2,1)S(1)}, u32[]{:S(2)}, u32[]{:S(2)}) collective-permute-start(bf16[128,128]{1,0:T(8,128)(2,1)S(1)} %fusion), channel_id=1, source_target_pairs={{0,6},{1,7},{2,4},{3,5},{4,2},{5,3},{6,0},{7,1},{8,14},{9,15},{10,... | collective-permute-start | bytes 98312 | tf_op jit(solution)/shard_map/ppermute | solution.py:404
  21.7 3.9 %collective-permute-start.4 = (bf16[128,128]{1,0:T(8,128)(2,1)S(1)}, bf16[128,128]{1,0:T(8,128)(2,1)S(1)}, u32[]{:S(2)}, u32[]{:S(2)}) collective-permute-start(bf16[128,128]{1,0:T(8,128)(2,1)S(1)} %fusion), channel_id=1, source_target_pairs={{0,4},{1,5},{2,6},{3,7},{4,0},{5,1},{6,2},{7,3},{8,12},{9,13},{10,... | collective-permute-start | bytes 98312 | tf_op jit(solution)/shard_map/ppermute | solution.py:404
  21.7 3.9 %collective-permute-start.3 = (bf16[128,128]{1,0:T(8,128)(2,1)S(1)}, bf16[128,128]{1,0:T(8,128)(2,1)S(1)}, u32[]{:S(2)}, u32[]{:S(2)}) collective-permute-start(bf16[128,128]{1,0:T(8,128)(2,1)S(1)} %fusion), channel_id=1, source_target_pairs={{0,2},{1,3},{2,0},{3,1},{4,6},{5,7},{6,4},{7,5},{8,10},{9,11},{10,... | collective-permute-start | bytes 98312 | tf_op jit(solution)/shard_map/ppermute | solution.py:404
  25.7 6.9 %collective-permute-start.6 = (bf16[128,128]{1,0:T(8,128)(2,1)S(1)}, bf16[128,128]{1,0:T(8,128)(2,1)S(1)}, u32[]{:S(2)}, u32[]{:S(2)}) collective-permute-start(bf16[128,128]{1,0:T(8,128)(2,1)S(1)} %fusion.1._), channel_id=1, source_target_pairs={{0,8},{1,9},{2,10},{3,11},{4,12},{5,13},{6,14},{7,15},{8,0},{9,1},... | collective-permute-start | bytes 98312 | tf_op jit(solution)/shard_map/ppermute | solution.py:404
  34.0 9.4 %collective-permute-start.8 = (f32[8,3,256]{2,1,0:T(4,128)S(1)}, f32[8,3,256]{2,1,0:T(4,128)S(1)}, u32[]{:S(2)}, u32[]{:S(2)}) collective-permute-start(f32[8,3,256]{2,1,0:T(4,128)S(1)} %get-tuple-element.26), channel_id=1, source_target_pairs={{16,32},{48,64},{80,96},{32,16},{64,48},{96,80},{17,33},{49,65},{8... | collective-permute-start | bytes 73736 | tf_op jit(solution)/shard_map/ppermute | solution.py:398
  40.5 4.2 %collective-permute-start.7 = (f32[8,3,256]{2,1,0:T(4,128)S(1)}, f32[8,3,256]{2,1,0:T(4,128)S(1)}, u32[]{:S(2)}, u32[]{:S(2)}) collective-permute-start(f32[8,3,256]{2,1,0:T(4,128)S(1)} %get-tuple-element.27), channel_id=1, source_target_pairs={{0,16},{16,0},{32,48},{48,32},{64,80},{80,64},{96,112},{112,96},{1... | collective-permute-start | bytes 73736 | tf_op jit(solution)/shard_map/ppermute | solution.py:395
